TPU v7x, 32 devices: a whole 2x2x4 slice. The times are simulated.
32 devices in a mesh: rep: 2 (over x), fsdp: 16 (over z, y, core).
Axes of the slice: x: 2, y: 2, z: 4, core: 2. Of those that a mesh axis runs over, the one named last changes fastest.
Arguments:
- tokens: bfloat16 [64, 512, 768], P(('rep', 'fsdp')), may hold values from -6 to 6
- mask_pos: int32 [64, 128], P(('rep', 'fsdp')), may hold values from 0 to 511, as said below
- group_id: int32 [64], P(('rep', 'fsdp')), may hold values from 0 to 1, as said below
- cotangent: bfloat16 [64, 512, 768], P(('rep', 'fsdp')), may hold values from -6 to 6
- w_qkv: float32 [768, 2304], P('fsdp'), may hold values from -0.21875 to 0.21875
- b_query: float32 [768], P('fsdp'), may hold values from -3 to 3
- b_value: float32 [768], P('fsdp'), may hold values from -3 to 3
- w_out: float32 [768, 768], P('fsdp'), may hold values from -3 to 3
- b_out: float32 [768], P('fsdp'), may hold values from -3 to 3
- w_up: float32 [768, 3072], P('fsdp'), may hold values from -0.21875 to 0.21875
- b_up: float32 [3072], P('fsdp'), may hold values from -3 to 3
- w_down: float32 [3072, 768], P('fsdp'), may hold values from -0.109375 to 0.109375
- b_down: float32 [768], P('fsdp'), may hold values from -3 to 3
- ln1_gain: float32 [768], P('fsdp'), may hold values from 0.1 to 1.9
- ln1_bias: float32 [768], P('fsdp'), may hold values from -3 to 3
- ln2_gain: float32 [768], P('fsdp'), may hold values from 0.1 to 1.9
- ln2_bias: float32 [768], P('fsdp'), may hold values from -3 to 3
- mask_embed: float32 [768], P('fsdp'), may hold values from -4 to 4
Outputs:
- output: bfloat16 [64, 512, 768], P(('rep', 'fsdp'))
- token_grad: bfloat16 [64, 512, 768], P(('rep', 'fsdp'))
- w_qkv_grad: float32 [768, 2304], P('fsdp')
- b_query_grad: float32 [768], P('fsdp')
- b_value_grad: float32 [768], P('fsdp')
- w_out_grad: float32 [768, 768], P('fsdp')
- b_out_grad: float32 [768], P('fsdp')
- w_up_grad: float32 [768, 3072], P('fsdp')
- b_up_grad: float32 [3072], P('fsdp')
- w_down_grad: float32 [3072, 768], P('fsdp')
- b_down_grad: float32 [768], P('fsdp')
- ln1_gain_grad: float32 [768], P('fsdp')
- ln1_bias_grad: float32 [768], P('fsdp')
- ln2_gain_grad: float32 [768], P('fsdp')
- ln2_bias_grad: float32 [768], P('fsdp')
- mask_embed_grad: float32 [768], P('fsdp')
Inputs may be any that keep to these rules, and one draw needn't show every extreme that they name: `group_id`: all 2 clips of one device share one group id; both ids occur in every draw. A clip of group 1 has half of 512 patches, the rest of its rows are padding. `mask_pos`: the 128 positions of a clip are distinct and lie below the clip's number of patches.
All inputs are finite; a program needn't handle non-finite values.
Results may differ from a plain program's by a relative error of at most 0.014.
The roundings to bfloat16 on the way count: a program that leaves them out, or rounds other values in their place, can miss the bound.
Values may be sent and summed in bfloat16 or wider, within the bound.
No kernel may reach another device: no remote copies, remote signals or barrier semaphores. Data moves between devices by JAX's collectives and lax.ppermute only.
A program may use at most 192 MiB of HBM per device.

v0:
```python
import functools

import jax
import jax.numpy as jnp
from jax import lax
from jax.experimental import pallas as pl
from jax.experimental.pallas import tpu as pltpu
from jax.sharding import PartitionSpec as P

HEADS = 12
BLOCKS = 16
EPS = 1e-06
BF = jnp.bfloat16
F32 = jnp.float32
VMEM_LIMIT = 56 * 1024 * 1024

B_QUERY, B_VALUE, B_OUT, B_DOWN, GAIN1, BIAS1, GAIN2, BIAS2, EMBED, B_UP = range(10)
VECS = 13


def dot(a, b):
    return jnp.dot(a, b, preferred_element_type=F32)


def dot_nt(a, b):
    return lax.dot_general(a, b, (((1,), (1,)), ((), ())), preferred_element_type=F32)


def dot_tn(a, b):
    return lax.dot_general(a, b, (((0,), (0,)), ((), ())), preferred_element_type=F32)


def normalise(values):
    centre = values - jnp.mean(values, -1, keepdims=True)
    spread = jnp.mean(centre * centre, -1, keepdims=True)
    r = lax.rsqrt(spread + EPS)
    return centre * r, r


def norm_back(x_hat, r, q, gain):
    qg = q * gain
    m1 = jnp.mean(qg, -1, keepdims=True)
    m2 = jnp.mean(qg * x_hat, -1, keepdims=True)
    return r * (qg - m1 - x_hat * m2)


def colsum(values):
    return jnp.sum(values, 0, keepdims=True)


def gelu_both(u):
    x = jnp.abs(u)
    t = pl.reciprocal(1.0 + x * (0.3275911 * 0.7071067811865476), approx=False)
    e = jnp.exp2(u * u * (-0.5 * 1.4426950408889634))
    poly = 0.5 * 1.061405429
    for c in (-1.453152027, 1.421413741, -0.284496736, 0.254829592):
        poly = poly * t + 0.5 * c
    tail = poly * t * e
    cdf = jnp.where(u < 0, tail, 1.0 - tail)
    return u * cdf, cdf + u * (e * 0.3989422804014327)


def pack_kernel(
    w_qkv, w_out, w_up, w_down, b_query, b_value, b_out, b_down, g1, b1, g2, b2, embed, b_up, one_ref, two_ref, table
):
    width, dim = w_out.shape
    for i in range(3):
        one_ref[i * width : (i + 1) * width] = w_qkv[:, i * dim : (i + 1) * dim].astype(BF)
    one_ref[3 * width : 4 * width] = w_out[...].astype(BF)
    table[...] = jnp.zeros_like(table)
    for k, ref in enumerate((b_query, b_value, b_out, b_down, g1, b1, g2, b2, embed, b_up)):
        table[k : k + 1, 0 : ref.shape[1]] = ref[...]
    one_ref[4 * width :] = table[...].astype(BF)
    two_ref[0 : 4 * width] = w_down[...].astype(BF)
    for i in range(4):
        two_ref[(4 + i) * width : (5 + i) * width] = w_up[:, i * dim : (i + 1) * dim].astype(BF)


def pack_call(masters):
    (w_qkv, b_query, b_value, w_out, b_out, w_up, b_up, w_down, b_down,
     ln1_gain, ln1_bias, ln2_gain, ln2_bias, mask_embed) = masters
    width, dim = w_out.shape
    vectors = (b_query, b_value, b_out, b_down, ln1_gain, ln1_bias, ln2_gain, ln2_bias, mask_embed, b_up)
    return pl.pallas_call(
        pack_kernel,
        out_shape=[
            jax.ShapeDtypeStruct((4 * width + 16, dim), BF),
            jax.ShapeDtypeStruct((8 * width, dim), BF),
        ],
        scratch_shapes=[pltpu.VMEM((16, dim), F32)],
        name="pack",
    )(w_qkv, w_out, w_up, w_down, *(v.reshape(1, -1) for v in vectors))


def load_pieces(place, pieces, dest, sems):
    z, y, c, r = (place[i] for i in range(4))
    half = dest.shape[2] // 2
    kinds = ((0, 0, 0), (1, 0, 0), (0, 1, 0), (1, 1, 0), (1, 1, 2))
    copies = []
    for p, ref in enumerate(pieces):
        dx, dy, first = kinds[p % 5]
        dc = p // 5
        for k in range(ref.shape[0]):
            at = ((z + 4 - k - first) % 4) * 4 + (y ^ dy) * 2 + (c ^ dc)
            lanes = pl.ds(pl.multiple_of((r ^ dx) * half, 128), half)
            copies.append(pltpu.make_async_copy(ref.at[k], dest.at[at, :, lanes], sems.at[len(copies)]))
    for copy in copies:
        copy.start()
    for copy in copies:
        copy.wait()


def forward_kernel(count, group_ref, place_ref, tok_ref, mask_ref, *refs):
    pieces = refs[:count]
    normed_ref, qkv_ref, att_ref, lse_ref, vec_ref, w1_ref, sems = refs[count:]
    clip = pl.program_id(0)
    seq, dim = tok_ref.shape[1], tok_ref.shape[2]

    @pl.when(clip == 0)
    def _():
        if count == 1:
            copy = pltpu.make_async_copy(pieces[0], w1_ref, sems.at[0])
            copy.start()
            copy.wait()
        else:
            load_pieces(place_ref, pieces, w1_ref, sems)
        table = [w1_ref[i, 192:208, :].astype(F32) for i in range(BLOCKS)]
        vec_ref[0:B_UP] = jnp.concatenate([t[0:B_UP, 0:48] for t in table], 1)
        for j in range(4):
            vec_ref[B_UP + j : B_UP + j + 1] = jnp.concatenate(
                [t[B_UP : B_UP + 1, 0:192] for t in table[4 * j : 4 * j + 4]], 1
            )
        vec_ref[VECS:] = jnp.zeros((16 - VECS, dim), F32)

    vec = lambda k: vec_ref[k : k + 1, :]
    weight = lambda k: w1_ref[:, 48 * k : 48 * (k + 1), :].reshape(dim, dim)
    step = seq // 2
    for r in range(0, seq, step):
        rows = slice(r, r + step)
        blended = jnp.where(mask_ref[0, rows] > 0, vec(EMBED), tok_ref[0, rows].astype(F32))
        x_hat, _ = normalise(blended)
        normed = (x_hat * vec(GAIN1) + vec(BIAS1)).astype(BF)
        normed_ref[0, rows] = normed
        qkv_ref[0, rows, 0:dim] = (dot(normed, weight(0)) + vec(B_QUERY)).astype(BF)
        qkv_ref[0, rows, dim : 2 * dim] = dot(normed, weight(1)).astype(BF)
        qkv_ref[0, rows, 2 * dim :] = (dot(normed, weight(2)) + vec(B_VALUE)).astype(BF)
    head = dim // HEADS
    scale = head**-0.5 * 1.4426950408889634

    def attend(length):
        if length < seq:
            att_ref[0, length:, :] = jnp.zeros((seq - length, dim), BF)
            lse_ref[0, :, :] = jnp.zeros((HEADS, seq), F32)
        chunk = min(length, 512)
        lane = lax.broadcasted_iota(jnp.int32, (chunk, 2 * head), 1)

        @pl.loop(0, HEADS // 2, unroll=2)
        def _(pair):
            lanes = lambda i: pl.ds(pl.multiple_of(i * dim + pair * 2 * head, 128), 2 * head)
            k = qkv_ref[0, 0:length, lanes(1)]
            vt = qkv_ref[0, 0:length, lanes(2)].T
            for c in range(0, length, chunk):
                q = qkv_ref[0, c : c + chunk, lanes(0)]
                zero = jnp.zeros_like(q)
                both = jnp.concatenate([jnp.where(lane < head, q, zero), jnp.where(lane < head, zero, q)], 0)
                st = dot_nt(k, both)
                top = jnp.max(st, 0, keepdims=True) * scale
                e = jnp.exp2(st * scale - top)
                total = jnp.sum(e, 0, keepdims=True)
                p = (e * (1.0 / total)).astype(BF)
                o0 = dot(vt[0:head], p[:, 0:chunk])
                o1 = dot(vt[head:], p[:, chunk:])
                lse = top + jnp.log2(total)
                lse_ref[0, pl.ds(2 * pair, 1), c : c + chunk] = lse[:, 0:chunk]
                lse_ref[0, pl.ds(2 * pair + 1, 1), c : c + chunk] = lse[:, chunk:]
                att_ref[0, c : c + chunk, lanes(0)] = jnp.concatenate([o0, o1], 0).T.astype(BF)

    full = group_ref[clip] == 0
    pl.when(full)(lambda: attend(seq))
    pl.when(jnp.logical_not(full))(lambda: attend(seq // 2))


def weight_spec(index):
    return pl.BlockSpec((BLOCKS, 48, 768), lambda *g: (0, index, 0))


def forward_call(group_id, place, tokens, mask, pieces):
    clips, seq, dim = tokens.shape
    row = lambda *tail: pl.BlockSpec((1, *tail), lambda c, *_: (c,) + (0,) * len(tail))
    return pl.pallas_call(
        functools.partial(forward_kernel, len(pieces)),
        grid_spec=pltpu.PrefetchScalarGridSpec(
            num_scalar_prefetch=2,
            grid=(clips,),
            in_specs=[row(seq, dim), row(seq, 1)] + [pl.BlockSpec(memory_space=pl.ANY)] * len(pieces),
            out_specs=[row(seq, dim), row(seq, 3 * dim), row(seq, dim), row(HEADS, seq), whole(16, dim), whole(BLOCKS, 208, dim)],
            scratch_shapes=[pltpu.SemaphoreType.DMA((32,))],
        ),
        out_shape=[
            jax.ShapeDtypeStruct((clips, seq, dim), BF),
            jax.ShapeDtypeStruct((clips, seq, 3 * dim), BF),
            jax.ShapeDtypeStruct((clips, seq, dim), BF),
            jax.ShapeDtypeStruct((clips, HEADS, seq), F32),
            jax.ShapeDtypeStruct((16, dim), F32),
            jax.ShapeDtypeStruct((BLOCKS, 208, dim), BF),
        ],
        compiler_params=pltpu.CompilerParams(vmem_limit_bytes=VMEM_LIMIT),
        cost_estimate=pl.CostEstimate(flops=9 * 10**9, bytes_accessed=16 * 2**20, transcendentals=0),
        name="attention_forward",
    )(group_id, place, tokens, mask, *pieces)


def store_by_core(core, value, keep_ref, send_ref, rows):
    for own in range(2):

        @pl.when(core == own)
        def _():
            keep_ref[:, rows] = value[:, own]
            send_ref[:, rows] = value[:, 1 - own]


def mlp_kernel(
    group_ref, place_ref, tok_ref, mask_ref, cot_ref, att_ref, vec_ref, wo_ref, wu_ref, wd_ref,
    out_ref, gb_ref, gw_ref, keep_ref, send_ref, gvec_ref,
    hidden, n2, gr, act, gpre, acc, gn2,
):
    j = pl.program_id(0)
    last = pl.num_programs(0) - 1
    rows_all, dim = tok_ref.shape
    seq = rows_all // group_ref.shape[0]
    vec = lambda k: vec_ref[k : k + 1, :]
    step = 256
    keeps = [group_ref[r // seq] == 0 if (r % seq) >= seq // 2 else None for r in range(0, rows_all, step)]
    weight = [1.0 if keep is None else jnp.where(keep, 1.0, 0.0) for keep in keeps]

    @pl.when(j == 0)
    def _():
        gvec_ref[...] = jnp.zeros_like(gvec_ref)
        w_out = wo_ref[...].reshape(dim, dim)
        for i, r in enumerate(range(0, rows_all, step)):
            rows = slice(r, r + step)
            blended = jnp.where(mask_ref[rows] > 0, vec(EMBED), tok_ref[rows].astype(F32))
            h = blended + dot(att_ref[rows], w_out) + vec(B_OUT)
            hidden[rows] = h
            x_hat, _ = normalise(h)
            n2[rows] = (x_hat * vec(GAIN2) + vec(BIAS2)).astype(BF)
            g = cot_ref[rows].astype(F32) * weight[i]
            gr[rows] = g.astype(BF)
            gvec_ref[B_DOWN : B_DOWN + 1] += colsum(g)
            acc[rows] = h + vec(B_DOWN)
            gn2[rows] = jnp.zeros((step, dim), F32)

    @pl.when(j < last)
    def _():
        w_up = wu_ref[...].reshape(dim, dim)
        w_down = wd_ref[...].reshape(dim, dim)
        b_up = vec_ref[pl.ds(B_UP + j, 1), :]
        bsum = jnp.zeros((1, dim), F32)
        big = 512
        for r in range(0, rows_all, big):
            rows = slice(r, r + big)
            pre = dot(n2[rows], w_up) + b_up
            ga = dot_nt(gr[rows], w_down)
            value, slope = gelu_both(pre)
            value = value.astype(BF)
            act[rows] = value
            grad = (slope * ga).astype(BF)
            gpre[rows] = grad
            bsum += colsum(grad.astype(F32))
            acc[rows] += dot(value, w_down)
            gn2[rows] += dot_nt(grad, w_up)
        gvec_ref[pl.ds(B_UP + j, 1), :] = bsum
        gw_ref[...] = dot_tn(n2[...], gpre[...]).astype(BF).reshape(gw_ref.shape)
        down = dot_tn(act[...], gr[...]).astype(BF).reshape(2, 2, 192, dim)
        store_by_core(place_ref[2], down, keep_ref, send_ref, slice(0, 192))

    @pl.when(j == last)
    def _():
        for i, r in enumerate(range(0, rows_all, step)):
            rows = slice(r, r + step)
            out_ref[rows] = (acc[rows] * weight[i]).astype(BF)
            x_hat, scale = normalise(hidden[rows])
            q = gn2[rows]
            gvec_ref[GAIN2 : GAIN2 + 1] += colsum(q * x_hat)
            gvec_ref[BIAS2 : BIAS2 + 1] += colsum(q)
            gh = cot_ref[rows].astype(F32) * weight[i] + norm_back(x_hat, scale, q, vec(GAIN2))
            gb = gh.astype(BF)
            gb_ref[rows] = gb
            gvec_ref[B_OUT : B_OUT + 1] += colsum(gb.astype(F32))
        gw_ref[...] = dot_tn(att_ref[...], gb_ref[...]).astype(BF).reshape(gw_ref.shape)


def whole(*shape):
    return pl.BlockSpec(shape, lambda *g: (0,) * len(shape))


def mlp_call(group_id, place, tokens, mask, cotangent, att, vecs, w1, w2):
    rows, dim = tokens.shape
    out = lambda shape, kind: jax.ShapeDtypeStruct(shape, kind)
    return pl.pallas_call(
        mlp_kernel,
        grid_spec=pltpu.PrefetchScalarGridSpec(
            num_scalar_prefetch=2,
            grid=(5,),
            in_specs=[
                whole(rows, dim),
                whole(rows, 1),
                whole(rows, dim),
                whole(rows, dim),
                whole(*vecs.shape),
                weight_spec(3),
                pl.BlockSpec((BLOCKS, 48, dim), lambda j, *_: (0, 4 + jnp.minimum(j, 3), 0)),
                pl.BlockSpec((4, 192, dim), lambda j, *_: (jnp.minimum(j, 3), 0, 0)),
            ],
            out_specs=[
                whole(rows, dim),
                whole(rows, dim),
                pl.BlockSpec((BLOCKS, 48, dim), lambda j, *_: (0, j, 0)),
                pl.BlockSpec((2, 192, dim), lambda j, *_: (jnp.minimum(j, 3), 0, 0)),
                pl.BlockSpec((2, 192, dim), lambda j, *_: (jnp.minimum(j, 3), 0, 0)),
                whole(16, dim),
            ],
            scratch_shapes=[
                pltpu.VMEM((rows, dim), F32),
                pltpu.VMEM((rows, dim), BF),
                pltpu.VMEM((rows, dim), BF),
                pltpu.VMEM((rows, dim), BF),
                pltpu.VMEM((rows, dim), BF),
                pltpu.VMEM((rows, dim), F32),
                pltpu.VMEM((rows, dim), F32),
            ],
        ),
        out_shape=[
            out((rows, dim), BF),
            out((rows, dim), BF),
            out((BLOCKS, 240, dim), BF),
            out((BLOCKS // 2, 192, dim), BF),
            out((BLOCKS // 2, 192, dim), BF),
            out((16, dim), F32),
        ],
        compiler_params=pltpu.CompilerParams(vmem_limit_bytes=VMEM_LIMIT),
        cost_estimate=pl.CostEstimate(flops=45 * 10**9, bytes_accessed=30 * 2**20, transcendentals=0),
        name="mlp",
    )(group_id, place, tokens, mask, cotangent, att, vecs, w1, w2, w2)


GROUPS = 2


def attention_back_kernel(
    part, group_ref, place_ref, q_ref, k_ref, v_ref, lse_ref, gb_ref, wo_ref, normed_ref, gj, keep_ref, send_ref, gatt, all_gj
):
    clip = pl.program_id(0)
    seq, dim = gb_ref.shape[1], gb_ref.shape[2]
    wide = dim // GROUPS
    head = dim // HEADS
    scale = head**-0.5
    gatt[...] = dot_nt(gb_ref[0], wo_ref[...].reshape(wide, dim)).astype(BF)

    def back(length):
        if length < seq:
            gj[0, length:, :] = jnp.zeros((seq - length, 3 * wide), BF)
        lane = lax.broadcasted_iota(jnp.int32, (length, 2 * head), 1)

        @pl.loop(0, HEADS // 2 // GROUPS)
        def _(pair):
            lanes = lambda i: pl.ds(pl.multiple_of(i * wide + pair * 2 * head, 128), 2 * head)
            k = k_ref[0, 0:length, lanes(0)]
            v = v_ref[0, 0:length, lanes(0)]
            kt = k.T
            zero = jnp.zeros((length, 2 * head), BF)
            split = lambda a: jnp.concatenate([jnp.where(lane < head, a, zero), jnp.where(lane < head, zero, a)], 0)
            q = split(q_ref[0, 0:length, lanes(0)])
            ga = split(gatt[0:length, lanes(0)])
            first = part * (HEADS // GROUPS) + 2 * pair
            lse = jnp.concatenate([lse_ref[0, pl.ds(first + h, 1), 0:length] for h in range(2)], 1)
            p = jnp.exp2(dot_nt(k, q) * (scale * 1.4426950408889634) - lse)
            gp = dot_nt(v, ga)
            inner = jnp.sum(p * gp, 0, keepdims=True)
            ds = (p * (gp - inner)).astype(BF)
            dq = [dot(kt[h * head : (h + 1) * head], ds[:, h * length : (h + 1) * length]) for h in range(2)]
            gj[0, 0:length, lanes(0)] = (jnp.concatenate(dq, 0).T * scale).astype(BF)
            gj[0, 0:length, lanes(1)] = (dot(ds, q) * scale).astype(BF)
            gj[0, 0:length, lanes(2)] = dot(p.astype(BF), ga).astype(BF)

    full = group_ref[clip] == 0
    pl.when(full)(lambda: back(seq))
    pl.when(jnp.logical_not(full))(lambda: back(seq // 2))
    all_gj[pl.ds(clip * seq, seq)] = gj[0]

    @pl.when(clip == pl.num_programs(0) - 1)
    def _():
        grad = dot_tn(normed_ref[...], all_gj[...])
        for i in range(3):
            value = grad[:, i * wide : (i + 1) * wide].astype(BF).reshape(BLOCKS // 2, 2, 48, wide)
            store_by_core(place_ref[2], value, keep_ref, send_ref, slice(48 * i, 48 * (i + 1)))


def attention_back_call(part, group_id, place, qkv, lse, gb, w1, normed):
    clips, seq, dim = gb.shape
    wide = dim // GROUPS
    columns = lambda i: pl.BlockSpec((1, seq, wide), lambda c, *_: (c, 0, GROUPS * i + part))
    row = lambda *tail: pl.BlockSpec((1, *tail), lambda c, *_: (c,) + (0,) * len(tail))
    return pl.pallas_call(
        functools.partial(attention_back_kernel, part),
        grid_spec=pltpu.PrefetchScalarGridSpec(
            num_scalar_prefetch=2,
            grid=(clips,),
            in_specs=[
                columns(0),
                columns(1),
                columns(2),
                row(HEADS, seq),
                row(seq, dim),
                pl.BlockSpec((BLOCKS // GROUPS, 48, dim), lambda *g: (part, 3, 0)),
                whole(clips * seq, dim),
            ],
            out_specs=[row(seq, 3 * wide), whole(BLOCKS // 2, 144, wide), whole(BLOCKS // 2, 144, wide)],
            scratch_shapes=[pltpu.VMEM((seq, wide), BF), pltpu.VMEM((clips * seq, 3 * wide), BF)],
        ),
        out_shape=[
            jax.ShapeDtypeStruct((clips, seq, 3 * wide), BF),
            jax.ShapeDtypeStruct((BLOCKS // 2, 144, wide), BF),
            jax.ShapeDtypeStruct((BLOCKS // 2, 144, wide), BF),
        ],
        compiler_params=pltpu.CompilerParams(vmem_limit_bytes=VMEM_LIMIT),
        cost_estimate=pl.CostEstimate(flops=10**8, bytes_accessed=2**20, transcendentals=0),
        name="attention_backward",
    )(group_id, place, qkv, qkv, qkv, lse, gb, w1, normed)


def norm_one_kernel(
    place_ref, tok_ref, mask_ref, gb_ref, gj0_ref, gj1_ref, vec_ref, wq_ref, wk_ref, wv_ref, gmlp_ref,
    tg_ref, keep_ref, send_ref, gvec_ref,
):
    step = pl.program_id(0)
    dim = tok_ref.shape[1]
    wide = dim // GROUPS
    vec = lambda k: vec_ref[k : k + 1, :]

    @pl.when(step == 0)
    def _():
        gvec_ref[...] = gmlp_ref[...]

    gq, gk, gv = (
        jnp.concatenate([ref[:, i * wide : (i + 1) * wide] for ref in (gj0_ref, gj1_ref)], 1) for i in range(3)
    )
    gvec_ref[B_QUERY : B_QUERY + 1] += colsum(gq.astype(F32))
    gvec_ref[B_VALUE : B_VALUE + 1] += colsum(gv.astype(F32))
    g = dot_nt(gq, wq_ref[...].reshape(dim, dim))
    g += dot_nt(gk, wk_ref[...].reshape(dim, dim))
    g += dot_nt(gv, wv_ref[...].reshape(dim, dim))
    masked = mask_ref[...] > 0
    x_hat, r_std = normalise(jnp.where(masked, vec(EMBED), tok_ref[...].astype(F32)))
    gvec_ref[GAIN1 : GAIN1 + 1] += colsum(g * x_hat)
    gvec_ref[BIAS1 : BIAS1 + 1] += colsum(g)
    total = gb_ref[...].astype(F32) + norm_back(x_hat, r_std, g, vec(GAIN1))
    tg_ref[...] = jnp.where(masked, 0.0, total).astype(BF)
    gvec_ref[EMBED : EMBED + 1] += colsum(jnp.where(masked, total, 0.0))

    @pl.when(step == pl.num_programs(0) - 1)
    def _():
        table = gvec_ref[...]
        for i in range(BLOCKS):
            few = table[0:B_UP, 48 * i : 48 * (i + 1)]
            few = jnp.concatenate([few, jnp.zeros((B_UP, wide - 48), F32)], 1)
            at = 192 * (i % 4)
            up = table[B_UP + i // 4 : B_UP + i // 4 + 1, at : at + 192]
            up = jnp.concatenate([up, jnp.zeros((1, wide - 192), F32)], 1)
            few = jnp.concatenate([few, up, jnp.zeros((16 - B_UP - 1, wide), F32)], 0).astype(BF)
            for ref, same in ((keep_ref, True), (send_ref, False)):

                @pl.when((place_ref[2] == i % 2) == same)
                def _():
                    ref[i // 2] = few


def norm_one_call(place, tokens, mask, gb, gj0, gj1, vecs, w1, gvec):
    rows, dim = tokens.shape
    step = rows // 4
    part = lambda width: pl.BlockSpec((step, width), lambda i, *_: (i, 0))
    small = (BLOCKS // 2, 16, dim // GROUPS)
    return pl.pallas_call(
        norm_one_kernel,
        grid_spec=pltpu.PrefetchScalarGridSpec(
            num_scalar_prefetch=1,
            grid=(4,),
            in_specs=[
                part(dim),
                part(1),
                part(dim),
                part(3 * dim // GROUPS),
                part(3 * dim // GROUPS),
                whole(*vecs.shape),
                weight_spec(0),
                weight_spec(1),
                weight_spec(2),
                whole(16, dim),
            ],
            out_specs=[part(dim), whole(*small), whole(*small)],
            scratch_shapes=[pltpu.VMEM((16, dim), F32)],
        ),
        out_shape=[
            jax.ShapeDtypeStruct((rows, dim), BF),
            jax.ShapeDtypeStruct(small, BF),
            jax.ShapeDtypeStruct(small, BF),
        ],
        compiler_params=pltpu.CompilerParams(vmem_limit_bytes=VMEM_LIMIT),
        cost_estimate=pl.CostEstimate(flops=10**8, bytes_accessed=2**20, transcendentals=0),
        name="norm_one_backward",
    )(place, tokens, mask, gb, gj0, gj1, vecs, w1, w1, w1, gvec)


def to_blocks(gathered, kinds):
    n, rows, dim = gathered.shape
    m = n // BLOCKS
    parts = gathered.reshape(BLOCKS, m, kinds, rows // kinds, dim)
    return jnp.swapaxes(parts, 1, 2).reshape(BLOCKS, rows * m, dim)


def from_blocks(blocks, kinds, n):
    _, rows, dim = blocks.shape
    m = n // BLOCKS
    parts = blocks.reshape(BLOCKS, kinds, m, rows // (kinds * m), dim)
    return jnp.swapaxes(parts, 1, 2).reshape(n, rows // m, dim)


def split_columns(matrix, dim):
    return [matrix[:, i : i + dim] for i in range(0, matrix.shape[1], dim)]


def swap(bit):
    return [(i, i ^ bit) for i in range(BLOCKS)]


def turn(k):
    return [(i, (i + 4 * k) % BLOCKS) for i in range(BLOCKS)]


REP = [(0, 1), (1, 0)]


def gather_pieces(pack, r):
    lanes = pack.shape[1] // 2
    half = lax.dynamic_slice_in_dim(pack, r * lanes, lanes, 1)
    along_z = jnp.stack([half] + [lax.ppermute(half, "fsdp", turn(k)) for k in (1, 2, 3)])
    by_x = lax.ppermute(along_z, "rep", REP)
    by_y = lax.ppermute(along_z, "fsdp", swap(2))
    by_xy = lax.ppermute(by_x[:2], "fsdp", swap(2))
    by_yx = lax.ppermute(by_y[2:], "rep", REP)
    own = [along_z, by_x, by_y, by_xy, by_yx]
    return own + [lax.ppermute(piece, "fsdp", swap(1)) for piece in own]


def add(a, b):
    return (a.astype(F32) + b.astype(F32)).astype(BF)


def pick(a, i, axis):
    return lax.dynamic_index_in_dim(a, i, axis, keepdims=False)


def half_of(a, i):
    rows = a.shape[-2] // 2
    return lax.dynamic_slice_in_dim(a, i * rows, rows, a.ndim - 2)


def scatter_steps(keep, send, z, y, r):
    _, rows, dim = keep.shape
    got = lax.ppermute(send, "fsdp", swap(1))
    kept = yield (keep,)
    summed = add(kept[0], got).reshape(4, 2, rows, dim)
    a, b = summed[:2], summed[2:]
    kept = half_of(a, r), pick(b, y, 1)
    sent = yield half_of(a, 1 - r), pick(b, 1 - y, 1), *kept
    got = lax.ppermute(sent[0], "rep", REP), lax.ppermute(sent[1], "fsdp", swap(2))
    kept = yield sent[2:]
    a, b = add(kept[0], got[0]), add(kept[1], got[1])
    sent = yield pick(a, 1 - y, 1), half_of(b, 1 - r), pick(a, y, 1), half_of(b, r)
    got = lax.ppermute(sent[0], "fsdp", swap(2)), lax.ppermute(sent[1], "rep", REP)
    kept = yield sent[2:]
    both = jnp.concatenate([add(kept[0], got[0]), add(kept[1], got[1])])
    sent = yield tuple(pick(both, (z + k) % 4, 0) for k in range(4))
    got = [lax.ppermute(sent[k], "fsdp", turn(k)) for k in (1, 2, 3)]
    kept = yield sent[:1]
    total = kept[0].astype(F32)
    for term in got:
        total += term.astype(F32)
    mine = yield (total.astype(BF),)
    other = lax.ppermute(mine[0], "rep", REP)
    mine = (yield mine)[0]
    yield jnp.where(r == 0, jnp.concatenate([mine, other]), jnp.concatenate([other, mine])).astype(F32)


class Scatter:
    def __init__(self, *args):
        self.steps = scatter_steps(*args)
        self.value = next(self.steps)

    def go(self, *ties):
        self.value, *ties = lax.optimization_barrier((self.value, *ties))
        self.value = self.steps.send(self.value)
        return ties

    def finish(self):
        while isinstance(self.value, tuple):
            self.value = self.steps.send(self.value)
        return self.value


def by_core(keep, send, c):
    first, second = jnp.where(c == 0, keep, send), jnp.where(c == 0, send, keep)
    return jnp.stack([first, second], 1).reshape(BLOCKS, *keep.shape[1:])


def scatter_whole(send):
    own = lax.psum_scatter(send, "fsdp", scatter_dimension=0)
    other = lax.ppermute(own, "rep", REP)
    return own.astype(F32) + other.astype(F32)


def local(n, tokens, mask_pos, group_id, cotangent, *masters):
    clips, seq, dim = tokens.shape
    width = dim // n
    me, r = lax.axis_index("fsdp"), lax.axis_index("rep")
    z, y, c = me // 4, (me // 2) % 2, me % 2
    place = jnp.stack([z, y, c, r]).astype(jnp.int32)
    if n == BLOCKS:
        pack1, pack2 = pack_call(masters)
        w2 = lax.all_gather(pack2, "fsdp", axis=0)
        pieces = gather_pieces(pack1, r)
    else:
        (w_qkv, b_query, b_value, w_out, b_out, w_up, b_up, w_down, b_down,
         ln1_gain, ln1_bias, ln2_gain, ln2_bias, mask_embed) = (m.astype(BF) for m in masters)
        gather = lambda a: lax.all_gather(a, "fsdp", axis=0)
        vec_all = gather(
            jnp.concatenate(
                [b_query, b_value, b_out, b_down, ln1_gain, ln1_bias, ln2_gain, ln2_bias, mask_embed, b_up]
            )
        )
        flat = jnp.swapaxes(vec_all[:, : B_UP * width].reshape(n, B_UP, width), 0, 1).reshape(B_UP, BLOCKS, dim // BLOCKS)
        table = jnp.zeros((BLOCKS, 16, dim), BF)
        table = table.at[:, :B_UP, : dim // BLOCKS].set(jnp.swapaxes(flat, 0, 1))
        table = table.at[:, B_UP, : 4 * dim // BLOCKS].set(vec_all[:, B_UP * width :].reshape(BLOCKS, 4 * dim // BLOCKS))
        one = to_blocks(gather(jnp.concatenate(split_columns(w_qkv, dim) + [w_out])), 4)
        pieces = [jnp.concatenate([one, table], 1)]
        w2 = jnp.concatenate(
            [to_blocks(gather(w_down), 1), to_blocks(gather(jnp.concatenate(split_columns(w_up, dim))), 4)], 1
        )

    positions = lax.iota(jnp.int32, seq)
    mask = jnp.any(mask_pos[:, :, None] == positions[None, None, :], axis=1).astype(F32)[..., None]
    normed, qkv, att, lse, vecs, w1 = forward_call(group_id, place, tokens, mask, pieces)
    flat = lambda a: a.reshape(clips * seq, a.shape[-1])
    output, gb, g2, down_keep, down_send, gvec = mlp_call(
        group_id, place, flat(tokens), flat(mask), flat(cotangent), flat(att), vecs, w1, w2
    )
    gb3 = gb.reshape(tokens.shape)
    wide = dim // GROUPS
    back = lambda part, gb3: attention_back_call(part, group_id, place, qkv, lse, gb3, w1, flat(normed))
    after = lambda gj0, gj1, gvec: norm_one_call(place, flat(tokens), flat(mask), gb, flat(gj0), flat(gj1), vecs, w1, gvec)
    if n == BLOCKS:
        down = Scatter(down_keep, down_send, z, y, r)
        down.go()
        (gb3,) = down.go(gb3)
        gj0, keep0, send0 = back(0, gb3)
        keep0, send0 = down.go(keep0, send0)
        (gb3,) = down.go(gb3)
        first = Scatter(keep0, send0, z, y, r)
        gj1, keep1, send1 = back(1, gb3)
        keep1, send1 = down.go(keep1, send1)
        (gvec,) = down.go(gvec)
        first.go()
        (gvec,) = first.go(gvec)
        token_grad, keep2, send2 = after(gj0, gj1, gvec)
        keep2, send2 = down.go(keep2, send2)
        keep2, send2 = first.go(keep2, send2)
        second = Scatter(jnp.concatenate([keep1, keep2], 1), jnp.concatenate([send1, send2], 1), z, y, r)
        down_grad = down.finish()
        sum0 = first.finish()
        sum1 = second.finish()
        sum2 = scatter_whole(g2)
        up_grad, out_grad = sum2[: 4 * width], sum2[4 * width :]
        qkv_grad = jnp.concatenate([a[i * width : (i + 1) * width] for i in range(3) for a in (sum0, sum1)], 1)
        vg = [sum1[3 * width + k, :width] for k in range(B_UP)] + [sum1[3 * width + B_UP, : 4 * width]]
    else:
        (gj0, *parts0), (gj1, *parts1) = (back(part, gb3) for part in range(GROUPS))
        token_grad, *table = after(gj0, gj1, gvec)
        down_grad = scatter_whole(from_blocks(by_core(down_keep, down_send, place[2]), 1, n))
        rest = scatter_whole(from_blocks(g2, 5, n))
        up_grad, out_grad = rest[: 4 * width], rest[4 * width :]
        sums = [scatter_whole(from_blocks(by_core(*parts, place[2]), 3, n)) for parts in (parts0, parts1)]
        qkv_grad = jnp.concatenate([a[i * width : (i + 1) * width] for i in range(3) for a in sums], 1)
        table = by_core(*table, place[2])
        few = jnp.swapaxes(table[:, :B_UP, : dim // BLOCKS], 0, 1).reshape(B_UP, n, width)
        few = jnp.swapaxes(few, 0, 1).reshape(n, B_UP * width)
        line = scatter_whole(jnp.concatenate([few, table[:, B_UP, : 4 * dim // BLOCKS].reshape(n, 4 * width)], 1))
        vg = [line[i * width : (i + 1) * width] for i in range(B_UP)] + [line[B_UP * width :]]
    up_grad = jnp.concatenate([up_grad[i * width : (i + 1) * width] for i in range(4)], 1)
    return (
        output.reshape(tokens.shape),
        token_grad.reshape(tokens.shape),
        qkv_grad,
        vg[B_QUERY],
        vg[B_VALUE],
        out_grad,
        vg[B_OUT],
        up_grad,
        vg[B_UP],
        down_grad,
        vg[B_DOWN],
        vg[GAIN1],
        vg[BIAS1],
        vg[GAIN2],
        vg[BIAS2],
        vg[EMBED],
    )


def solution(mesh):
    clip3, clip2, clip1 = P(("rep", "fsdp"), None, None), P(("rep", "fsdp"), None), P(("rep", "fsdp"))
    mat, line = P("fsdp", None), P("fsdp")
    params = (mat, line, line, mat, line, mat, line, mat, line, line, line, line, line, line)
    return jax.shard_map(
        functools.partial(local, mesh.shape["fsdp"]),
        mesh=mesh,
        in_specs=(clip3, clip2, clip1, clip3) + params,
        out_specs=(clip3, clip3) + params,
        check_vma=False,
    )
```

profile of v0, /device:TPU:0, one launch (start us, length us, event | category | flops | bytes accessed | tf_op | source)
XLA Modules:
  0.0 300.3 jit_solution(16456587284525859327)
XLA Ops:
  7.2 2.5 pack.1
  9.8 0.9 constant_dynamic-slice_fusion.10
  10.8 3.1 %collective-permute-start = (bf16[208,384]{1,0:T(8,128)(2,1)S(1)}, bf16[208,384]{1,0:T(8,128)(2,1)S(1)}, u32[]{:S(2)}, u32[]{:S(2)}) collective-permute-start(bf16[208,384]{1,0:T(8,128)(2,1)S(1)} %constant_dynamic-slice_fusion.10), channel_id=1, source_target_pairs={{0,4},{1,5},{2,6},{3,7},{4,8},{5,9},{6,10},{7,11},{8,12},{9,13},{1... | collective-permute-start | bytes 479240 | tf_op jit(solution)/shard_map/ppermute | solution.py:546
  13.8 2.6 collective-permute-start.1
  16.4 1.3 collective-permute-start.2
  17.8 0.9 fusion.41
  18.7 2.2 collective-permute-done
  20.9 8.7 %collective-permute-done.1 = bf16[208,384]{1,0:T(8,128)(2,1)S(1)} collective-permute-done((bf16[208,384]{1,0:T(8,128)(2,1)S(1)}, bf16[208,384]{1,0:T(8,128)(2,1)S(1)}, u32[]{:S(2)}, u32[]{:S(2)}) %collective-permute-start.1) | collective-permute-done | bytes 159776 | tf_op jit(solution)/shard_map/ppermute | solution.py:546
  29.7 1.6 collective-permute-start.3
  31.3 1.6 collective-permute-start.4
  32.8 12.2 %collective-permute-done.3.refs_1_ = bf16[4,208,384]{2,1,0:T(8,128)(2,1)S(1)} collective-permute-done((bf16[4,208,384]{2,1,0:T(8,128)(2,1)S(1)}, bf16[4,208,384]{2,1,0:T(8,128)(2,1)S(1)}, u32[]{:S(2)}, u32[]{:S(2)}) %collective-permute-start.3) | collective-permute-done | bytes 639008 | tf_op jit(solution)/shard_map/ppermute | solution.py:547
  45.0 1.6 collective-permute-start.5
  46.7 1.6 collective-permute-start.6
  49.0 4.1 %collective-permute-done.5.refs_3_ = bf16[2,208,384]{2,1,0:T(8,128)(2,1)S(1)} collective-permute-done((bf16[2,208,384]{2,1,0:T(8,128)(2,1)S(1)}, bf16[2,208,384]{2,1,0:T(8,128)(2,1)S(1)}, u32[]{:S(2)}, u32[]{:S(2)}) %collective-permute-start.5) | collective-permute-done | bytes 319520 | tf_op jit(solution)/shard_map/ppermute | solution.py:549
  53.1 1.1 collective-permute-done.6.refs_4_
  54.2 1.0 copy.47.mask_ref
  55.3 1.0 copy.61
  56.3 0.6 pad_add_fusion.place_ref
  57.0 0.8 copy-done.11
  57.7 0.7 copy-done.13
  58.5 25.6 %attention_forward.1 = (bf16[2,512,768]{2,1,0:T(8,128)(2,1)}, bf16[2,512,2304]{2,1,0:T(8,128)(2,1)}, bf16[2,512,768]{2,1,0:T(8,128)(2,1)}, f32[2,12,512]{2,1,0:T...) custom-call(s32[2]{0:T(128)} %group_ref.7, s32[4]{0:T(128)} %pad_add_fusion.place_ref, ...), custom_call_target="tpu_custom_call" | custom-call | flops 8999999488 | bytes 16777216 | tf_op jit(solution)/shard_map/attention_forward/pallas_call | solution.py:190
  84.1 22.2 %all-gather.3.cloned.1.call-done = bf16[6144,768]{1,0:T(8,128)(2,1)} async-done(((bf16[384,768]{1,0:T(8,128)(2,1)}), bf16[6144,768]{1,0:T(8,128)(2,1)}) %all-gather.3.cloned.1.call-update) | async-done | bytes 9437200 | tf_op jit(solution)/shard_map/all_gather | solution.py:630
  106.3 49.6 %mlp.1 = (bf16[1024,768]{1,0:T(8,128)(2,1)}, bf16[1024,768]{1,0:T(8,128)(2,1)}, bf16[16,240,768]{2,1,0:T(8,128)(2,1)}, bf16[8,192,768]{2,1,0:T(8,128)(2,1)}, bf1...) custom-call(s32[2]{0:T(128)} %group_ref.7, s32[4]{0:T(128)} %pad_add_fusion.place_ref, bf16[1024,768]{1,0:T(8,128)(2,1)} %bitcast.137, ...), custom_call_target="tpu_custom_call" | custom-call | flops 44999999488 | bytes 31457280 | tf_op jit(solution)/shard_map/mlp/pallas_call | solution.py:300
  156.3 4.6 %collective-permute-done.12 = bf16[8,192,768]{2,1,0:T(8,128)(2,1)} collective-permute-done((bf16[8,192,768]{2,1,0:T(8,128)(2,1)}, bf16[8,192,768]{2,1,0:T(8,128)(2,1)}, u32[]{:S(2)}, u32[]{:S(2)}) %collective-permute-start.12) | collective-permute-done | bytes 2359328 | tf_op jit(solution)/shard_map/ppermute | solution.py:570
  160.9 2.3 add_convert_fusion
  163.5 1.4 collective-permute-start.14
  164.9 1.1 collective-permute-start.13
  166.1 19.2 %attention_backward.2 = (bf16[2,512,1152]{2,1,0:T(8,128)(2,1)}, bf16[8,144,384]{2,1,0:T(8,128)(2,1)}, bf16[8,144,384]{2,1,0:T(8,128)(2,1)}) custom-call(s32[2]{0:T(128)} %group_ref.7, s32[4]{0:T(128)} %pad_add_fusion.place_ref, bf16[2,512,2304]{2,1,0:T(8,128)(2,1)} %get-tuple-element.81.q_ref.k_ref.v_ref, ...), custom_call_target="tpu_custom_call" | custom-call | flops 100000000 | bytes 1048576 | tf_op jit(solution)/shard_map/attention_backward/pallas_call | solution.py:404
  185.8 0.9 copy-done.10
  186.7 0.6 collective-permute-start.16
  187.3 19.1 %attention_backward.3 = (bf16[2,512,1152]{2,1,0:T(8,128)(2,1)}, bf16[8,144,384]{2,1,0:T(8,128)(2,1)}, bf16[8,144,384]{2,1,0:T(8,128)(2,1)}) custom-call(s32[2]{0:T(128)} %group_ref.7, s32[4]{0:T(128)} %pad_add_fusion.place_ref, bf16[2,512,2304]{2,1,0:T(8,128)(2,1)} %get-tuple-element.81.q_ref.k_ref.v_ref, ...), custom_call_target="tpu_custom_call" | custom-call | flops 100000000 | bytes 1048576 | tf_op jit(solution)/shard_map/attention_backward/pallas_call | solution.py:404
  206.9 0.7 copy-done.3
  208.3 3.7 %collective-permute-start.38 = (bf16[96,768]{1,0:T(8,128)(2,1)S(1)}, bf16[96,768]{1,0:T(8,128)(2,1)S(1)}, u32[]{:S(2)}, u32[]{:S(2)}) collective-permute-start(bf16[96,768]{1,0:T(8,128)(2,1)S(1)} %get-tuple-element.131), channel_id=1, source_target_pairs={{0,12},{1,13},{2,14},{3,15},{4,0},{5,1},{6,2},{7,3},{8,4},{9,5},{1... | collective-permute-start | bytes 442376 | tf_op jit(solution)/shard_map/ppermute | solution.py:584
  212.0 11.7 %norm_one_backward.1 = (bf16[1024,768]{1,0:T(8,128)(2,1)}, bf16[8,16,384]{2,1,0:T(8,128)(2,1)}, bf16[8,16,384]{2,1,0:T(8,128)(2,1)}) custom-call(s32[4]{0:T(128)} %pad_add_fusion.place_ref, bf16[1024,768]{1,0:T(8,128)(2,1)} %bitcast.138, f32[1024,1]{1,0:T(8,128)} %bitcast.131, bf16[1024,768]{1,0:T(8,128)(2,1)} %get-tuple-element.80.gb_ref, ...), custom_call_target="tpu_custom_call" | custom-call | flops 100000000 | bytes 1048576 | tf_op jit(solution)/shard_map/norm_one_backward/pallas_call | solution.py:483
  223.7 1.0 pad_maximum_fusion
  224.8 1.5 collective-permute-start.20
  226.3 1.1 collective-permute-start.18
  227.4 1.7 collective-permute-done.37
  229.4 3.3 %collective-permute-done.20 = bf16[2,144,384]{2,1,0:T(8,128)(2,1)S(1)} collective-permute-done((bf16[2,144,384]{2,1,0:T(8,128)(2,1)S(1)}, bf16[2,144,384]{2,1,0:T(8,128)(2,1)S(1)}, u32[]{:S(2)}, u32[]{:S(2)}) %collective-permute-start.20) | collective-permute-done | bytes 221216 | tf_op jit(solution)/shard_map/ppermute | solution.py:576
  232.7 0.9 collective-permute-start.21
  233.6 1.0 collective-permute-done.18
  234.7 0.8 collective-permute-start.19
  235.5 2.2 collective-permute-done.39
  237.8 0.9 fusion.2
  238.6 0.7 collective-permute-done.21
  239.7 4.2 %collective-permute-start.22 = (bf16[72,384]{1,0:T(8,128)(2,1)S(1)}, bf16[72,384]{1,0:T(8,128)(2,1)S(1)}, u32[]{:S(2)}, u32[]{:S(2)}) collective-permute-start(bf16[72,384]{1,0:T(8,128)(2,1)S(1)} %get-tuple-element.173), channel_id=1, source_target_pairs={{0,4},{1,5},{2,6},{3,7},{4,8},{5,9},{6,10},{7,11},{8,12},{9,13},{1... | collective-permute-start | bytes 165896 | tf_op jit(solution)/shard_map/ppermute | solution.py:584
  243.9 2.4 collective-permute-start.24
  246.7 1.7 collective-permute-start.29
  248.4 4.6 %collective-permute-done.23 = bf16[72,384]{1,0:T(8,128)(2,1)S(1)} collective-permute-done((bf16[72,384]{1,0:T(8,128)(2,1)S(1)}, bf16[72,384]{1,0:T(8,128)(2,1)S(1)}, u32[]{:S(2)}, u32[]{:S(2)}) %collective-permute-start.23) | collective-permute-done | bytes 55328 | tf_op jit(solution)/shard_map/ppermute | solution.py:584
  253.2 2.1 collective-permute-start.27
  255.5 5.6 %collective-permute-done.27 = bf16[2,2,80,384]{3,2,0,1:T(8,128)(2,1)S(1)} collective-permute-done((bf16[2,2,80,384]{3,2,0,1:T(8,128)(2,1)S(1)}, bf16[2,2,80,384]{3,2,0,1:T(8,128)(2,1)S(1)}, u32[]{:S(2)}, u32[]{:S(2)}) %collective-permute-start.27) | collective-permute-done | bytes 245792 | tf_op jit(solution)/shard_map/ppermute | solution.py:576
  261.2 0.9 collective-permute-start.28
  262.5 3.7 %collective-permute-done.28 = bf16[2,80,384]{2,1,0:T(8,128)(2,1)S(1)} collective-permute-done((bf16[2,80,384]{2,1,0:T(8,128)(2,1)S(1)}, bf16[2,80,384]{2,1,0:T(8,128)(2,1)S(1)}, u32[]{:S(2)}, u32[]{:S(2)}) %collective-permute-start.28) | collective-permute-done | bytes 122912 | tf_op jit(solution)/shard_map/ppermute | solution.py:580
  266.3 4.8 %collective-permute-start.31 = (bf16[80,384]{1,0:T(8,128)(2,1)S(1)}, bf16[80,384]{1,0:T(8,128)(2,1)S(1)}, u32[]{:S(2)}, u32[]{:S(2)}) collective-permute-start(bf16[80,384]{1,0:T(8,128)(2,1)S(1)} %get-tuple-element.170), channel_id=1, source_target_pairs={{0,4},{1,5},{2,6},{3,7},{4,8},{5,9},{6,10},{7,11},{8,12},{9,13},{1... | collective-permute-start | bytes 184328 | tf_op jit(solution)/shard_map/ppermute | solution.py:584
  271.1 0.9 collective-permute-start.32
  272.0 1.6 collective-permute-start.33
  273.6 2.9 collective-permute-done.32
  276.9 0.8 collective-permute-start.34
  277.7 4.2 %collective-permute-done.34 = bf16[80,384]{1,0:T(8,128)(2,1)S(1)} collective-permute-done((bf16[80,384]{1,0:T(8,128)(2,1)S(1)}, bf16[80,384]{1,0:T(8,128)(2,1)S(1)}, u32[]{:S(2)}, u32[]{:S(2)}) %collective-permute-start.34) | collective-permute-done | bytes 61472 | tf_op jit(solution)/shard_map/ppermute | solution.py:590
  282.6 0.8 collective-permute-start.35
  284.0 6.4 %collective-permute-done.35 = bf16[240,768]{1,0:T(8,128)(2,1)S(1)} collective-permute-done((bf16[240,768]{1,0:T(8,128)(2,1)}, bf16[240,768]{1,0:T(8,128)(2,1)S(1)}, u32[]{:S(2)}, u32[]{:S(2)}) %collective-permute-start.35) | collective-permute-done | bytes 368672 | tf_op jit(solution)/shard_map/ppermute | solution.py:618
  290.4 1.1 convert_add_fusion
  291.4 0.7 fusion.40
  292.2 0.9 pad_maximum_fusion.2
  (121 shorter events, 6.8 us)
Async XLA Ops:
  7.2 99.1 %all-gather.3.cloned.1.call-start = ((), (), s32[]{:S(2)}) async-start(), calls=%async_computation.2 | async-start | bytes 10027008 | tf_op jit(solution)/shard_map/all_gather | solution.py:630
  9.7 39.1 %copy-start.9 = (s32[2,128]{1,0:T(2,128)S(1)}, s32[2,128]{1,0:T(2,128)}, u32[]{:S(2)}) copy-start(s32[2,128]{1,0:T(2,128)} %param.19) | copy-start | bytes 3076
  9.8 272.8 %reduce-scatter.2.cloned.1.call-start = ((), (), s32[]{:S(2)}) async-start(), calls=%async_computation.1 | async-start | bytes 6266880 | tf_op jit(solution)/shard_map/reduce_scatter | solution.py:617
  10.8 10.1 %collective-permute-start = (bf16[208,384]{1,0:T(8,128)(2,1)S(1)}, bf16[208,384]{1,0:T(8,128)(2,1)S(1)}, u32[]{:S(2)}, u32[]{:S(2)}) collective-permute-start(bf16[208,384]{1,0:T(8,128)(2,1)S(1)} %constant_dynamic-slice_fusion.10), channel_id=1, source_target_pairs={{0,4},{1,5},{2,6},{3,7},{4,8},{5,9},{6,10},{7,11},{8,12},{9,13},{1... | collective-permute-start | bytes 479240 | tf_op jit(solution)/shard_map/ppermute | solution.py:546
  13.8 15.7 %collective-permute-start.1 = (bf16[208,384]{1,0:T(8,128)(2,1)S(1)}, bf16[208,384]{1,0:T(8,128)(2,1)S(1)}, u32[]{:S(2)}, u32[]{:S(2)}) collective-permute-start(bf16[208,384]{1,0:T(8,128)(2,1)S(1)} %constant_dynamic-slice_fusion.10), channel_id=1, source_target_pairs={{0,8},{1,9},{2,10},{3,11},{4,12},{5,13},{6,14},{7,15},{8,0},{9,1},... | collective-permute-start | bytes 479240 | tf_op jit(solution)/shard_map/ppermute | solution.py:546
  16.4 13.1 %collective-permute-start.2 = (bf16[208,384]{1,0:T(8,128)(2,1)S(1)}, bf16[208,384]{1,0:T(8,128)(2,1)S(1)}, u32[]{:S(2)}, u32[]{:S(2)}) collective-permute-start(bf16[208,384]{1,0:T(8,128)(2,1)S(1)} %constant_dynamic-slice_fusion.10), channel_id=1, source_target_pairs={{0,12},{1,13},{2,14},{3,15},{4,0},{5,1},{6,2},{7,3},{8,4},{9,5},{1... | collective-permute-start | bytes 479240 | tf_op jit(solution)/shard_map/ppermute | solution.py:546
  29.7 27.3 %copy-start.4 = (bf16[4,208,384]{2,1,0:T(8,128)(2,1)}, bf16[4,208,384]{2,1,0:T(8,128)(2,1)S(1)}, u32[]{:S(2)}) copy-start(bf16[4,208,384]{2,1,0:T(8,128)(2,1)S(1)} %pad_maximum_fusion.1.refs_0_) | copy-start | bytes 1916932
  29.7 15.3 %collective-permute-start.3 = (bf16[4,208,384]{2,1,0:T(8,128)(2,1)S(1)}, bf16[4,208,384]{2,1,0:T(8,128)(2,1)S(1)}, u32[]{:S(2)}, u32[]{:S(2)}) collective-permute-start(bf16[4,208,384]{2,1,0:T(8,128)(2,1)S(1)} %pad_maximum_fusion.1.refs_0_), channel_id=1, source_target_pairs={{0,16},{16,0},{1,17},{17,1},{2,18},{18,2},{3,19},{19,3},{4,20},{20... | collective-permute-start | bytes 1916936 | tf_op jit(solution)/shard_map/ppermute | solution.py:547
  31.3 15.4 %collective-permute-start.4 = (bf16[4,208,384]{2,1,0:T(8,128)(2,1)S(1)}, bf16[4,208,384]{2,1,0:T(8,128)(2,1)S(1)}, u32[]{:S(2)}, u32[]{:S(2)}) collective-permute-start(bf16[4,208,384]{2,1,0:T(8,128)(2,1)S(1)} %pad_maximum_fusion.1.refs_0_), channel_id=1, source_target_pairs={{0,2},{1,3},{2,0},{3,1},{4,6},{5,7},{6,4},{7,5},{8,10},{9,11},{10,... | collective-permute-start | bytes 1916936 | tf_op jit(solution)/shard_map/ppermute | solution.py:548
  45.0 11.9 %copy-start.5 = (bf16[4,208,384]{2,1,0:T(8,128)(2,1)}, bf16[4,208,384]{2,1,0:T(8,128)(2,1)S(1)}, u32[]{:S(2)}) copy-start(bf16[4,208,384]{2,1,0:T(8,128)(2,1)S(1)} %collective-permute-done.3.refs_1_) | copy-start | bytes 1916932
  45.0 8.0 %collective-permute-start.5 = (bf16[2,208,384]{2,1,0:T(8,128)(2,1)S(1)}, bf16[2,208,384]{2,1,0:T(8,128)(2,1)S(1)}, u32[]{:S(2)}, u32[]{:S(2)}) collective-permute-start(bf16[2,208,384]{2,1,0:T(8,128)(2,1)S(1)} %slice.145), channel_id=1, source_target_pairs={{0,2},{1,3},{2,0},{3,1},{4,6},{5,7},{6,4},{7,5},{8,10},{9,11},{10,... | collective-permute-start | bytes 958472 | tf_op jit(solution)/shard_map/ppermute | solution.py:549
  46.7 10.3 %copy-start.6 = (bf16[4,208,384]{2,1,0:T(8,128)(2,1)}, bf16[4,208,384]{2,1,0:T(8,128)(2,1)S(1)}, u32[]{:S(2)}) copy-start(bf16[4,208,384]{2,1,0:T(8,128)(2,1)S(1)} %collective-permute-done.4.refs_2_) | copy-start | bytes 1916932
  46.7 7.5 %collective-permute-start.6 = (bf16[2,208,384]{2,1,0:T(8,128)(2,1)S(1)}, bf16[2,208,384]{2,1,0:T(8,128)(2,1)}, u32[]{:S(2)}, u32[]{:S(2)}) collective-permute-start(bf16[2,208,384]{2,1,0:T(8,128)(2,1)S(1)} %slice.146), channel_id=1, source_target_pairs={{0,16},{16,0},{1,17},{17,1},{2,18},{18,2},{3,19},{19,3},{4,20},{20... | collective-permute-start | bytes 958472 | tf_op jit(solution)/shard_map/ppermute | solution.py:550
  48.3 8.6 %collective-permute-start.7 = (bf16[4,208,384]{2,1,0:T(8,128)(2,1)S(1)}, bf16[4,208,384]{2,1,0:T(8,128)(2,1)S(1)}, u32[]{:S(2)}, u32[]{:S(2)}) collective-permute-start(bf16[4,208,384]{2,1,0:T(8,128)(2,1)S(1)} %pad_maximum_fusion.1.refs_0_), channel_id=1, source_target_pairs={{0,1},{1,0},{2,3},{3,2},{4,5},{5,4},{6,7},{7,6},{8,9},{9,8},{10,11... | collective-permute-start | bytes 1916936 | tf_op jit(solution)/shard_map/ppermute | solution.py:552
  48.3 8.6 %collective-permute-start.8 = (bf16[4,208,384]{2,1,0:T(8,128)(2,1)S(1)}, bf16[4,208,384]{2,1,0:T(8,128)(2,1)}, u32[]{:S(2)}, u32[]{:S(2)}) collective-permute-start(bf16[4,208,384]{2,1,0:T(8,128)(2,1)S(1)} %collective-permute-done.3.refs_1_), channel_id=1, source_target_pairs={{0,1},{1,0},{2,3},{3,2},{4,5},{5,4},{6,7},{7,6},{8,9},{9,8},{10,11... | collective-permute-start | bytes 1916936 | tf_op jit(solution)/shard_map/ppermute | solution.py:552
  48.8 8.1 %collective-permute-start.9 = (bf16[4,208,384]{2,1,0:T(8,128)(2,1)S(1)}, bf16[4,208,384]{2,1,0:T(8,128)(2,1)}, u32[]{:S(2)}, u32[]{:S(2)}) collective-permute-start(bf16[4,208,384]{2,1,0:T(8,128)(2,1)S(1)} %collective-permute-done.4.refs_2_), channel_id=1, source_target_pairs={{0,1},{1,0},{2,3},{3,2},{4,5},{5,4},{6,7},{7,6},{8,9},{9,8},{10,11... | collective-permute-start | bytes 1916936 | tf_op jit(solution)/shard_map/ppermute | solution.py:552
  53.1 3.9 %copy-start.12 = (bf16[2,208,384]{2,1,0:T(8,128)(2,1)}, bf16[2,208,384]{2,1,0:T(8,128)(2,1)S(1)}, u32[]{:S(2)}) copy-start(bf16[2,208,384]{2,1,0:T(8,128)(2,1)S(1)} %collective-permute-done.5.refs_3_) | copy-start | bytes 958468
  53.1 3.8 %collective-permute-start.10 = (bf16[2,208,384]{2,1,0:T(8,128)(2,1)S(1)}, bf16[2,208,384]{2,1,0:T(8,128)(2,1)}, u32[]{:S(2)}, u32[]{:S(2)}) collective-permute-start(bf16[2,208,384]{2,1,0:T(8,128)(2,1)S(1)} %collective-permute-done.5.refs_3_), channel_id=1, source_target_pairs={{0,1},{1,0},{2,3},{3,2},{4,5},{5,4},{6,7},{7,6},{8,9},{9,8},{10,11... | collective-permute-start | bytes 958472 | tf_op jit(solution)/shard_map/ppermute | solution.py:552
  54.2 2.7 collective-permute-start.11
  56.9 0.8 copy-start.11
  57.7 0.7 copy-start.13
  155.9 4.9 %collective-permute-start.12 = (bf16[8,192,768]{2,1,0:T(8,128)(2,1)}, bf16[8,192,768]{2,1,0:T(8,128)(2,1)}, u32[]{:S(2)}, u32[]{:S(2)}) collective-permute-start(bf16[8,192,768]{2,1,0:T(8,128)(2,1)} %get-tuple-element.84), channel_id=1, source_target_pairs={{0,1},{1,0},{2,3},{3,2},{4,5},{5,4},{6,7},{7,6},{8,9},{9,8},{10,11... | collective-permute-start | bytes 7077896 | tf_op jit(solution)/shard_map/ppermute | solution.py:570
  156.3 4.6 %copy-start = (bf16[8,192,768]{2,1,0:T(8,128)(2,1)S(1)}, bf16[8,192,768]{2,1,0:T(8,128)(2,1)}, u32[]{:S(2)}) copy-start(bf16[8,192,768]{2,1,0:T(8,128)(2,1)} %get-tuple-element.83) | copy-start | bytes 7077892
  163.5 21.8 %collective-permute-start.14 = (bf16[2,192,768]{2,1,0:T(8,128)(2,1)S(1)}, bf16[2,192,768]{2,1,0:T(8,128)(2,1)S(1)}, u32[]{:S(2)}, u32[]{:S(2)}) collective-permute-start(bf16[2,192,768]{2,1,0:T(8,128)(2,1)S(1)} %get-tuple-element.95), channel_id=1, source_target_pairs={{0,2},{1,3},{2,0},{3,1},{4,6},{5,7},{6,4},{7,5},{8,10},{9,11},{10,... | collective-permute-start | bytes 1769480 | tf_op jit(solution)/shard_map/ppermute | solution.py:576
  164.9 20.6 %collective-permute-start.13 = (bf16[2,2,96,768]{3,2,1,0:T(8,128)(2,1)S(1)}, bf16[2,2,96,768]{3,2,1,0:T(8,128)(2,1)S(1)}, u32[]{:S(2)}, u32[]{:S(2)}) collective-permute-start(bf16[2,2,96,768]{3,2,1,0:T(8,128)(2,1)S(1)} %get-tuple-element.93), channel_id=1, source_target_pairs={{0,16},{16,0},{1,17},{17,1},{2,18},{18,2},{3,19},{19,3},{4,20},{20... | collective-permute-start | bytes 1769480 | tf_op jit(solution)/shard_map/ppermute | solution.py:576
  185.4 1.3 copy-start.10
  185.7 20.7 %collective-permute-start.17 = (bf16[2,96,768]{2,1,0:T(8,128)(2,1)S(1)}, bf16[2,96,768]{2,1,0:T(8,128)(2,1)S(1)}, u32[]{:S(2)}, u32[]{:S(2)}) collective-permute-start(bf16[2,96,768]{2,1,0:T(8,128)(2,1)S(1)} %get-tuple-element.107), channel_id=1, source_target_pairs={{0,16},{16,0},{1,17},{17,1},{2,18},{18,2},{3,19},{19,3},{4,20},{20... | collective-permute-start | bytes 884744 | tf_op jit(solution)/shard_map/ppermute | solution.py:580
  186.7 20.2 %collective-permute-start.15 = (bf16[8,144,384]{2,1,0:T(8,128)(2,1)S(1)}, bf16[8,144,384]{2,1,0:T(8,128)(2,1)S(1)}, u32[]{:S(2)}, u32[]{:S(2)}) collective-permute-start(bf16[8,144,384]{2,1,0:T(8,128)(2,1)S(1)} %copy-done.10), channel_id=1, source_target_pairs={{0,1},{1,0},{2,3},{3,2},{4,5},{5,4},{6,7},{7,6},{8,9},{9,8},{10,11... | collective-permute-start | bytes 2654216 | tf_op jit(solution)/shard_map/ppermute | solution.py:570
  186.7 19.8 %collective-permute-start.16 = (bf16[2,96,768]{2,1,0:T(8,128)(2,1)S(1)}, bf16[2,96,768]{2,1,0:T(8,128)(2,1)S(1)}, u32[]{:S(2)}, u32[]{:S(2)}) collective-permute-start(bf16[2,96,768]{2,1,0:T(8,128)(2,1)S(1)} %get-tuple-element.105), channel_id=1, source_target_pairs={{0,2},{1,3},{2,0},{3,1},{4,6},{5,7},{6,4},{7,5},{8,10},{9,11},{10,... | collective-permute-start | bytes 884744 | tf_op jit(solution)/shard_map/ppermute | solution.py:580
  206.4 1.2 copy-start.3
  208.2 18.2 %collective-permute-start.36 = (bf16[96,768]{1,0:T(8,128)(2,1)S(1)}, bf16[96,768]{1,0:T(8,128)(2,1)S(1)}, u32[]{:S(2)}, u32[]{:S(2)}) collective-permute-start(bf16[96,768]{1,0:T(8,128)(2,1)S(1)} %get-tuple-element.129), channel_id=1, source_target_pairs={{0,4},{1,5},{2,6},{3,7},{4,8},{5,9},{6,10},{7,11},{8,12},{9,13},{1... | collective-permute-start | bytes 442376 | tf_op jit(solution)/shard_map/ppermute | solution.py:584
  208.2 20.9 %collective-permute-start.37 = (bf16[96,768]{1,0:T(8,128)(2,1)S(1)}, bf16[96,768]{1,0:T(8,128)(2,1)S(1)}, u32[]{:S(2)}, u32[]{:S(2)}) collective-permute-start(bf16[96,768]{1,0:T(8,128)(2,1)S(1)} %get-tuple-element.130), channel_id=1, source_target_pairs={{0,8},{1,9},{2,10},{3,11},{4,12},{5,13},{6,14},{7,15},{8,0},{9,1},... | collective-permute-start | bytes 442376 | tf_op jit(solution)/shard_map/ppermute | solution.py:584
  208.3 20.9 %collective-permute-start.38 = (bf16[96,768]{1,0:T(8,128)(2,1)S(1)}, bf16[96,768]{1,0:T(8,128)(2,1)S(1)}, u32[]{:S(2)}, u32[]{:S(2)}) collective-permute-start(bf16[96,768]{1,0:T(8,128)(2,1)S(1)} %get-tuple-element.131), channel_id=1, source_target_pairs={{0,12},{1,13},{2,14},{3,15},{4,0},{5,1},{6,2},{7,3},{8,4},{9,5},{1... | collective-permute-start | bytes 442376 | tf_op jit(solution)/shard_map/ppermute | solution.py:584
  212.0 11.7 %copy-start.2 = (bf16[8,144,384]{2,1,0:T(8,128)(2,1)S(1)}, bf16[8,144,384]{2,1,0:T(8,128)(2,1)}, u32[]{:S(2)}) copy-start(bf16[8,144,384]{2,1,0:T(8,128)(2,1)} %get-tuple-element.125) | copy-start | bytes 2654212
  224.7 21.6 %collective-permute-start.26 = (bf16[8,160,384]{2,1,0:T(8,128)(2,1)S(1)}, bf16[8,160,384]{2,1,0:T(8,128)(2,1)S(1)}, u32[]{:S(2)}, u32[]{:S(2)}) collective-permute-start(bf16[8,160,384]{2,1,0:T(8,128)(2,1)S(1)} %pad_maximum_fusion), channel_id=1, source_target_pairs={{0,1},{1,0},{2,3},{3,2},{4,5},{5,4},{6,7},{7,6},{8,9},{9,8},{10,11... | collective-permute-start | bytes 2949128 | tf_op jit(solution)/shard_map/ppermute | solution.py:570
  224.8 7.8 %collective-permute-start.20 = (bf16[2,144,384]{2,1,0:T(8,128)(2,1)S(1)}, bf16[2,144,384]{2,1,0:T(8,128)(2,1)S(1)}, u32[]{:S(2)}, u32[]{:S(2)}) collective-permute-start(bf16[2,144,384]{2,1,0:T(8,128)(2,1)S(1)} %get-tuple-element.122), channel_id=1, source_target_pairs={{0,2},{1,3},{2,0},{3,1},{4,6},{5,7},{6,4},{7,5},{8,10},{9,11},{10,... | collective-permute-start | bytes 663560 | tf_op jit(solution)/shard_map/ppermute | solution.py:576
  226.3 8.3 %collective-permute-start.18 = (bf16[2,2,72,384]{3,2,0,1:T(8,128)(2,1)S(1)}, bf16[2,2,72,384]{3,2,0,1:T(8,128)(2,1)S(1)}, u32[]{:S(2)}, u32[]{:S(2)}) collective-permute-start(bf16[2,2,72,384]{3,2,0,1:T(8,128)(2,1)S(1)} %copy.55), channel_id=1, source_target_pairs={{0,16},{16,0},{1,17},{17,1},{2,18},{18,2},{3,19},{19,3},{4,20},{20... | collective-permute-start | bytes 663560 | tf_op jit(solution)/shard_map/ppermute | solution.py:576
  229.3 17.0 %copy-start.1 = (bf16[8,144,384]{2,1,0:T(8,128)(2,1)S(1)}, bf16[8,144,384]{2,1,0:T(8,128)(2,1)}, u32[]{:S(2)}) copy-start(bf16[8,144,384]{2,1,0:T(8,128)(2,1)} %get-tuple-element.123) | copy-start | bytes 2654212
  229.3 17.0 %copy-start.7 = (bf16[8,16,384]{2,1,0:T(8,128)(2,1)S(1)}, bf16[8,16,384]{2,1,0:T(8,128)(2,1)}, u32[]{:S(2)}) copy-start(bf16[8,16,384]{2,1,0:T(8,128)(2,1)} %get-tuple-element.124) | copy-start | bytes 294916
  229.3 8.5 %collective-permute-start.39 = (bf16[96,768]{1,0:T(8,128)(2,1)S(1)}, bf16[96,768]{1,0:T(8,128)(2,1)S(1)}, u32[]{:S(2)}, u32[]{:S(2)}) collective-permute-start(bf16[96,768]{1,0:T(8,128)(2,1)S(1)} %add_convert_fusion.10), channel_id=1, source_target_pairs={{0,16},{16,0},{1,17},{17,1},{2,18},{18,2},{3,19},{19,3},{4,20},{20... | collective-permute-start | bytes 442376 | tf_op jit(solution)/shard_map/ppermute | solution.py:590
  232.7 6.6 %collective-permute-start.21 = (bf16[2,72,384]{2,1,0:T(8,128)(2,1)S(1)}, bf16[2,72,384]{2,1,0:T(8,128)(2,1)S(1)}, u32[]{:S(2)}, u32[]{:S(2)}) collective-permute-start(bf16[2,72,384]{2,1,0:T(8,128)(2,1)S(1)} %constant_dynamic-slice_fusion.3), channel_id=1, source_target_pairs={{0,16},{16,0},{1,17},{17,1},{2,18},{18,2},{3,19},{19,3},{4,20},{20... | collective-permute-start | bytes 331784 | tf_op jit(solution)/shard_map/ppermute | solution.py:580
  234.7 4.8 %collective-permute-start.19 = (bf16[2,72,384]{2,1,0:T(8,128)(2,1)S(1)}, bf16[2,72,384]{2,1,0:T(8,128)(2,1)S(1)}, u32[]{:S(2)}, u32[]{:S(2)}) collective-permute-start(bf16[2,72,384]{2,1,0:T(8,128)(2,1)S(1)} %dynamic-slice_bitcast_fusion.8), channel_id=1, source_target_pairs={{0,2},{1,3},{2,0},{3,1},{4,6},{5,7},{6,4},{7,5},{8,10},{9,11},{10,... | collective-permute-start | bytes 331784 | tf_op jit(solution)/shard_map/ppermute | solution.py:580
  239.7 8.7 %collective-permute-start.22 = (bf16[72,384]{1,0:T(8,128)(2,1)S(1)}, bf16[72,384]{1,0:T(8,128)(2,1)S(1)}, u32[]{:S(2)}, u32[]{:S(2)}) collective-permute-start(bf16[72,384]{1,0:T(8,128)(2,1)S(1)} %get-tuple-element.173), channel_id=1, source_target_pairs={{0,4},{1,5},{2,6},{3,7},{4,8},{5,9},{6,10},{7,11},{8,12},{9,13},{1... | collective-permute-start | bytes 165896 | tf_op jit(solution)/shard_map/ppermute | solution.py:584
  243.9 9.1 %collective-permute-start.23 = (bf16[72,384]{1,0:T(8,128)(2,1)S(1)}, bf16[72,384]{1,0:T(8,128)(2,1)S(1)}, u32[]{:S(2)}, u32[]{:S(2)}) collective-permute-start(bf16[72,384]{1,0:T(8,128)(2,1)S(1)} %get-tuple-element.174), channel_id=1, source_target_pairs={{0,8},{1,9},{2,10},{3,11},{4,12},{5,13},{6,14},{7,15},{8,0},{9,1},... | collective-permute-start | bytes 165896 | tf_op jit(solution)/shard_map/ppermute | solution.py:584
  243.9 9.1 %collective-permute-start.24 = (bf16[72,384]{1,0:T(8,128)(2,1)S(1)}, bf16[72,384]{1,0:T(8,128)(2,1)S(1)}, u32[]{:S(2)}, u32[]{:S(2)}) collective-permute-start(bf16[72,384]{1,0:T(8,128)(2,1)S(1)} %get-tuple-element.175), channel_id=1, source_target_pairs={{0,12},{1,13},{2,14},{3,15},{4,0},{5,1},{6,2},{7,3},{8,4},{9,5},{1... | collective-permute-start | bytes 165896 | tf_op jit(solution)/shard_map/ppermute | solution.py:584
  246.7 8.5 %collective-permute-start.29 = (bf16[2,160,384]{2,1,0:T(8,128)(2,1)S(1)}, bf16[2,160,384]{2,1,0:T(8,128)(2,1)S(1)}, u32[]{:S(2)}, u32[]{:S(2)}) collective-permute-start(bf16[2,160,384]{2,1,0:T(8,128)(2,1)S(1)} %dynamic-slice_bitcast_fusion.4), channel_id=1, source_target_pairs={{0,2},{1,3},{2,0},{3,1},{4,6},{5,7},{6,4},{7,5},{8,10},{9,11},{10,... | collective-permute-start | bytes 737288 | tf_op jit(solution)/shard_map/ppermute | solution.py:576
  253.0 20.5 %collective-permute-start.25 = (bf16[72,384]{1,0:T(8,128)(2,1)S(1)}, bf16[72,384]{1,0:T(8,128)(2,1)S(1)}, u32[]{:S(2)}, u32[]{:S(2)}) collective-permute-start(bf16[72,384]{1,0:T(8,128)(2,1)S(1)} %fusion.20), channel_id=1, source_target_pairs={{0,16},{16,0},{1,17},{17,1},{2,18},{18,2},{3,19},{19,3},{4,20},{20... | collective-permute-start | bytes 165896 | tf_op jit(solution)/shard_map/ppermute | solution.py:590
  253.2 7.9 %collective-permute-start.27 = (bf16[2,2,80,384]{3,2,0,1:T(8,128)(2,1)S(1)}, bf16[2,2,80,384]{3,2,0,1:T(8,128)(2,1)S(1)}, u32[]{:S(2)}, u32[]{:S(2)}) collective-permute-start(bf16[2,2,80,384]{3,2,0,1:T(8,128)(2,1)S(1)} %copy.58), channel_id=1, source_target_pairs={{0,16},{16,0},{1,17},{17,1},{2,18},{18,2},{3,19},{19,3},{4,20},{20... | collective-permute-start | bytes 737288 | tf_op jit(solution)/shard_map/ppermute | solution.py:576
  255.4 7.0 %collective-permute-start.30 = (bf16[2,80,384]{2,1,0:T(8,128)(2,1)S(1)}, bf16[2,80,384]{2,1,0:T(8,128)(2,1)S(1)}, u32[]{:S(2)}, u32[]{:S(2)}) collective-permute-start(bf16[2,80,384]{2,1,0:T(8,128)(2,1)S(1)} %constant_dynamic-slice_fusion), channel_id=1, source_target_pairs={{0,16},{16,0},{1,17},{17,1},{2,18},{18,2},{3,19},{19,3},{4,20},{20... | collective-permute-start | bytes 368648 | tf_op jit(solution)/shard_map/ppermute | solution.py:580
  261.2 4.9 %collective-permute-start.28 = (bf16[2,80,384]{2,1,0:T(8,128)(2,1)S(1)}, bf16[2,80,384]{2,1,0:T(8,128)(2,1)S(1)}, u32[]{:S(2)}, u32[]{:S(2)}) collective-permute-start(bf16[2,80,384]{2,1,0:T(8,128)(2,1)S(1)} %dynamic-slice_bitcast_fusion.7), channel_id=1, source_target_pairs={{0,2},{1,3},{2,0},{3,1},{4,6},{5,7},{6,4},{7,5},{8,10},{9,11},{10,... | collective-permute-start | bytes 368648 | tf_op jit(solution)/shard_map/ppermute | solution.py:580
  266.3 7.3 %collective-permute-start.31 = (bf16[80,384]{1,0:T(8,128)(2,1)S(1)}, bf16[80,384]{1,0:T(8,128)(2,1)S(1)}, u32[]{:S(2)}, u32[]{:S(2)}) collective-permute-start(bf16[80,384]{1,0:T(8,128)(2,1)S(1)} %get-tuple-element.170), channel_id=1, source_target_pairs={{0,4},{1,5},{2,6},{3,7},{4,8},{5,9},{6,10},{7,11},{8,12},{9,13},{1... | collective-permute-start | bytes 184328 | tf_op jit(solution)/shard_map/ppermute | solution.py:584
  271.1 5.4 %collective-permute-start.32 = (bf16[80,384]{1,0:T(8,128)(2,1)S(1)}, bf16[80,384]{1,0:T(8,128)(2,1)S(1)}, u32[]{:S(2)}, u32[]{:S(2)}) collective-permute-start(bf16[80,384]{1,0:T(8,128)(2,1)S(1)} %get-tuple-element.171), channel_id=1, source_target_pairs={{0,8},{1,9},{2,10},{3,11},{4,12},{5,13},{6,14},{7,15},{8,0},{9,1},... | collective-permute-start | bytes 184328 | tf_op jit(solution)/shard_map/ppermute | solution.py:584
  272.0 4.9 %collective-permute-start.33 = (bf16[80,384]{1,0:T(8,128)(2,1)S(1)}, bf16[80,384]{1,0:T(8,128)(2,1)S(1)}, u32[]{:S(2)}, u32[]{:S(2)}) collective-permute-start(bf16[80,384]{1,0:T(8,128)(2,1)S(1)} %get-tuple-element.172), channel_id=1, source_target_pairs={{0,12},{1,13},{2,14},{3,15},{4,0},{5,1},{6,2},{7,3},{8,4},{9,5},{1... | collective-permute-start | bytes 184328 | tf_op jit(solution)/shard_map/ppermute | solution.py:584
  276.9 5.0 %collective-permute-start.34 = (bf16[80,384]{1,0:T(8,128)(2,1)S(1)}, bf16[80,384]{1,0:T(8,128)(2,1)S(1)}, u32[]{:S(2)}, u32[]{:S(2)}) collective-permute-start(bf16[80,384]{1,0:T(8,128)(2,1)S(1)} %fusion.16), channel_id=1, source_target_pairs={{0,16},{16,0},{1,17},{17,1},{2,18},{18,2},{3,19},{19,3},{4,20},{20... | collective-permute-start | bytes 184328 | tf_op jit(solution)/shard_map/ppermute | solution.py:590
  282.6 7.8 %collective-permute-start.35 = (bf16[240,768]{1,0:T(8,128)(2,1)}, bf16[240,768]{1,0:T(8,128)(2,1)S(1)}, u32[]{:S(2)}, u32[]{:S(2)}) collective-permute-start(bf16[240,768]{1,0:T(8,128)(2,1)} %bitcast.139), channel_id=1, source_target_pairs={{0,16},{16,0},{1,17},{17,1},{2,18},{18,2},{3,19},{19,3},{4,20},{20... | collective-permute-start | bytes 1105928 | tf_op jit(solution)/shard_map/ppermute | solution.py:618
  283.9 9.1 %copy-start.8 = (f32[48,2304]{1,0:T(8,128)}, f32[48,2304]{1,0:T(8,128)S(1)}, u32[]{:S(2)}) copy-start(f32[48,2304]{1,0:T(8,128)S(1)} %slice_dynamic-update-slice_fusion) | copy-start | bytes 1327108
Sparse Core Ops, SparseCore 0:
  10.9 95.3 all-gather.2
  156.4 102.0 reduce-scatter.1
where the time goes:
time: 306 us; the launch traced here: 300 us
  Pallas kernels  128 us (42%)
  waiting for transfers between devices  92.4 us (30%)
  starting transfers between devices  46.1 us (15%)
  between operations  15.1 us (5%)
  local copies, waits for them, and re-layouts  10.1 us (3%)
  other arithmetic  8.86 us (3%)
    pallas_call x1, Pallas kernels, mlp_call(): pl.pallas_call(mlp_kernel, grid_spec=pltpu.PrefetchScalarGridSpec(num_sca...  49.6 us
    pallas_call x2, Pallas kernels, attention_back_call(): pl.pallas_call(functools.partial(attention_back_kernel, part), grid_spec=...  38.3 us
    pallas_call x1, Pallas kernels, forward_call(): pl.pallas_call(functools.partial(forward_kernel, len(pieces)), grid_spec=...  25.6 us
    all_gather x1, waiting for transfers between devices, local(): w2 = lax.all_gather(pack2, 'fsdp', axis=0)  22.2 us
    ppermute x9, starting transfers between devices, scatter_steps(): got = [lax.ppermute(sent[k], 'fsdp', turn(k)) for k in (1, 2, 3)]  17.8 us
    ppermute x1, waiting for transfers between devices, gather_pieces(): by_x = lax.ppermute(along_z, 'rep', REP)  12.2 us
    pallas_call x1, Pallas kernels, norm_one_call(): pl.pallas_call(norm_one_kernel, grid_spec=pltpu.PrefetchScalarGridSpec(nu...  11.7 us
    ppermute x3, waiting for transfers between devices, gather_pieces(): lax.ppermute(half, 'fsdp', turn(k))  10.9 us
  transfers between devices with their start and end apart: 42, of which 21 were waited for; matrix products, arithmetic and copies ran while one was open for 4% of the time, Pallas kernels for 25%

commit v1 on v0

--- a/solution.py
+++ b/solution.py
@@ -566,10 +566,10 @@
 
 
 def scatter_steps(keep, send, z, y, r):
-    _, rows, dim = keep.shape
-    got = lax.ppermute(send, "fsdp", swap(1))
-    kept = yield (keep,)
-    summed = add(kept[0], got).reshape(4, 2, rows, dim)
+    got = [lax.ppermute(a, "fsdp", swap(1)) for a in send]
+    kept = yield tuple(keep)
+    summed = jnp.concatenate([add(*pair) for pair in zip(kept, got)], 1)
+    summed = summed.reshape(4, 2, *summed.shape[1:])
     a, b = summed[:2], summed[2:]
     kept = half_of(a, r), pick(b, y, 1)
     sent = yield half_of(a, 1 - r), pick(b, 1 - y, 1), *kept
@@ -597,15 +597,12 @@
         self.steps = scatter_steps(*args)
         self.value = next(self.steps)
 
-    def go(self, *ties):
-        self.value, *ties = lax.optimization_barrier((self.value, *ties))
-        self.value = self.steps.send(self.value)
-        return ties
-
-    def finish(self):
-        while isinstance(self.value, tuple):
-            self.value = self.steps.send(self.value)
-        return self.value
+
+def step(scatters, *ties):
+    values, ties = lax.optimization_barrier(([s.value for s in scatters], list(ties)))
+    for s, value in zip(scatters, values):
+        s.value = s.steps.send(value)
+    return ties
 
 
 def by_core(keep, send, c):
@@ -660,29 +657,39 @@
     back = lambda part, gb3: attention_back_call(part, group_id, place, qkv, lse, gb3, w1, flat(normed))
     after = lambda gj0, gj1, gvec: norm_one_call(place, flat(tokens), flat(mask), gb, flat(gj0), flat(gj1), vecs, w1, gvec)
     if n == BLOCKS:
-        down = Scatter(down_keep, down_send, z, y, r)
-        down.go()
-        (gb3,) = down.go(gb3)
+        down = Scatter([down_keep], [down_send], z, y, r)
+        step([down])
+        (gb3,) = step([down], gb3)
         gj0, keep0, send0 = back(0, gb3)
-        keep0, send0 = down.go(keep0, send0)
-        (gb3,) = down.go(gb3)
-        first = Scatter(keep0, send0, z, y, r)
+        keep0, send0 = step([down], keep0, send0)
+        (gb3,) = step([down], gb3)
         gj1, keep1, send1 = back(1, gb3)
-        keep1, send1 = down.go(keep1, send1)
-        (gvec,) = down.go(gvec)
-        first.go()
-        (gvec,) = first.go(gvec)
+        keep0, keep1, send0, send1 = step([down], keep0, keep1, send0, send1)
+        rest = Scatter([keep0, keep1], [send0, send1], z, y, r)
+        step([rest])
+        (gvec,) = step([rest], gvec)
         token_grad, keep2, send2 = after(gj0, gj1, gvec)
-        keep2, send2 = down.go(keep2, send2)
-        keep2, send2 = first.go(keep2, send2)
-        second = Scatter(jnp.concatenate([keep1, keep2], 1), jnp.concatenate([send1, send2], 1), z, y, r)
-        down_grad = down.finish()
-        sum0 = first.finish()
-        sum1 = second.finish()
-        sum2 = scatter_whole(g2)
+        keep2, send2 = step([rest], keep2, send2)
+        keep2, send2 = step([down, rest], keep2, send2)
+        few = add(keep2, lax.ppermute(send2, "fsdp", swap(1))).reshape(4, 2, *keep2.shape[1:])
+        few = add(pick(few, y, 1), lax.ppermute(pick(few, 1 - y, 1), "fsdp", swap(2)))
+        few = step([down, rest], *(pick(few, (z + k) % 4, 0) for k in range(4)))
+        own2 = lax.psum_scatter(g2, "fsdp", scatter_dimension=0)
+        *few, own2 = step([down, rest], *few, own2)
+        other2 = lax.ppermute(own2, "rep", REP)
+        got = [lax.ppermute(few[k], "fsdp", turn(k)) for k in (1, 2, 3)]
+        few, own2 = step([down, rest], few[0], own2)
+        total = few.astype(F32)
+        for term in got:
+            total += term.astype(F32)
+        (few,) = step([rest], total.astype(BF))
+        sum2 = own2.astype(F32) + other2.astype(F32)
+        few = few.astype(F32) + lax.ppermute(few, "rep", REP).astype(F32)
+        sum1 = rest.steps.send(rest.value)
+        down_grad = down.value
         up_grad, out_grad = sum2[: 4 * width], sum2[4 * width :]
-        qkv_grad = jnp.concatenate([a[i * width : (i + 1) * width] for i in range(3) for a in (sum0, sum1)], 1)
-        vg = [sum1[3 * width + k, :width] for k in range(B_UP)] + [sum1[3 * width + B_UP, : 4 * width]]
+        qkv_grad = jnp.concatenate([sum1[i * width : (i + 1) * width] for i in (0, 3, 1, 4, 2, 5)], 1)
+        vg = [few[k, :width] for k in range(B_UP)] + [few[B_UP, : 4 * width]]
     else:
         (gj0, *parts0), (gj1, *parts1) = (back(part, gb3) for part in range(GROUPS))
         token_grad, *table = after(gj0, gj1, gvec)

time: 306 us -> 295 us (0.964)
  the two profiles are of different devices: /device:TPU:0 before, /device:TPU:8 now
where the time goes in v1:
time: 295 us; the launch traced here: 290 us
  Pallas kernels  129 us (44%)
  waiting for transfers between devices  92.6 us (31%)
  starting transfers between devices  35.9 us (12%)
  between operations  15.1 us (5%)
  local copies, waits for them, and re-layouts  9.59 us (3%)
  other arithmetic  8.1 us (3%)
    pallas_call x1, Pallas kernels, mlp_call(): pl.pallas_call(mlp_kernel, grid_spec=pltpu.PrefetchScalarGridSpec(num_sca...  49.6 us
    pallas_call x2, Pallas kernels, attention_back_call(): pl.pallas_call(functools.partial(attention_back_kernel, part), grid_spec=...  39.2 us
    pallas_call x1, Pallas kernels, forward_call(): pl.pallas_call(functools.partial(forward_kernel, len(pieces)), grid_spec=...  25.6 us
    ppermute x3, waiting for transfers between devices, gather_pieces(): lax.ppermute(half, 'fsdp', turn(k))  22.2 us
    ppermute x6, waiting for transfers between devices, scatter_steps(): got = [lax.ppermute(sent[k], 'fsdp', turn(k)) for k in (1, 2, 3)]  19.1 us
    ppermute x1, waiting for transfers between devices, gather_pieces(): by_x = lax.ppermute(along_z, 'rep', REP)  12.4 us
    pallas_call x1, Pallas kernels, norm_one_call(): pl.pallas_call(norm_one_kernel, grid_spec=pltpu.PrefetchScalarGridSpec(nu...  11.6 us
    ppermute x1, waiting for transfers between devices, gather_pieces(): by_xy = lax.ppermute(by_x[:2], 'fsdp', swap(2))  11.5 us
  transfers between devices with their start and end apart: 40, of which 19 were waited for; matrix products, arithmetic and copies ran while one was open for 5% of the time, Pallas kernels for 26%

profile of v1, /device:TPU:8, one launch (start us, length us, event | category | flops | bytes accessed | tf_op | source)
XLA Modules:
  0.0 289.8 jit_solution(2398661870797953862)
XLA Ops:
  7.2 2.5 pack.1
  9.8 0.9 constant_dynamic-slice_fusion.8
  10.8 1.6 collective-permute-start
  12.4 1.1 collective-permute-start.1
  13.5 1.9 collective-permute-start.2
  15.4 0.9 fusion.23
  16.4 9.5 %collective-permute-done = bf16[208,384]{1,0:T(8,128)(2,1)S(1)} collective-permute-done((bf16[208,384]{1,0:T(8,128)(2,1)S(1)}, bf16[208,384]{1,0:T(8,128)(2,1)S(1)}, u32[]{:S(2)}, u32[]{:S(2)}) %collective-permute-start) | collective-permute-done | bytes 159776 | tf_op jit(solution)/shard_map/ppermute | solution.py:546
  25.9 10.6 %collective-permute-done.1 = bf16[208,384]{1,0:T(8,128)(2,1)S(1)} collective-permute-done((bf16[208,384]{1,0:T(8,128)(2,1)S(1)}, bf16[208,384]{1,0:T(8,128)(2,1)S(1)}, u32[]{:S(2)}, u32[]{:S(2)}) %collective-permute-start.1) | collective-permute-done | bytes 159776 | tf_op jit(solution)/shard_map/ppermute | solution.py:546
  36.5 2.0 collective-permute-done.2
  38.7 1.6 collective-permute-start.3
  40.2 1.6 collective-permute-start.4
  41.8 12.4 %collective-permute-done.3.refs_1_ = bf16[4,208,384]{2,1,0:T(8,128)(2,1)S(1)} collective-permute-done((bf16[4,208,384]{2,1,0:T(8,128)(2,1)S(1)}, bf16[4,208,384]{2,1,0:T(8,128)(2,1)S(1)}, u32[]{:S(2)}, u32[]{:S(2)}) %collective-permute-start.3) | collective-permute-done | bytes 639008 | tf_op jit(solution)/shard_map/ppermute | solution.py:547
  54.2 1.7 collective-permute-start.5
  55.9 3.4 %collective-permute-done.4.refs_2_ = bf16[4,208,384]{2,1,0:T(8,128)(2,1)S(1)} collective-permute-done((bf16[4,208,384]{2,1,0:T(8,128)(2,1)S(1)}, bf16[4,208,384]{2,1,0:T(8,128)(2,1)S(1)}, u32[]{:S(2)}, u32[]{:S(2)}) %collective-permute-start.4) | collective-permute-done | bytes 639008 | tf_op jit(solution)/shard_map/ppermute | solution.py:548
  59.5 0.5 collective-permute-start.8
  60.2 11.5 %collective-permute-done.5.refs_3_ = bf16[2,208,384]{2,1,0:T(8,128)(2,1)S(1)} collective-permute-done((bf16[2,208,384]{2,1,0:T(8,128)(2,1)S(1)}, bf16[2,208,384]{2,1,0:T(8,128)(2,1)S(1)}, u32[]{:S(2)}, u32[]{:S(2)}) %collective-permute-start.5) | collective-permute-done | bytes 319520 | tf_op jit(solution)/shard_map/ppermute | solution.py:549
  71.7 0.5 collective-permute-start.11
  72.2 1.1 copy.37.mask_ref
  73.3 1.0 copy.41
  74.3 0.6 pad_add_fusion.place_ref
  75.0 0.8 copy-done.10
  75.8 0.7 copy-done.12
  76.5 25.6 %attention_forward.1 = (bf16[2,512,768]{2,1,0:T(8,128)(2,1)}, bf16[2,512,2304]{2,1,0:T(8,128)(2,1)}, bf16[2,512,768]{2,1,0:T(8,128)(2,1)}, f32[2,12,512]{2,1,0:T...) custom-call(s32[2]{0:T(128)} %group_ref.7, s32[4]{0:T(128)} %pad_add_fusion.place_ref, ...), custom_call_target="tpu_custom_call" | custom-call | flops 8999999488 | bytes 16777216 | tf_op jit(solution)/shard_map/attention_forward/pallas_call | solution.py:190
  102.1 49.6 %mlp.1 = (bf16[1024,768]{1,0:T(8,128)(2,1)}, bf16[1024,768]{1,0:T(8,128)(2,1)}, bf16[16,240,768]{2,1,0:T(8,128)(2,1)}, bf16[8,192,768]{2,1,0:T(8,128)(2,1)}, bf1...) custom-call(s32[2]{0:T(128)} %group_ref.7, s32[4]{0:T(128)} %pad_add_fusion.place_ref, bf16[1024,768]{1,0:T(8,128)(2,1)} %bitcast.118, ...), custom_call_target="tpu_custom_call" | custom-call | flops 44999999488 | bytes 31457280 | tf_op jit(solution)/shard_map/mlp/pallas_call | solution.py:300
  151.9 4.8 %collective-permute-done.12 = bf16[8,192,768]{2,1,0:T(8,128)(2,1)} collective-permute-done((bf16[8,192,768]{2,1,0:T(8,128)(2,1)}, bf16[8,192,768]{2,1,0:T(8,128)(2,1)}, u32[]{:S(2)}, u32[]{:S(2)}) %collective-permute-start.12) | collective-permute-done | bytes 2359328 | tf_op jit(solution)/shard_map/ppermute | solution.py:569
  156.7 2.2 add_convert_fusion
  159.3 2.5 collective-permute-start.14
  161.8 19.2 %attention_backward.2 = (bf16[2,512,1152]{2,1,0:T(8,128)(2,1)}, bf16[8,144,384]{2,1,0:T(8,128)(2,1)}, bf16[8,144,384]{2,1,0:T(8,128)(2,1)}) custom-call(s32[2]{0:T(128)} %group_ref.7, s32[4]{0:T(128)} %pad_add_fusion.place_ref, bf16[2,512,2304]{2,1,0:T(8,128)(2,1)} %get-tuple-element.110.q_ref.k_ref.v_ref, ...), custom_call_target="tpu_custom_call" | custom-call | flops 100000000 | bytes 1048576 | tf_op jit(solution)/shard_map/attention_backward/pallas_call | solution.py:404
  181.3 0.8 dynamic-slice_bitcast_fusion.4
  182.1 20.1 %attention_backward.3 = (bf16[2,512,1152]{2,1,0:T(8,128)(2,1)}, bf16[8,144,384]{2,1,0:T(8,128)(2,1)}, bf16[8,144,384]{2,1,0:T(8,128)(2,1)}) custom-call(s32[2]{0:T(128)} %group_ref.7, s32[4]{0:T(128)} %pad_add_fusion.place_ref, bf16[2,512,2304]{2,1,0:T(8,128)(2,1)} %get-tuple-element.110.q_ref.k_ref.v_ref, ...), custom_call_target="tpu_custom_call" | custom-call | flops 100000000 | bytes 1048576 | tf_op jit(solution)/shard_map/attention_backward/pallas_call | solution.py:404
  202.8 1.2 collective-permute-start.18
  203.9 1.6 collective-permute-done.15
  205.5 1.4 add_convert_fusion.2
  207.6 0.5 collective-permute-start.20
  208.1 3.6 %collective-permute-done.18 = bf16[2,96,768]{2,1,0:T(8,128)(2,1)S(1)} collective-permute-done((bf16[2,96,768]{2,1,0:T(8,128)(2,1)S(1)}, bf16[2,96,768]{2,1,0:T(8,128)(2,1)S(1)}, u32[]{:S(2)}, u32[]{:S(2)}) %collective-permute-start.18) | collective-permute-done | bytes 294944 | tf_op jit(solution)/shard_map/ppermute | solution.py:580
  211.8 2.2 collective-permute-done.17
  214.1 1.0 collective-permute-start.19
  215.3 11.6 %norm_one_backward.1 = (bf16[1024,768]{1,0:T(8,128)(2,1)}, bf16[8,16,384]{2,1,0:T(8,128)(2,1)}, bf16[8,16,384]{2,1,0:T(8,128)(2,1)}) custom-call(s32[4]{0:T(128)} %pad_add_fusion.place_ref, bf16[1024,768]{1,0:T(8,128)(2,1)} %bitcast.119, f32[1024,1]{1,0:T(8,128)} %bitcast.117, bf16[1024,768]{1,0:T(8,128)(2,1)} %get-tuple-element.109.gb_ref, ...), custom_call_target="tpu_custom_call" | custom-call | flops 100000000 | bytes 1048576 | tf_op jit(solution)/shard_map/norm_one_backward/pallas_call | solution.py:483
  227.3 0.6 copy-done.13
  227.9 1.3 collective-permute-done.21
  229.3 1.2 collective-permute-start.27
  230.5 1.9 collective-permute-start.26
  232.5 4.7 %collective-permute-start.24 = (bf16[96,768]{1,0:T(8,128)(2,1)S(1)}, bf16[96,768]{1,0:T(8,128)(2,1)S(1)}, u32[]{:S(2)}, u32[]{:S(2)}) collective-permute-start(bf16[96,768]{1,0:T(8,128)(2,1)S(1)} %get-tuple-element.163), channel_id=1, source_target_pairs={{0,8},{1,9},{2,10},{3,11},{4,12},{5,13},{6,14},{7,15},{8,0},{9,1},... | collective-permute-start | bytes 442376 | tf_op jit(solution)/shard_map/ppermute | solution.py:584
  237.4 2.0 collective-permute-done.23
  239.4 6.5 %collective-permute-done.24 = bf16[96,768]{1,0:T(8,128)(2,1)S(1)} collective-permute-done((bf16[96,768]{1,0:T(8,128)(2,1)S(1)}, bf16[96,768]{1,0:T(8,128)(2,1)S(1)}, u32[]{:S(2)}, u32[]{:S(2)}) %collective-permute-start.24) | collective-permute-done | bytes 147488 | tf_op jit(solution)/shard_map/ppermute | solution.py:584
  245.9 2.8 collective-permute-done.25
  249.3 1.7 collective-permute-start.32
  251.0 0.9 collective-permute-start.33
  251.9 1.2 collective-permute-start.28
  253.1 3.1 %collective-permute-start.29 = (bf16[144,384]{1,0:T(8,128)(2,1)S(1)}, bf16[144,384]{1,0:T(8,128)(2,1)S(1)}, u32[]{:S(2)}, u32[]{:S(2)}) collective-permute-start(bf16[144,384]{1,0:T(8,128)(2,1)S(1)} %get-tuple-element.180), channel_id=1, source_target_pairs={{0,8},{1,9},{2,10},{3,11},{4,12},{5,13},{6,14},{7,15},{8,0},{9,1},... | collective-permute-start | bytes 331784 | tf_op jit(solution)/shard_map/ppermute | solution.py:584
  256.3 4.7 %collective-permute-done.28 = bf16[144,384]{1,0:T(8,128)(2,1)S(1)} collective-permute-done((bf16[144,384]{1,0:T(8,128)(2,1)S(1)}, bf16[144,384]{1,0:T(8,128)(2,1)S(1)}, u32[]{:S(2)}, u32[]{:S(2)}) %collective-permute-start.28) | collective-permute-done | bytes 110624 | tf_op jit(solution)/shard_map/ppermute | solution.py:584
  261.0 1.2 collective-permute-done.29
  262.2 1.8 collective-permute-done.30
  264.1 1.4 collective-permute-start.35
  265.5 0.7 collective-permute-start.37
  266.2 1.3 collective-permute-start.36
  267.6 0.7 collective-permute-start.34
  268.3 0.6 slice.149
  268.8 0.5 slice_bitcast_fusion
  269.4 2.9 %collective-permute-done.37 = bf16[96,768]{1,0:T(8,128)(2,1)S(1)} collective-permute-done((bf16[96,768]{1,0:T(8,128)(2,1)S(1)}, bf16[96,768]{1,0:T(8,128)(2,1)S(1)}, u32[]{:S(2)}, u32[]{:S(2)}) %collective-permute-start.37) | collective-permute-done | bytes 147488 | tf_op jit(solution)/shard_map/ppermute | solution.py:590
  272.3 0.9 fusion.2
  273.2 7.5 %collective-permute-done.34 = bf16[144,384]{1,0:T(8,128)(2,1)S(1)} collective-permute-done((bf16[144,384]{1,0:T(8,128)(2,1)S(1)}, bf16[144,384]{1,0:T(8,128)(2,1)S(1)}, u32[]{:S(2)}, u32[]{:S(2)}) %collective-permute-start.34) | collective-permute-done | bytes 110624 | tf_op jit(solution)/shard_map/ppermute | solution.py:590
  280.9 0.7 fusion.22
  281.7 0.9 pad_maximum_fusion.2
  (107 shorter events, 4.7 us)
Async XLA Ops:
  7.2 94.9 %all-gather.3.cloned.1.call-start = ((), (), s32[]{:S(2)}) async-start(), calls=%async_computation.2 | async-start | bytes 10027008 | tf_op jit(solution)/shard_map/all_gather | solution.py:627
  9.8 50.3 %copy-start.9 = (s32[2,128]{1,0:T(2,128)S(1)}, s32[2,128]{1,0:T(2,128)}, u32[]{:S(2)}) copy-start(s32[2,128]{1,0:T(2,128)} %param.19) | copy-start | bytes 3076
  9.8 239.5 %reduce-scatter.2.cloned.1.call-start = ((), (), s32[]{:S(2)}) async-start(), calls=%async_computation.1 | async-start | bytes 6266880 | tf_op jit(solution)/shard_map/reduce_scatter | solution.py:677
  10.8 15.1 %collective-permute-start = (bf16[208,384]{1,0:T(8,128)(2,1)S(1)}, bf16[208,384]{1,0:T(8,128)(2,1)S(1)}, u32[]{:S(2)}, u32[]{:S(2)}) collective-permute-start(bf16[208,384]{1,0:T(8,128)(2,1)S(1)} %constant_dynamic-slice_fusion.8), channel_id=1, source_target_pairs={{0,4},{1,5},{2,6},{3,7},{4,8},{5,9},{6,10},{7,11},{8,12},{9,13},{1... | collective-permute-start | bytes 479240 | tf_op jit(solution)/shard_map/ppermute | solution.py:546
  12.4 24.1 %collective-permute-start.1 = (bf16[208,384]{1,0:T(8,128)(2,1)S(1)}, bf16[208,384]{1,0:T(8,128)(2,1)S(1)}, u32[]{:S(2)}, u32[]{:S(2)}) collective-permute-start(bf16[208,384]{1,0:T(8,128)(2,1)S(1)} %constant_dynamic-slice_fusion.8), channel_id=1, source_target_pairs={{0,8},{1,9},{2,10},{3,11},{4,12},{5,13},{6,14},{7,15},{8,0},{9,1},... | collective-permute-start | bytes 479240 | tf_op jit(solution)/shard_map/ppermute | solution.py:546
  13.5 25.1 %collective-permute-start.2 = (bf16[208,384]{1,0:T(8,128)(2,1)S(1)}, bf16[208,384]{1,0:T(8,128)(2,1)S(1)}, u32[]{:S(2)}, u32[]{:S(2)}) collective-permute-start(bf16[208,384]{1,0:T(8,128)(2,1)S(1)} %constant_dynamic-slice_fusion.8), channel_id=1, source_target_pairs={{0,12},{1,13},{2,14},{3,15},{4,0},{5,1},{6,2},{7,3},{8,4},{9,5},{1... | collective-permute-start | bytes 479240 | tf_op jit(solution)/shard_map/ppermute | solution.py:546
  38.7 36.3 %copy-start.3 = (bf16[4,208,384]{2,1,0:T(8,128)(2,1)}, bf16[4,208,384]{2,1,0:T(8,128)(2,1)S(1)}, u32[]{:S(2)}) copy-start(bf16[4,208,384]{2,1,0:T(8,128)(2,1)S(1)} %pad_maximum_fusion.1.refs_0_) | copy-start | bytes 1916932
  38.7 15.5 %collective-permute-start.3 = (bf16[4,208,384]{2,1,0:T(8,128)(2,1)S(1)}, bf16[4,208,384]{2,1,0:T(8,128)(2,1)S(1)}, u32[]{:S(2)}, u32[]{:S(2)}) collective-permute-start(bf16[4,208,384]{2,1,0:T(8,128)(2,1)S(1)} %pad_maximum_fusion.1.refs_0_), channel_id=1, source_target_pairs={{0,16},{16,0},{1,17},{17,1},{2,18},{18,2},{3,19},{19,3},{4,20},{20... | collective-permute-start | bytes 1916936 | tf_op jit(solution)/shard_map/ppermute | solution.py:547
  40.2 19.1 %collective-permute-start.4 = (bf16[4,208,384]{2,1,0:T(8,128)(2,1)S(1)}, bf16[4,208,384]{2,1,0:T(8,128)(2,1)S(1)}, u32[]{:S(2)}, u32[]{:S(2)}) collective-permute-start(bf16[4,208,384]{2,1,0:T(8,128)(2,1)S(1)} %pad_maximum_fusion.1.refs_0_), channel_id=1, source_target_pairs={{0,2},{1,3},{2,0},{3,1},{4,6},{5,7},{6,4},{7,5},{8,10},{9,11},{10,... | collective-permute-start | bytes 1916936 | tf_op jit(solution)/shard_map/ppermute | solution.py:548
  54.2 20.8 %copy-start.5 = (bf16[4,208,384]{2,1,0:T(8,128)(2,1)}, bf16[4,208,384]{2,1,0:T(8,128)(2,1)S(1)}, u32[]{:S(2)}) copy-start(bf16[4,208,384]{2,1,0:T(8,128)(2,1)S(1)} %collective-permute-done.3.refs_1_) | copy-start | bytes 1916932
  54.2 17.5 %collective-permute-start.5 = (bf16[2,208,384]{2,1,0:T(8,128)(2,1)S(1)}, bf16[2,208,384]{2,1,0:T(8,128)(2,1)S(1)}, u32[]{:S(2)}, u32[]{:S(2)}) collective-permute-start(bf16[2,208,384]{2,1,0:T(8,128)(2,1)S(1)} %slice.129), channel_id=1, source_target_pairs={{0,2},{1,3},{2,0},{3,1},{4,6},{5,7},{6,4},{7,5},{8,10},{9,11},{10,... | collective-permute-start | bytes 958472 | tf_op jit(solution)/shard_map/ppermute | solution.py:549
  59.3 15.6 %copy-start.6 = (bf16[4,208,384]{2,1,0:T(8,128)(2,1)}, bf16[4,208,384]{2,1,0:T(8,128)(2,1)S(1)}, u32[]{:S(2)}) copy-start(bf16[4,208,384]{2,1,0:T(8,128)(2,1)S(1)} %collective-permute-done.4.refs_2_) | copy-start | bytes 1916932
  59.4 12.4 %collective-permute-start.6 = (bf16[2,208,384]{2,1,0:T(8,128)(2,1)S(1)}, bf16[2,208,384]{2,1,0:T(8,128)(2,1)}, u32[]{:S(2)}, u32[]{:S(2)}) collective-permute-start(bf16[2,208,384]{2,1,0:T(8,128)(2,1)S(1)} %slice.130), channel_id=1, source_target_pairs={{0,16},{16,0},{1,17},{17,1},{2,18},{18,2},{3,19},{19,3},{4,20},{20... | collective-permute-start | bytes 958472 | tf_op jit(solution)/shard_map/ppermute | solution.py:550
  59.4 15.5 %collective-permute-start.7 = (bf16[4,208,384]{2,1,0:T(8,128)(2,1)S(1)}, bf16[4,208,384]{2,1,0:T(8,128)(2,1)S(1)}, u32[]{:S(2)}, u32[]{:S(2)}) collective-permute-start(bf16[4,208,384]{2,1,0:T(8,128)(2,1)S(1)} %pad_maximum_fusion.1.refs_0_), channel_id=1, source_target_pairs={{0,1},{1,0},{2,3},{3,2},{4,5},{5,4},{6,7},{7,6},{8,9},{9,8},{10,11... | collective-permute-start | bytes 1916936 | tf_op jit(solution)/shard_map/ppermute | solution.py:552
  59.5 15.4 %collective-permute-start.8 = (bf16[4,208,384]{2,1,0:T(8,128)(2,1)S(1)}, bf16[4,208,384]{2,1,0:T(8,128)(2,1)}, u32[]{:S(2)}, u32[]{:S(2)}) collective-permute-start(bf16[4,208,384]{2,1,0:T(8,128)(2,1)S(1)} %collective-permute-done.3.refs_1_), channel_id=1, source_target_pairs={{0,1},{1,0},{2,3},{3,2},{4,5},{5,4},{6,7},{7,6},{8,9},{9,8},{10,11... | collective-permute-start | bytes 1916936 | tf_op jit(solution)/shard_map/ppermute | solution.py:552
  60.0 14.9 %collective-permute-start.9 = (bf16[4,208,384]{2,1,0:T(8,128)(2,1)S(1)}, bf16[4,208,384]{2,1,0:T(8,128)(2,1)}, u32[]{:S(2)}, u32[]{:S(2)}) collective-permute-start(bf16[4,208,384]{2,1,0:T(8,128)(2,1)S(1)} %collective-permute-done.4.refs_2_), channel_id=1, source_target_pairs={{0,1},{1,0},{2,3},{3,2},{4,5},{5,4},{6,7},{7,6},{8,9},{9,8},{10,11... | collective-permute-start | bytes 1916936 | tf_op jit(solution)/shard_map/ppermute | solution.py:552
  71.7 3.3 %copy-start.11 = (bf16[2,208,384]{2,1,0:T(8,128)(2,1)}, bf16[2,208,384]{2,1,0:T(8,128)(2,1)S(1)}, u32[]{:S(2)}) copy-start(bf16[2,208,384]{2,1,0:T(8,128)(2,1)S(1)} %collective-permute-done.5.refs_3_) | copy-start | bytes 958468
  71.7 3.2 %collective-permute-start.10 = (bf16[2,208,384]{2,1,0:T(8,128)(2,1)S(1)}, bf16[2,208,384]{2,1,0:T(8,128)(2,1)}, u32[]{:S(2)}, u32[]{:S(2)}) collective-permute-start(bf16[2,208,384]{2,1,0:T(8,128)(2,1)S(1)} %collective-permute-done.5.refs_3_), channel_id=1, source_target_pairs={{0,1},{1,0},{2,3},{3,2},{4,5},{5,4},{6,7},{7,6},{8,9},{9,8},{10,11... | collective-permute-start | bytes 958472 | tf_op jit(solution)/shard_map/ppermute | solution.py:552
  71.7 3.2 %collective-permute-start.11 = (bf16[2,208,384]{2,1,0:T(8,128)(2,1)}, bf16[2,208,384]{2,1,0:T(8,128)(2,1)S(1)}, u32[]{:S(2)}, u32[]{:S(2)}) collective-permute-start(bf16[2,208,384]{2,1,0:T(8,128)(2,1)} %collective-permute-done.6.refs_4_), channel_id=1, source_target_pairs={{0,1},{1,0},{2,3},{3,2},{4,5},{5,4},{6,7},{7,6},{8,9},{9,8},{10,11... | collective-permute-start | bytes 958472 | tf_op jit(solution)/shard_map/ppermute | solution.py:552
  74.9 0.8 copy-start.10
  75.8 0.7 copy-start.12
  151.7 4.9 %collective-permute-start.12 = (bf16[8,192,768]{2,1,0:T(8,128)(2,1)}, bf16[8,192,768]{2,1,0:T(8,128)(2,1)}, u32[]{:S(2)}, u32[]{:S(2)}) collective-permute-start(bf16[8,192,768]{2,1,0:T(8,128)(2,1)} %get-tuple-element.113), channel_id=1, source_target_pairs={{0,1},{1,0},{2,3},{3,2},{4,5},{5,4},{6,7},{7,6},{8,9},{9,8},{10,11... | collective-permute-start | bytes 7077896 | tf_op jit(solution)/shard_map/ppermute | solution.py:569
  151.8 4.9 %copy-start = (bf16[8,192,768]{2,1,0:T(8,128)(2,1)S(1)}, bf16[8,192,768]{2,1,0:T(8,128)(2,1)}, u32[]{:S(2)}) copy-start(bf16[8,192,768]{2,1,0:T(8,128)(2,1)} %get-tuple-element.112) | copy-start | bytes 7077892
  159.3 21.7 %collective-permute-start.14 = (bf16[2,192,768]{2,1,0:T(8,128)(2,1)S(1)}, bf16[2,192,768]{2,1,0:T(8,128)(2,1)S(1)}, u32[]{:S(2)}, u32[]{:S(2)}) collective-permute-start(bf16[2,192,768]{2,1,0:T(8,128)(2,1)S(1)} %get-tuple-element.124), channel_id=1, source_target_pairs={{0,2},{1,3},{2,0},{3,1},{4,6},{5,7},{6,4},{7,5},{8,10},{9,11},{10,... | collective-permute-start | bytes 1769480 | tf_op jit(solution)/shard_map/ppermute | solution.py:576
  161.8 19.4 %collective-permute-start.13 = (bf16[2,2,96,768]{3,2,1,0:T(8,128)(2,1)S(1)}, bf16[2,2,96,768]{3,2,1,0:T(8,128)(2,1)S(1)}, u32[]{:S(2)}, u32[]{:S(2)}) collective-permute-start(bf16[2,2,96,768]{3,2,1,0:T(8,128)(2,1)S(1)} %get-tuple-element.122), channel_id=1, source_target_pairs={{0,16},{16,0},{1,17},{17,1},{2,18},{18,2},{3,19},{19,3},{4,20},{20... | collective-permute-start | bytes 1769480 | tf_op jit(solution)/shard_map/ppermute | solution.py:576
  182.1 23.4 %copy-start.1 = (bf16[8,144,384]{2,1,0:T(8,128)(2,1)S(1)}, bf16[8,144,384]{2,1,0:T(8,128)(2,1)}, u32[]{:S(2)}) copy-start(bf16[8,144,384]{2,1,0:T(8,128)(2,1)} %get-tuple-element.135) | copy-start | bytes 2654212
  202.2 4.7 %copy-start.2 = (bf16[8,144,384]{2,1,0:T(8,128)(2,1)S(1)}, bf16[8,144,384]{2,1,0:T(8,128)(2,1)}, u32[]{:S(2)}) copy-start(bf16[8,144,384]{2,1,0:T(8,128)(2,1)} %get-tuple-element.137) | copy-start | bytes 2654212
  202.2 3.3 %collective-permute-start.15 = (bf16[8,144,384]{2,1,0:T(8,128)(2,1)}, bf16[8,144,384]{2,1,0:T(8,128)(2,1)}, u32[]{:S(2)}, u32[]{:S(2)}) collective-permute-start(bf16[8,144,384]{2,1,0:T(8,128)(2,1)} %get-tuple-element.136), channel_id=1, source_target_pairs={{0,1},{1,0},{2,3},{3,2},{4,5},{5,4},{6,7},{7,6},{8,9},{9,8},{10,11... | collective-permute-start | bytes 2654216 | tf_op jit(solution)/shard_map/ppermute | solution.py:569
  202.3 4.6 %collective-permute-start.16 = (bf16[8,144,384]{2,1,0:T(8,128)(2,1)}, bf16[8,144,384]{2,1,0:T(8,128)(2,1)S(1)}, u32[]{:S(2)}, u32[]{:S(2)}) collective-permute-start(bf16[8,144,384]{2,1,0:T(8,128)(2,1)} %get-tuple-element.138), channel_id=1, source_target_pairs={{0,1},{1,0},{2,3},{3,2},{4,5},{5,4},{6,7},{7,6},{8,9},{9,8},{10,11... | collective-permute-start | bytes 2654216 | tf_op jit(solution)/shard_map/ppermute | solution.py:569
  202.8 9.0 %collective-permute-start.18 = (bf16[2,96,768]{2,1,0:T(8,128)(2,1)S(1)}, bf16[2,96,768]{2,1,0:T(8,128)(2,1)S(1)}, u32[]{:S(2)}, u32[]{:S(2)}) collective-permute-start(bf16[2,96,768]{2,1,0:T(8,128)(2,1)S(1)} %get-tuple-element.145), channel_id=1, source_target_pairs={{0,16},{16,0},{1,17},{17,1},{2,18},{18,2},{3,19},{19,3},{4,20},{20... | collective-permute-start | bytes 884744 | tf_op jit(solution)/shard_map/ppermute | solution.py:580
  203.9 10.1 %collective-permute-start.17 = (bf16[2,96,768]{2,1,0:T(8,128)(2,1)}, bf16[2,96,768]{2,1,0:T(8,128)(2,1)S(1)}, u32[]{:S(2)}, u32[]{:S(2)}) collective-permute-start(bf16[2,96,768]{2,1,0:T(8,128)(2,1)} %get-tuple-element.143), channel_id=1, source_target_pairs={{0,2},{1,3},{2,0},{3,1},{4,6},{5,7},{6,4},{7,5},{8,10},{9,11},{10,... | collective-permute-start | bytes 884744 | tf_op jit(solution)/shard_map/ppermute | solution.py:580
  207.6 19.3 %collective-permute-start.20 = (bf16[2,288,384]{2,1,0:T(8,128)(2,1)S(1)}, bf16[2,288,384]{2,1,0:T(8,128)(2,1)S(1)}, u32[]{:S(2)}, u32[]{:S(2)}) collective-permute-start(bf16[2,288,384]{2,1,0:T(8,128)(2,1)S(1)} %get-tuple-element.153), channel_id=1, source_target_pairs={{0,2},{1,3},{2,0},{3,1},{4,6},{5,7},{6,4},{7,5},{8,10},{9,11},{10,... | collective-permute-start | bytes 1327112 | tf_op jit(solution)/shard_map/ppermute | solution.py:576
  214.1 13.0 %collective-permute-start.19 = (bf16[2,2,144,384]{3,2,1,0:T(8,128)(2,1)S(1)}, bf16[2,2,144,384]{3,2,1,0:T(8,128)(2,1)S(1)}, u32[]{:S(2)}, u32[]{:S(2)}) collective-permute-start(bf16[2,2,144,384]{3,2,1,0:T(8,128)(2,1)S(1)} %get-tuple-element.151), channel_id=1, source_target_pairs={{0,16},{16,0},{1,17},{17,1},{2,18},{18,2},{3,19},{19,3},{4,20},{20... | collective-permute-start | bytes 1327112 | tf_op jit(solution)/shard_map/ppermute | solution.py:576
  227.0 0.9 copy-start.13
  227.0 2.2 copy-start.7
  227.9 1.3 collective-permute-start.21
  229.2 7.9 %collective-permute-start.22 = (bf16[4,16,384]{2,1,0:T(8,128)(2,1)S(1)}, bf16[4,16,384]{2,1,0:T(8,128)(2,1)S(1)}, u32[]{:S(2)}, u32[]{:S(2)}) collective-permute-start(bf16[4,16,384]{2,1,0:T(8,128)(2,1)S(1)} %dynamic-slice_bitcast_fusion.8), channel_id=1, source_target_pairs={{0,2},{1,3},{2,0},{3,1},{4,6},{5,7},{6,4},{7,5},{8,10},{9,11},{10,... | collective-permute-start | bytes 147464 | tf_op jit(solution)/shard_map/ppermute | solution.py:675
  229.3 19.5 %collective-permute-start.27 = (bf16[2,144,384]{2,1,0:T(8,128)(2,1)S(1)}, bf16[2,144,384]{2,1,0:T(8,128)(2,1)S(1)}, u32[]{:S(2)}, u32[]{:S(2)}) collective-permute-start(bf16[2,144,384]{2,1,0:T(8,128)(2,1)S(1)} %get-tuple-element.168), channel_id=1, source_target_pairs={{0,16},{16,0},{1,17},{17,1},{2,18},{18,2},{3,19},{19,3},{4,20},{20... | collective-permute-start | bytes 663560 | tf_op jit(solution)/shard_map/ppermute | solution.py:580
  230.5 18.4 %collective-permute-start.26 = (bf16[2,144,384]{2,1,0:T(8,128)(2,1)S(1)}, bf16[2,144,384]{2,1,0:T(8,128)(2,1)S(1)}, u32[]{:S(2)}, u32[]{:S(2)}) collective-permute-start(bf16[2,144,384]{2,1,0:T(8,128)(2,1)S(1)} %get-tuple-element.166), channel_id=1, source_target_pairs={{0,2},{1,3},{2,0},{3,1},{4,6},{5,7},{6,4},{7,5},{8,10},{9,11},{10,... | collective-permute-start | bytes 663560 | tf_op jit(solution)/shard_map/ppermute | solution.py:580
  232.5 6.9 %collective-permute-start.23 = (bf16[96,768]{1,0:T(8,128)(2,1)S(1)}, bf16[96,768]{1,0:T(8,128)(2,1)S(1)}, u32[]{:S(2)}, u32[]{:S(2)}) collective-permute-start(bf16[96,768]{1,0:T(8,128)(2,1)S(1)} %get-tuple-element.162), channel_id=1, source_target_pairs={{0,4},{1,5},{2,6},{3,7},{4,8},{5,9},{6,10},{7,11},{8,12},{9,13},{1... | collective-permute-start | bytes 442376 | tf_op jit(solution)/shard_map/ppermute | solution.py:584
  232.5 13.4 %collective-permute-start.24 = (bf16[96,768]{1,0:T(8,128)(2,1)S(1)}, bf16[96,768]{1,0:T(8,128)(2,1)S(1)}, u32[]{:S(2)}, u32[]{:S(2)}) collective-permute-start(bf16[96,768]{1,0:T(8,128)(2,1)S(1)} %get-tuple-element.163), channel_id=1, source_target_pairs={{0,8},{1,9},{2,10},{3,11},{4,12},{5,13},{6,14},{7,15},{8,0},{9,1},... | collective-permute-start | bytes 442376 | tf_op jit(solution)/shard_map/ppermute | solution.py:584
  237.1 11.6 %collective-permute-start.25 = (bf16[96,768]{1,0:T(8,128)(2,1)S(1)}, bf16[96,768]{1,0:T(8,128)(2,1)S(1)}, u32[]{:S(2)}, u32[]{:S(2)}) collective-permute-start(bf16[96,768]{1,0:T(8,128)(2,1)S(1)} %get-tuple-element.164), channel_id=1, source_target_pairs={{0,12},{1,13},{2,14},{3,15},{4,0},{5,1},{6,2},{7,3},{8,4},{9,5},{1... | collective-permute-start | bytes 442376 | tf_op jit(solution)/shard_map/ppermute | solution.py:584
  249.2 31.6 %copy-start.4 = (bf16[1,240,768]{2,1,0:T(8,128)(2,1)S(1)}, bf16[1,240,768]{2,1,0:T(8,128)(2,1)}, u32[]{:S(2)}) copy-start(bf16[1,240,768]{2,1,0:T(8,128)(2,1)} %reduce-scatter.2.cloned.1.call-done) | copy-start | bytes 1105924
  249.3 6.9 %collective-permute-start.31 = (bf16[16,384]{1,0:T(8,128)(2,1)S(1)}, bf16[16,384]{1,0:T(8,128)(2,1)S(1)}, u32[]{:S(2)}, u32[]{:S(2)}) collective-permute-start(bf16[16,384]{1,0:T(8,128)(2,1)S(1)} %get-tuple-element.183), channel_id=1, source_target_pairs={{0,4},{1,5},{2,6},{3,7},{4,8},{5,9},{6,10},{7,11},{8,12},{9,13},{1... | collective-permute-start | bytes 36872 | tf_op jit(solution)/shard_map/ppermute | solution.py:680
  249.3 7.0 %collective-permute-start.32 = (bf16[16,384]{1,0:T(8,128)(2,1)S(1)}, bf16[16,384]{1,0:T(8,128)(2,1)S(1)}, u32[]{:S(2)}, u32[]{:S(2)}) collective-permute-start(bf16[16,384]{1,0:T(8,128)(2,1)S(1)} %get-tuple-element.184), channel_id=1, source_target_pairs={{0,8},{1,9},{2,10},{3,11},{4,12},{5,13},{6,14},{7,15},{8,0},{9,1},... | collective-permute-start | bytes 36872 | tf_op jit(solution)/shard_map/ppermute | solution.py:680
  251.0 5.3 %collective-permute-start.33 = (bf16[16,384]{1,0:T(8,128)(2,1)S(1)}, bf16[16,384]{1,0:T(8,128)(2,1)S(1)}, u32[]{:S(2)}, u32[]{:S(2)}) collective-permute-start(bf16[16,384]{1,0:T(8,128)(2,1)S(1)} %get-tuple-element.185), channel_id=1, source_target_pairs={{0,12},{1,13},{2,14},{3,15},{4,0},{5,1},{6,2},{7,3},{8,4},{9,5},{1... | collective-permute-start | bytes 36872 | tf_op jit(solution)/shard_map/ppermute | solution.py:680
  251.9 9.1 %collective-permute-start.28 = (bf16[144,384]{1,0:T(8,128)(2,1)S(1)}, bf16[144,384]{1,0:T(8,128)(2,1)S(1)}, u32[]{:S(2)}, u32[]{:S(2)}) collective-permute-start(bf16[144,384]{1,0:T(8,128)(2,1)S(1)} %get-tuple-element.179), channel_id=1, source_target_pairs={{0,4},{1,5},{2,6},{3,7},{4,8},{5,9},{6,10},{7,11},{8,12},{9,13},{1... | collective-permute-start | bytes 331784 | tf_op jit(solution)/shard_map/ppermute | solution.py:584
  253.1 9.1 %collective-permute-start.29 = (bf16[144,384]{1,0:T(8,128)(2,1)S(1)}, bf16[144,384]{1,0:T(8,128)(2,1)S(1)}, u32[]{:S(2)}, u32[]{:S(2)}) collective-permute-start(bf16[144,384]{1,0:T(8,128)(2,1)S(1)} %get-tuple-element.180), channel_id=1, source_target_pairs={{0,8},{1,9},{2,10},{3,11},{4,12},{5,13},{6,14},{7,15},{8,0},{9,1},... | collective-permute-start | bytes 331784 | tf_op jit(solution)/shard_map/ppermute | solution.py:584
  256.1 7.9 %collective-permute-start.30 = (bf16[144,384]{1,0:T(8,128)(2,1)S(1)}, bf16[144,384]{1,0:T(8,128)(2,1)S(1)}, u32[]{:S(2)}, u32[]{:S(2)}) collective-permute-start(bf16[144,384]{1,0:T(8,128)(2,1)S(1)} %get-tuple-element.181), channel_id=1, source_target_pairs={{0,12},{1,13},{2,14},{3,15},{4,0},{5,1},{6,2},{7,3},{8,4},{9,5},{1... | collective-permute-start | bytes 331784 | tf_op jit(solution)/shard_map/ppermute | solution.py:584
  264.1 4.1 %collective-permute-start.35 = (bf16[16,384]{1,0:T(8,128)(2,1)S(1)}, bf16[16,384]{1,0:T(8,128)(2,1)S(1)}, u32[]{:S(2)}, u32[]{:S(2)}) collective-permute-start(bf16[16,384]{1,0:T(8,128)(2,1)S(1)} %add_convert_fusion.14), channel_id=1, source_target_pairs={{0,16},{16,0},{1,17},{17,1},{2,18},{18,2},{3,19},{19,3},{4,20},{20... | collective-permute-start | bytes 36872 | tf_op jit(solution)/shard_map/ppermute | solution.py:687
  265.5 6.8 %collective-permute-start.37 = (bf16[96,768]{1,0:T(8,128)(2,1)S(1)}, bf16[96,768]{1,0:T(8,128)(2,1)S(1)}, u32[]{:S(2)}, u32[]{:S(2)}) collective-permute-start(bf16[96,768]{1,0:T(8,128)(2,1)S(1)} %add_convert_fusion.11), channel_id=1, source_target_pairs={{0,16},{16,0},{1,17},{17,1},{2,18},{18,2},{3,19},{19,3},{4,20},{20... | collective-permute-start | bytes 442376 | tf_op jit(solution)/shard_map/ppermute | solution.py:590
  266.2 14.6 %collective-permute-start.36 = (bf16[240,768]{1,0:T(8,128)(2,1)}, bf16[240,768]{1,0:T(8,128)(2,1)S(1)}, u32[]{:S(2)}, u32[]{:S(2)}) collective-permute-start(bf16[240,768]{1,0:T(8,128)(2,1)} %bitcast.122), channel_id=1, source_target_pairs={{0,16},{16,0},{1,17},{17,1},{2,18},{18,2},{3,19},{19,3},{4,20},{20... | collective-permute-start | bytes 1105928 | tf_op jit(solution)/shard_map/ppermute | solution.py:679
  267.6 13.1 %collective-permute-start.34 = (bf16[144,384]{1,0:T(8,128)(2,1)S(1)}, bf16[144,384]{1,0:T(8,128)(2,1)S(1)}, u32[]{:S(2)}, u32[]{:S(2)}) collective-permute-start(bf16[144,384]{1,0:T(8,128)(2,1)S(1)} %add_convert_fusion.12), channel_id=1, source_target_pairs={{0,16},{16,0},{1,17},{17,1},{2,18},{18,2},{3,19},{19,3},{4,20},{20... | collective-permute-start | bytes 331784 | tf_op jit(solution)/shard_map/ppermute | solution.py:590
  280.8 1.7 copy-start.8
Sparse Core Ops, SparseCore 0:
  10.9 89.9 all-gather.2
  152.0 84.4 reduce-scatter.1

commit v2 on v1

--- a/solution.py
+++ b/solution.py
@@ -362,7 +362,7 @@
             gj[0, length:, :] = jnp.zeros((seq - length, 3 * wide), BF)
         lane = lax.broadcasted_iota(jnp.int32, (length, 2 * head), 1)
 
-        @pl.loop(0, HEADS // 2 // GROUPS)
+        @pl.loop(0, HEADS // 2 // GROUPS, unroll=3)
         def _(pair):
             lanes = lambda i: pl.ds(pl.multiple_of(i * wide + pair * 2 * head, 128), 2 * head)
             k = k_ref[0, 0:length, lanes(0)]
@@ -423,7 +423,7 @@
             jax.ShapeDtypeStruct((BLOCKS // 2, 144, wide), BF),
             jax.ShapeDtypeStruct((BLOCKS // 2, 144, wide), BF),
         ],
-        compiler_params=pltpu.CompilerParams(vmem_limit_bytes=VMEM_LIMIT),
+        compiler_params=pltpu.CompilerParams(vmem_limit_bytes=32 * 2**20),
         cost_estimate=pl.CostEstimate(flops=10**8, bytes_accessed=2**20, transcendentals=0),
         name="attention_backward",
     )(group_id, place, qkv, qkv, qkv, lse, gb, w1, normed)
@@ -505,7 +505,7 @@
             jax.ShapeDtypeStruct(small, BF),
             jax.ShapeDtypeStruct(small, BF),
         ],
-        compiler_params=pltpu.CompilerParams(vmem_limit_bytes=VMEM_LIMIT),
+        compiler_params=pltpu.CompilerParams(vmem_limit_bytes=28 * 2**20),
         cost_estimate=pl.CostEstimate(flops=10**8, bytes_accessed=2**20, transcendentals=0),
         name="norm_one_backward",
     )(place, tokens, mask, gb, gj0, gj1, vecs, w1, w1, w1, gvec)
@@ -565,7 +565,7 @@
     return lax.dynamic_slice_in_dim(a, i * rows, rows, a.ndim - 2)
 
 
-def scatter_steps(keep, send, z, y, r):
+def scatter_steps(keep, send, z, y, r, extra=()):
     got = [lax.ppermute(a, "fsdp", swap(1)) for a in send]
     kept = yield tuple(keep)
     summed = jnp.concatenate([add(*pair) for pair in zip(kept, got)], 1)
@@ -580,6 +580,8 @@
     got = lax.ppermute(sent[0], "fsdp", swap(2)), lax.ppermute(sent[1], "rep", REP)
     kept = yield sent[2:]
     both = jnp.concatenate([add(kept[0], got[0]), add(kept[1], got[1])])
+    half = both.shape[1]
+    both = jnp.concatenate([both, *extra], 1)
     sent = yield tuple(pick(both, (z + k) % 4, 0) for k in range(4))
     got = [lax.ppermute(sent[k], "fsdp", turn(k)) for k in (1, 2, 3)]
     kept = yield sent[:1]
@@ -589,7 +591,9 @@
     mine = yield (total.astype(BF),)
     other = lax.ppermute(mine[0], "rep", REP)
     mine = (yield mine)[0]
-    yield jnp.where(r == 0, jnp.concatenate([mine, other]), jnp.concatenate([other, mine])).astype(F32)
+    few = mine[half:].astype(F32) + other[half:].astype(F32)
+    mine, other = mine[:half], other[:half]
+    yield jnp.where(r == 0, jnp.concatenate([mine, other]), jnp.concatenate([other, mine])).astype(F32), few
 
 
 class Scatter:
@@ -665,7 +669,8 @@
         (gb3,) = step([down], gb3)
         gj1, keep1, send1 = back(1, gb3)
         keep0, keep1, send0, send1 = step([down], keep0, keep1, send0, send1)
-        rest = Scatter([keep0, keep1], [send0, send1], z, y, r)
+        extra = []
+        rest = Scatter([keep0, keep1], [send0, send1], z, y, r, extra)
         step([rest])
         (gvec,) = step([rest], gvec)
         token_grad, keep2, send2 = after(gj0, gj1, gvec)
@@ -673,20 +678,16 @@
         keep2, send2 = step([down, rest], keep2, send2)
         few = add(keep2, lax.ppermute(send2, "fsdp", swap(1))).reshape(4, 2, *keep2.shape[1:])
         few = add(pick(few, y, 1), lax.ppermute(pick(few, 1 - y, 1), "fsdp", swap(2)))
-        few = step([down, rest], *(pick(few, (z + k) % 4, 0) for k in range(4)))
+        extra.append(few)
+        step([down, rest])
         own2 = lax.psum_scatter(g2, "fsdp", scatter_dimension=0)
-        *few, own2 = step([down, rest], *few, own2)
+        (own2,) = step([down, rest], own2)
         other2 = lax.ppermute(own2, "rep", REP)
-        got = [lax.ppermute(few[k], "fsdp", turn(k)) for k in (1, 2, 3)]
-        few, own2 = step([down, rest], few[0], own2)
-        total = few.astype(F32)
-        for term in got:
-            total += term.astype(F32)
-        (few,) = step([rest], total.astype(BF))
+        (own2,) = step([down, rest], own2)
+        step([rest])
         sum2 = own2.astype(F32) + other2.astype(F32)
-        few = few.astype(F32) + lax.ppermute(few, "rep", REP).astype(F32)
-        sum1 = rest.steps.send(rest.value)
-        down_grad = down.value
+        sum1, few = rest.steps.send(rest.value)
+        down_grad, _ = down.value
         up_grad, out_grad = sum2[: 4 * width], sum2[4 * width :]
         qkv_grad = jnp.concatenate([sum1[i * width : (i + 1) * width] for i in (0, 3, 1, 4, 2, 5)], 1)
         vg = [few[k, :width] for k in range(B_UP)] + [few[B_UP, : 4 * width]]

time: 295 us -> 286 us (0.969)
  the two profiles are of different devices: /device:TPU:8 before, /device:TPU:0 now
where the time goes in v2:
time: 286 us; the launch traced here: 281 us
  Pallas kernels  118 us (41%)
  waiting for transfers between devices  87.1 us (30%)
  starting transfers between devices  38 us (13%)
  between operations  15 us (5%)
  local copies, waits for them, and re-layouts  13.2 us (5%)
  other arithmetic  9.73 us (3%)
    pallas_call x1, Pallas kernels, mlp_call(): pl.pallas_call(mlp_kernel, grid_spec=pltpu.PrefetchScalarGridSpec(num_sca...  50 us
    pallas_call x2, Pallas kernels, attention_back_call(): pl.pallas_call(functools.partial(attention_back_kernel, part), grid_spec=...  30.4 us
    pallas_call x1, Pallas kernels, forward_call(): pl.pallas_call(functools.partial(forward_kernel, len(pieces)), grid_spec=...  25.7 us
    all_gather x1, waiting for transfers between devices, local(): w2 = lax.all_gather(pack2, 'fsdp', axis=0)  22.2 us
    ppermute x6, waiting for transfers between devices, scatter_steps(): got = [lax.ppermute(sent[k], 'fsdp', turn(k)) for k in (1, 2, 3)]  20.9 us
    ppermute x1, waiting for transfers between devices, gather_pieces(): by_x = lax.ppermute(along_z, 'rep', REP)  12.2 us
    ppermute x3, waiting for transfers between devices, gather_pieces(): lax.ppermute(half, 'fsdp', turn(k))  10.9 us
    pallas_call x1, Pallas kernels, norm_one_call(): pl.pallas_call(norm_one_kernel, grid_spec=pltpu.PrefetchScalarGridSpec(nu...  8.99 us
  transfers between devices with their start and end apart: 36, of which 15 were waited for; matrix products, arithmetic and copies ran while one was open for 6% of the time, Pallas kernels for 23%

profile of v2, /device:TPU:0, one launch (start us, length us, event | category | flops | bytes accessed | tf_op | source)
XLA Modules:
  0.0 280.6 jit_solution(3771395541311248977)
XLA Ops:
  7.2 2.5 pack.1
  9.8 0.9 constant_dynamic-slice_fusion.8
  10.8 3.1 %collective-permute-start = (bf16[208,384]{1,0:T(8,128)(2,1)S(1)}, bf16[208,384]{1,0:T(8,128)(2,1)S(1)}, u32[]{:S(2)}, u32[]{:S(2)}) collective-permute-start(bf16[208,384]{1,0:T(8,128)(2,1)S(1)} %constant_dynamic-slice_fusion.8), channel_id=1, source_target_pairs={{0,4},{1,5},{2,6},{3,7},{4,8},{5,9},{6,10},{7,11},{8,12},{9,13},{1... | collective-permute-start | bytes 479240 | tf_op jit(solution)/shard_map/ppermute | solution.py:546
  13.8 2.6 collective-permute-start.1
  16.4 1.3 collective-permute-start.2
  17.8 0.9 fusion.15
  18.7 2.2 collective-permute-done
  20.9 8.7 %collective-permute-done.1 = bf16[208,384]{1,0:T(8,128)(2,1)S(1)} collective-permute-done((bf16[208,384]{1,0:T(8,128)(2,1)S(1)}, bf16[208,384]{1,0:T(8,128)(2,1)S(1)}, u32[]{:S(2)}, u32[]{:S(2)}) %collective-permute-start.1) | collective-permute-done | bytes 159776 | tf_op jit(solution)/shard_map/ppermute | solution.py:546
  29.7 1.6 collective-permute-start.3
  31.3 1.6 collective-permute-start.4
  32.8 12.2 %collective-permute-done.3.refs_1_ = bf16[4,208,384]{2,1,0:T(8,128)(2,1)S(1)} collective-permute-done((bf16[4,208,384]{2,1,0:T(8,128)(2,1)S(1)}, bf16[4,208,384]{2,1,0:T(8,128)(2,1)S(1)}, u32[]{:S(2)}, u32[]{:S(2)}) %collective-permute-start.3) | collective-permute-done | bytes 639008 | tf_op jit(solution)/shard_map/ppermute | solution.py:547
  45.1 1.6 collective-permute-start.5
  46.7 1.6 collective-permute-start.6
  49.0 4.1 %collective-permute-done.5.refs_3_ = bf16[2,208,384]{2,1,0:T(8,128)(2,1)S(1)} collective-permute-done((bf16[2,208,384]{2,1,0:T(8,128)(2,1)S(1)}, bf16[2,208,384]{2,1,0:T(8,128)(2,1)S(1)}, u32[]{:S(2)}, u32[]{:S(2)}) %collective-permute-start.5) | collective-permute-done | bytes 319520 | tf_op jit(solution)/shard_map/ppermute | solution.py:549
  53.1 1.1 collective-permute-done.6.refs_4_
  54.3 1.1 copy.37.mask_ref
  55.3 1.0 copy.41
  56.4 0.6 pad_add_fusion.place_ref
  57.0 0.8 copy-done.22
  57.8 0.7 copy-done.24
  58.5 25.7 %attention_forward.1 = (bf16[2,512,768]{2,1,0:T(8,128)(2,1)}, bf16[2,512,2304]{2,1,0:T(8,128)(2,1)}, bf16[2,512,768]{2,1,0:T(8,128)(2,1)}, f32[2,12,512]{2,1,0:T...) custom-call(s32[2]{0:T(128)} %group_ref.7, s32[4]{0:T(128)} %pad_add_fusion.place_ref, ...), custom_call_target="tpu_custom_call" | custom-call | flops 8999999488 | bytes 16777216 | tf_op jit(solution)/shard_map/attention_forward/pallas_call | solution.py:190
  84.2 22.2 %all-gather.3.cloned.1.call-done = bf16[6144,768]{1,0:T(8,128)(2,1)} async-done(((bf16[384,768]{1,0:T(8,128)(2,1)}), bf16[6144,768]{1,0:T(8,128)(2,1)}) %all-gather.3.cloned.1.call-update) | async-done | bytes 9437200 | tf_op jit(solution)/shard_map/all_gather | solution.py:631
  106.4 50.0 %mlp.1 = (bf16[1024,768]{1,0:T(8,128)(2,1)}, bf16[1024,768]{1,0:T(8,128)(2,1)}, bf16[16,240,768]{2,1,0:T(8,128)(2,1)}, bf16[8,192,768]{2,1,0:T(8,128)(2,1)}, bf1...) custom-call(s32[2]{0:T(128)} %group_ref.7, s32[4]{0:T(128)} %pad_add_fusion.place_ref, bf16[1024,768]{1,0:T(8,128)(2,1)} %bitcast.112, ...), custom_call_target="tpu_custom_call" | custom-call | flops 44999999488 | bytes 31457280 | tf_op jit(solution)/shard_map/mlp/pallas_call | solution.py:300
  156.8 4.6 %collective-permute-done.12 = bf16[8,192,768]{2,1,0:T(8,128)(2,1)} collective-permute-done((bf16[8,192,768]{2,1,0:T(8,128)(2,1)}, bf16[8,192,768]{2,1,0:T(8,128)(2,1)}, u32[]{:S(2)}, u32[]{:S(2)}) %collective-permute-start.12) | collective-permute-done | bytes 2359328 | tf_op jit(solution)/shard_map/ppermute | solution.py:569
  161.3 2.5 add_convert_fusion
  164.3 1.3 collective-permute-start.14
  165.6 1.1 collective-permute-start.13
  166.9 0.6 copy-done.1
  167.4 0.6 copy-done
  168.0 15.1 %attention_backward.2 = (bf16[2,512,1152]{2,1,0:T(8,128)(2,1)S(1)}, bf16[8,144,384]{2,1,0:T(8,128)(2,1)S(1)}, bf16[8,144,384]{2,1,0:T(8,128)(2,1)}) custom-call(s32[2]{0:T(128)S(1)} %copy-done.12, s32[4]{0:T(128)S(1)} %copy-done.11, bf16[2,512,2304]{2,1,0:T(8,128)(2,1)S(1)} %bitcast.99, bf16[2,512,2304]{2,1,0:T(8,128)(2,1)S(1)} %bitcast.99, ...), custom_call_target="tpu_custom_call" | custom-call | flops 100000000 | bytes 1048576 | tf_op jit(solution)/shard_map/attention_backward/pallas_call | solution.py:404
  183.3 1.2 constant_dynamic-slice_fusion.4
  184.8 0.8 dynamic-slice_bitcast_fusion.4
  185.7 15.3 %attention_backward.3 = (bf16[2,512,1152]{2,1,0:T(8,128)(2,1)S(1)}, bf16[8,144,384]{2,1,0:T(8,128)(2,1)S(1)}, bf16[8,144,384]{2,1,0:T(8,128)(2,1)}) custom-call(s32[2]{0:T(128)S(1)} %copy-done.12, s32[4]{0:T(128)S(1)} %copy-done.11, bf16[2,512,2304]{2,1,0:T(8,128)(2,1)S(1)} %bitcast.99, bf16[2,512,2304]{2,1,0:T(8,128)(2,1)S(1)} %bitcast.99, ...), custom_call_target="tpu_custom_call" | custom-call | flops 100000000 | bytes 1048576 | tf_op jit(solution)/shard_map/attention_backward/pallas_call | solution.py:404
  201.0 1.4 copy-done.4
  202.9 0.7 collective-permute-start.18
  203.6 1.8 collective-permute-start.17
  205.3 1.6 add_convert_fusion.2
  207.0 1.5 add_convert_fusion.1
  209.0 1.0 collective-permute-start.20
  210.0 2.3 collective-permute-done.18
  212.4 1.2 collective-permute-done.17
  213.7 1.5 collective-permute-start.19
  215.5 9.0 %norm_one_backward.1 = (bf16[1024,768]{1,0:T(8,128)(2,1)}, bf16[8,16,384]{2,1,0:T(8,128)(2,1)S(1)}, bf16[8,16,384]{2,1,0:T(8,128)(2,1)S(1)}) custom-call(s32[4]{0:T(128)S(1)} %copy-done.11, bf16[1024,768]{1,0:T(8,128)(2,1)S(1)} %bitcast.113, f32[1024,1]{1,0:T(8,128)S(1)} %bitcast.111, bf16[1024,768]{1,0:T(8,128)(2,1)S(1)} %copy-done, ...), custom_call_target="tpu_custom_call" | custom-call | flops 100000000 | bytes 1048576 | tf_op jit(solution)/shard_map/norm_one_backward/pallas_call | solution.py:483
  224.9 1.1 collective-permute-start.24
  226.1 1.3 collective-permute-start.25
  227.4 1.2 collective-permute-start.22
  228.6 2.7 collective-permute-start.23
  231.3 7.3 %collective-permute-done.21 = bf16[96,768]{1,0:T(8,128)(2,1)S(1)} collective-permute-done((bf16[96,768]{1,0:T(8,128)(2,1)S(1)}, bf16[96,768]{1,0:T(8,128)(2,1)S(1)}, u32[]{:S(2)}, u32[]{:S(2)}) %collective-permute-start.21) | collective-permute-done | bytes 147488 | tf_op jit(solution)/shard_map/ppermute | solution.py:586
  238.6 0.9 collective-permute-start.27
  239.5 8.3 %collective-permute-done.22 = bf16[96,768]{1,0:T(8,128)(2,1)S(1)} collective-permute-done((bf16[96,768]{1,0:T(8,128)(2,1)S(1)}, bf16[96,768]{1,0:T(8,128)(2,1)S(1)}, u32[]{:S(2)}, u32[]{:S(2)}) %collective-permute-start.22) | collective-permute-done | bytes 147488 | tf_op jit(solution)/shard_map/ppermute | solution.py:586
  248.2 2.4 reduce-scatter.2.cloned.1.call-done
  250.6 2.0 collective-permute-start.28
  252.6 0.9 collective-permute-start.29
  253.5 1.6 collective-permute-start.30
  255.1 1.1 collective-permute-start.33
  256.2 0.9 collective-permute-start.32
  257.1 1.7 collective-permute-done.28
  258.8 3.5 %collective-permute-done.29 = bf16[160,384]{1,0:T(8,128)(2,1)S(1)} collective-permute-done((bf16[160,384]{1,0:T(8,128)(2,1)S(1)}, bf16[160,384]{1,0:T(8,128)(2,1)S(1)}, u32[]{:S(2)}, u32[]{:S(2)}) %collective-permute-start.29) | collective-permute-done | bytes 122912 | tf_op jit(solution)/shard_map/ppermute | solution.py:586
  262.4 2.1 collective-permute-start.31
  264.6 0.9 fusion.2
  265.4 5.1 %collective-permute-done.31 = bf16[160,384]{1,0:T(8,128)(2,1)S(1)} collective-permute-done((bf16[160,384]{1,0:T(8,128)(2,1)S(1)}, bf16[160,384]{1,0:T(8,128)(2,1)S(1)}, u32[]{:S(2)}, u32[]{:S(2)}) %collective-permute-start.31) | collective-permute-done | bytes 122912 | tf_op jit(solution)/shard_map/ppermute | solution.py:592
  270.6 0.6 slice.169
  271.9 0.7 fusion.14
  272.7 0.9 pad_maximum_fusion.2
  (137 shorter events, 5.3 us)
Async XLA Ops:
  7.2 99.2 %all-gather.3.cloned.1.call-start = ((), (), s32[]{:S(2)}) async-start(), calls=%async_computation.2 | async-start | bytes 10027008 | tf_op jit(solution)/shard_map/all_gather | solution.py:631
  9.8 39.1 %copy-start.21 = (s32[2,128]{1,0:T(2,128)S(1)}, s32[2,128]{1,0:T(2,128)}, u32[]{:S(2)}) copy-start(s32[2,128]{1,0:T(2,128)} %param.19) | copy-start | bytes 3076
  9.8 240.9 %reduce-scatter.2.cloned.1.call-start = ((), (), s32[]{:S(2)}) async-start(), calls=%async_computation.1 | async-start | bytes 6266880 | tf_op jit(solution)/shard_map/reduce_scatter | solution.py:683
  10.8 10.1 %collective-permute-start = (bf16[208,384]{1,0:T(8,128)(2,1)S(1)}, bf16[208,384]{1,0:T(8,128)(2,1)S(1)}, u32[]{:S(2)}, u32[]{:S(2)}) collective-permute-start(bf16[208,384]{1,0:T(8,128)(2,1)S(1)} %constant_dynamic-slice_fusion.8), channel_id=1, source_target_pairs={{0,4},{1,5},{2,6},{3,7},{4,8},{5,9},{6,10},{7,11},{8,12},{9,13},{1... | collective-permute-start | bytes 479240 | tf_op jit(solution)/shard_map/ppermute | solution.py:546
  13.8 15.7 %collective-permute-start.1 = (bf16[208,384]{1,0:T(8,128)(2,1)S(1)}, bf16[208,384]{1,0:T(8,128)(2,1)S(1)}, u32[]{:S(2)}, u32[]{:S(2)}) collective-permute-start(bf16[208,384]{1,0:T(8,128)(2,1)S(1)} %constant_dynamic-slice_fusion.8), channel_id=1, source_target_pairs={{0,8},{1,9},{2,10},{3,11},{4,12},{5,13},{6,14},{7,15},{8,0},{9,1},... | collective-permute-start | bytes 479240 | tf_op jit(solution)/shard_map/ppermute | solution.py:546
  16.4 13.2 %collective-permute-start.2 = (bf16[208,384]{1,0:T(8,128)(2,1)S(1)}, bf16[208,384]{1,0:T(8,128)(2,1)S(1)}, u32[]{:S(2)}, u32[]{:S(2)}) collective-permute-start(bf16[208,384]{1,0:T(8,128)(2,1)S(1)} %constant_dynamic-slice_fusion.8), channel_id=1, source_target_pairs={{0,12},{1,13},{2,14},{3,15},{4,0},{5,1},{6,2},{7,3},{8,4},{9,5},{1... | collective-permute-start | bytes 479240 | tf_op jit(solution)/shard_map/ppermute | solution.py:546
  29.7 27.3 %copy-start.16 = (bf16[4,208,384]{2,1,0:T(8,128)(2,1)}, bf16[4,208,384]{2,1,0:T(8,128)(2,1)S(1)}, u32[]{:S(2)}) copy-start(bf16[4,208,384]{2,1,0:T(8,128)(2,1)S(1)} %pad_maximum_fusion.1.refs_0_) | copy-start | bytes 1916932
  29.7 15.3 %collective-permute-start.3 = (bf16[4,208,384]{2,1,0:T(8,128)(2,1)S(1)}, bf16[4,208,384]{2,1,0:T(8,128)(2,1)S(1)}, u32[]{:S(2)}, u32[]{:S(2)}) collective-permute-start(bf16[4,208,384]{2,1,0:T(8,128)(2,1)S(1)} %pad_maximum_fusion.1.refs_0_), channel_id=1, source_target_pairs={{0,16},{16,0},{1,17},{17,1},{2,18},{18,2},{3,19},{19,3},{4,20},{20... | collective-permute-start | bytes 1916936 | tf_op jit(solution)/shard_map/ppermute | solution.py:547
  31.3 15.4 %collective-permute-start.4 = (bf16[4,208,384]{2,1,0:T(8,128)(2,1)S(1)}, bf16[4,208,384]{2,1,0:T(8,128)(2,1)S(1)}, u32[]{:S(2)}, u32[]{:S(2)}) collective-permute-start(bf16[4,208,384]{2,1,0:T(8,128)(2,1)S(1)} %pad_maximum_fusion.1.refs_0_), channel_id=1, source_target_pairs={{0,2},{1,3},{2,0},{3,1},{4,6},{5,7},{6,4},{7,5},{8,10},{9,11},{10,... | collective-permute-start | bytes 1916936 | tf_op jit(solution)/shard_map/ppermute | solution.py:548
  45.0 12.0 %copy-start.18 = (bf16[4,208,384]{2,1,0:T(8,128)(2,1)}, bf16[4,208,384]{2,1,0:T(8,128)(2,1)S(1)}, u32[]{:S(2)}) copy-start(bf16[4,208,384]{2,1,0:T(8,128)(2,1)S(1)} %collective-permute-done.3.refs_1_) | copy-start | bytes 1916932
  45.1 8.0 %collective-permute-start.5 = (bf16[2,208,384]{2,1,0:T(8,128)(2,1)S(1)}, bf16[2,208,384]{2,1,0:T(8,128)(2,1)S(1)}, u32[]{:S(2)}, u32[]{:S(2)}) collective-permute-start(bf16[2,208,384]{2,1,0:T(8,128)(2,1)S(1)} %slice.145), channel_id=1, source_target_pairs={{0,2},{1,3},{2,0},{3,1},{4,6},{5,7},{6,4},{7,5},{8,10},{9,11},{10,... | collective-permute-start | bytes 958472 | tf_op jit(solution)/shard_map/ppermute | solution.py:549
  46.7 10.3 %copy-start.19 = (bf16[4,208,384]{2,1,0:T(8,128)(2,1)}, bf16[4,208,384]{2,1,0:T(8,128)(2,1)S(1)}, u32[]{:S(2)}) copy-start(bf16[4,208,384]{2,1,0:T(8,128)(2,1)S(1)} %collective-permute-done.4.refs_2_) | copy-start | bytes 1916932
  46.7 7.5 %collective-permute-start.6 = (bf16[2,208,384]{2,1,0:T(8,128)(2,1)S(1)}, bf16[2,208,384]{2,1,0:T(8,128)(2,1)}, u32[]{:S(2)}, u32[]{:S(2)}) collective-permute-start(bf16[2,208,384]{2,1,0:T(8,128)(2,1)S(1)} %slice.146), channel_id=1, source_target_pairs={{0,16},{16,0},{1,17},{17,1},{2,18},{18,2},{3,19},{19,3},{4,20},{20... | collective-permute-start | bytes 958472 | tf_op jit(solution)/shard_map/ppermute | solution.py:550
  48.3 8.6 %collective-permute-start.7 = (bf16[4,208,384]{2,1,0:T(8,128)(2,1)S(1)}, bf16[4,208,384]{2,1,0:T(8,128)(2,1)S(1)}, u32[]{:S(2)}, u32[]{:S(2)}) collective-permute-start(bf16[4,208,384]{2,1,0:T(8,128)(2,1)S(1)} %pad_maximum_fusion.1.refs_0_), channel_id=1, source_target_pairs={{0,1},{1,0},{2,3},{3,2},{4,5},{5,4},{6,7},{7,6},{8,9},{9,8},{10,11... | collective-permute-start | bytes 1916936 | tf_op jit(solution)/shard_map/ppermute | solution.py:552
  48.3 8.6 %collective-permute-start.8 = (bf16[4,208,384]{2,1,0:T(8,128)(2,1)S(1)}, bf16[4,208,384]{2,1,0:T(8,128)(2,1)}, u32[]{:S(2)}, u32[]{:S(2)}) collective-permute-start(bf16[4,208,384]{2,1,0:T(8,128)(2,1)S(1)} %collective-permute-done.3.refs_1_), channel_id=1, source_target_pairs={{0,1},{1,0},{2,3},{3,2},{4,5},{5,4},{6,7},{7,6},{8,9},{9,8},{10,11... | collective-permute-start | bytes 1916936 | tf_op jit(solution)/shard_map/ppermute | solution.py:552
  48.8 8.1 %collective-permute-start.9 = (bf16[4,208,384]{2,1,0:T(8,128)(2,1)S(1)}, bf16[4,208,384]{2,1,0:T(8,128)(2,1)}, u32[]{:S(2)}, u32[]{:S(2)}) collective-permute-start(bf16[4,208,384]{2,1,0:T(8,128)(2,1)S(1)} %collective-permute-done.4.refs_2_), channel_id=1, source_target_pairs={{0,1},{1,0},{2,3},{3,2},{4,5},{5,4},{6,7},{7,6},{8,9},{9,8},{10,11... | collective-permute-start | bytes 1916936 | tf_op jit(solution)/shard_map/ppermute | solution.py:552
  53.1 3.9 %copy-start.23 = (bf16[2,208,384]{2,1,0:T(8,128)(2,1)}, bf16[2,208,384]{2,1,0:T(8,128)(2,1)S(1)}, u32[]{:S(2)}) copy-start(bf16[2,208,384]{2,1,0:T(8,128)(2,1)S(1)} %collective-permute-done.5.refs_3_) | copy-start | bytes 958468
  53.1 3.9 %collective-permute-start.10 = (bf16[2,208,384]{2,1,0:T(8,128)(2,1)S(1)}, bf16[2,208,384]{2,1,0:T(8,128)(2,1)}, u32[]{:S(2)}, u32[]{:S(2)}) collective-permute-start(bf16[2,208,384]{2,1,0:T(8,128)(2,1)S(1)} %collective-permute-done.5.refs_3_), channel_id=1, source_target_pairs={{0,1},{1,0},{2,3},{3,2},{4,5},{5,4},{6,7},{7,6},{8,9},{9,8},{10,11... | collective-permute-start | bytes 958472 | tf_op jit(solution)/shard_map/ppermute | solution.py:552
  54.2 2.8 collective-permute-start.11
  156.4 4.9 %collective-permute-start.12 = (bf16[8,192,768]{2,1,0:T(8,128)(2,1)}, bf16[8,192,768]{2,1,0:T(8,128)(2,1)}, u32[]{:S(2)}, u32[]{:S(2)}) collective-permute-start(bf16[8,192,768]{2,1,0:T(8,128)(2,1)} %get-tuple-element.102), channel_id=1, source_target_pairs={{0,1},{1,0},{2,3},{3,2},{4,5},{5,4},{6,7},{7,6},{8,9},{9,8},{10,11... | collective-permute-start | bytes 7077896 | tf_op jit(solution)/shard_map/ppermute | solution.py:569
  156.7 4.6 %copy-start.13 = (bf16[8,192,768]{2,1,0:T(8,128)(2,1)S(1)}, bf16[8,192,768]{2,1,0:T(8,128)(2,1)}, u32[]{:S(2)}) copy-start(bf16[8,192,768]{2,1,0:T(8,128)(2,1)} %get-tuple-element.101) | copy-start | bytes 7077892
  161.3 5.4 %slice-start = ((s8[4718592]{0:T(1024)(128)(4,1)}), s8[4194304]{0:T(1024)(128)(4,1)S(1)}, s32[]{:S(2)}) async-start(s8[4718592]{0:T(1024)(128)(4,1)} %bitcast.98), calls=%async_computation.3 | async-start | bytes 8388608
  161.3 5.4 %slice-start.2 = ((s8[5111808]{0:T(1024)(128)(4,1)}), s8[4194304]{0:T(1024)(128)(4,1)S(1)}, s32[]{:S(2)}) async-start(s8[5111808]{0:T(1024)(128)(4,1)} %bitcast.100), calls=%async_computation.5 | async-start | bytes 8388608
  163.9 2.9 %slice-start.1 = ((s8[4718592]{0:T(1024)(128)(4,1)}), s8[524288]{0:T(1024)(128)(4,1)S(1)}, s32[]{:S(2)}) async-start(s8[4718592]{0:T(1024)(128)(4,1)} %bitcast.98), calls=%async_computation.4 | async-start | bytes 1048576
  163.9 3.0 %slice-start.3 = ((s8[5111808]{0:T(1024)(128)(4,1)}), s8[917504]{0:T(1024)(128)(4,1)S(1)}, s32[]{:S(2)}) async-start(s8[5111808]{0:T(1024)(128)(4,1)} %bitcast.100), calls=%async_computation.6 | async-start | bytes 1835008
  164.0 3.4 %copy-start.1 = (bf16[2,512,768]{2,1,0:T(8,128)(2,1)S(1)}, bf16[2,512,768]{2,1,0:T(8,128)(2,1)}, u32[]{:S(2)}) copy-start(bf16[2,512,768]{2,1,0:T(8,128)(2,1)} %get-tuple-element.104) | copy-start | bytes 4718596
  164.2 3.8 %copy-start = (bf16[1024,768]{1,0:T(8,128)(2,1)S(1)}, bf16[1024,768]{1,0:T(8,128)(2,1)}, u32[]{:S(2)}) copy-start(bf16[1024,768]{1,0:T(8,128)(2,1)} %get-tuple-element.98.gb_ref) | copy-start | bytes 4718596
  164.2 3.8 %copy-start.8 = (f32[2,12,512]{2,1,0:T(8,128)S(1)}, f32[2,12,512]{2,1,0:T(8,128)}, u32[]{:S(2)}) copy-start(f32[2,12,512]{2,1,0:T(8,128)} %get-tuple-element.100.lse_ref) | copy-start | bytes 147460
  164.2 3.8 %copy-start.11 = (s32[4]{0:T(128)S(1)}, s32[4]{0:T(128)}, u32[]{:S(2)}) copy-start(s32[4]{0:T(128)} %pad_add_fusion.place_ref) | copy-start | bytes 52
  164.2 3.8 %copy-start.12 = (s32[2]{0:T(128)S(1)}, s32[2]{0:T(128)}, u32[]{:S(2)}) copy-start(s32[2]{0:T(128)} %group_ref.7) | copy-start | bytes 28
  164.3 18.8 %collective-permute-start.14 = (bf16[2,192,768]{2,1,0:T(8,128)(2,1)S(1)}, bf16[2,192,768]{2,1,0:T(8,128)(2,1)S(1)}, u32[]{:S(2)}, u32[]{:S(2)}) collective-permute-start(bf16[2,192,768]{2,1,0:T(8,128)(2,1)S(1)} %get-tuple-element.113), channel_id=1, source_target_pairs={{0,2},{1,3},{2,0},{3,1},{4,6},{5,7},{6,4},{7,5},{8,10},{9,11},{10,... | collective-permute-start | bytes 1769480 | tf_op jit(solution)/shard_map/ppermute | solution.py:576
  165.6 18.8 %collective-permute-start.13 = (bf16[2,2,96,768]{3,2,1,0:T(8,128)(2,1)S(1)}, bf16[2,2,96,768]{3,2,1,0:T(8,128)(2,1)S(1)}, u32[]{:S(2)}, u32[]{:S(2)}) collective-permute-start(bf16[2,2,96,768]{3,2,1,0:T(8,128)(2,1)S(1)} %get-tuple-element.111), channel_id=1, source_target_pairs={{0,16},{16,0},{1,17},{17,1},{2,18},{18,2},{3,19},{19,3},{4,20},{20... | collective-permute-start | bytes 1769480 | tf_op jit(solution)/shard_map/ppermute | solution.py:576
  183.1 1.7 copy-start.2
  202.4 2.9 %collective-permute-start.15 = (bf16[8,144,384]{2,1,0:T(8,128)(2,1)}, bf16[8,144,384]{2,1,0:T(8,128)(2,1)}, u32[]{:S(2)}, u32[]{:S(2)}) collective-permute-start(bf16[8,144,384]{2,1,0:T(8,128)(2,1)} %get-tuple-element.125), channel_id=1, source_target_pairs={{0,1},{1,0},{2,3},{3,2},{4,5},{5,4},{6,7},{7,6},{8,9},{9,8},{10,11... | collective-permute-start | bytes 2654216 | tf_op jit(solution)/shard_map/ppermute | solution.py:569
  202.6 4.3 %collective-permute-start.16 = (bf16[8,144,384]{2,1,0:T(8,128)(2,1)}, bf16[8,144,384]{2,1,0:T(8,128)(2,1)}, u32[]{:S(2)}, u32[]{:S(2)}) collective-permute-start(bf16[8,144,384]{2,1,0:T(8,128)(2,1)} %get-tuple-element.127), channel_id=1, source_target_pairs={{0,1},{1,0},{2,3},{3,2},{4,5},{5,4},{6,7},{7,6},{8,9},{9,8},{10,11... | collective-permute-start | bytes 2654216 | tf_op jit(solution)/shard_map/ppermute | solution.py:569
  202.9 9.4 %collective-permute-start.18 = (bf16[2,96,768]{2,1,0:T(8,128)(2,1)}, bf16[2,96,768]{2,1,0:T(8,128)(2,1)S(1)}, u32[]{:S(2)}, u32[]{:S(2)}) collective-permute-start(bf16[2,96,768]{2,1,0:T(8,128)(2,1)} %get-tuple-element.134), channel_id=1, source_target_pairs={{0,16},{16,0},{1,17},{17,1},{2,18},{18,2},{3,19},{19,3},{4,20},{20... | collective-permute-start | bytes 884744 | tf_op jit(solution)/shard_map/ppermute | solution.py:580
  203.6 10.1 %collective-permute-start.17 = (bf16[2,96,768]{2,1,0:T(8,128)(2,1)}, bf16[2,96,768]{2,1,0:T(8,128)(2,1)S(1)}, u32[]{:S(2)}, u32[]{:S(2)}) collective-permute-start(bf16[2,96,768]{2,1,0:T(8,128)(2,1)} %get-tuple-element.132), channel_id=1, source_target_pairs={{0,2},{1,3},{2,0},{3,1},{4,6},{5,7},{6,4},{7,5},{8,10},{9,11},{10,... | collective-permute-start | bytes 884744 | tf_op jit(solution)/shard_map/ppermute | solution.py:580
  205.3 10.1 %slice-start.4 = ((s8[5111808]{0:T(1024)(128)(4,1)}), s8[4194304]{0:T(1024)(128)(4,1)S(1)}, s32[]{:S(2)}) async-start(s8[5111808]{0:T(1024)(128)(4,1)} %bitcast.102), calls=%async_computation.7 | async-start | bytes 8388608
  208.4 6.9 %slice-start.5 = ((s8[5111808]{0:T(1024)(128)(4,1)}), s8[917504]{0:T(1024)(128)(4,1)S(1)}, s32[]{:S(2)}) async-start(s8[5111808]{0:T(1024)(128)(4,1)} %bitcast.102), calls=%async_computation.8 | async-start | bytes 1835008
  208.5 6.9 %copy-start.7 = (bf16[2,512,768]{2,1,0:T(8,128)(2,1)S(1)}, bf16[2,512,768]{2,1,0:T(8,128)(2,1)}, u32[]{:S(2)}) copy-start(bf16[2,512,768]{2,1,0:T(8,128)(2,1)} %tok_ref.1) | copy-start | bytes 4718596
  208.7 3.6 %copy-start.14 = (bf16[2,96,768]{2,1,0:T(8,128)(2,1)S(1)}, bf16[2,96,768]{2,1,0:T(8,128)(2,1)}, u32[]{:S(2)}) copy-start(bf16[2,96,768]{2,1,0:T(8,128)(2,1)} %get-tuple-element.133) | copy-start | bytes 884740
  208.7 4.9 %copy-start.15 = (bf16[2,96,768]{2,1,0:T(8,128)(2,1)S(1)}, bf16[2,96,768]{2,1,0:T(8,128)(2,1)}, u32[]{:S(2)}) copy-start(bf16[2,96,768]{2,1,0:T(8,128)(2,1)} %get-tuple-element.131) | copy-start | bytes 884740
  208.7 6.7 %copy-start.6 = (f32[1,1024]{0,1:T(8,128)S(1)}, f32[1,1024]{0,1:T(8,128)}, u32[]{:S(2)}) copy-start(f32[1,1024]{0,1:T(8,128)} %copy.41) | copy-start | bytes 12292
  208.7 6.7 %copy-start.9 = (f32[16,768]{1,0:T(8,128)S(1)}, f32[16,768]{1,0:T(8,128)}, u32[]{:S(2)}) copy-start(f32[16,768]{1,0:T(8,128)} %get-tuple-element.94.vec_ref) | copy-start | bytes 147460
  208.7 6.7 %copy-start.10 = (f32[16,768]{1,0:T(8,128)S(1)}, f32[16,768]{1,0:T(8,128)}, u32[]{:S(2)}) copy-start(f32[16,768]{1,0:T(8,128)} %get-tuple-element.129.gmlp_ref) | copy-start | bytes 147460
  208.9 6.6 %copy-start.5 = (bf16[2,512,1152]{2,1,0:T(8,128)(2,1)S(1)}, bf16[2,512,1152]{2,1,0:T(8,128)(2,1)}, u32[]{:S(2)}) copy-start(bf16[2,512,1152]{2,1,0:T(8,128)(2,1)} %copy-done.4) | copy-start | bytes 7077892
  209.0 6.5 %copy-start.3 = (bf16[2,512,1152]{2,1,0:T(8,128)(2,1)S(1)}, bf16[2,512,1152]{2,1,0:T(8,128)(2,1)}, u32[]{:S(2)}) copy-start(bf16[2,512,1152]{2,1,0:T(8,128)(2,1)} %copy-done.2) | copy-start | bytes 7077892
  209.0 15.5 %collective-permute-start.20 = (bf16[2,288,384]{2,1,0:T(8,128)(2,1)S(1)}, bf16[2,288,384]{2,1,0:T(8,128)(2,1)S(1)}, u32[]{:S(2)}, u32[]{:S(2)}) collective-permute-start(bf16[2,288,384]{2,1,0:T(8,128)(2,1)S(1)} %get-tuple-element.142), channel_id=1, source_target_pairs={{0,2},{1,3},{2,0},{3,1},{4,6},{5,7},{6,4},{7,5},{8,10},{9,11},{10,... | collective-permute-start | bytes 1327112 | tf_op jit(solution)/shard_map/ppermute | solution.py:576
  213.7 11.0 %collective-permute-start.19 = (bf16[2,2,144,384]{3,2,1,0:T(8,128)(2,1)S(1)}, bf16[2,2,144,384]{3,2,1,0:T(8,128)(2,1)S(1)}, u32[]{:S(2)}, u32[]{:S(2)}) collective-permute-start(bf16[2,2,144,384]{3,2,1,0:T(8,128)(2,1)S(1)} %get-tuple-element.140), channel_id=1, source_target_pairs={{0,16},{16,0},{1,17},{17,1},{2,18},{18,2},{3,19},{19,3},{4,20},{20... | collective-permute-start | bytes 1327112 | tf_op jit(solution)/shard_map/ppermute | solution.py:576
  224.8 3.7 %collective-permute-start.26 = (bf16[8,16,384]{2,1,0:T(8,128)(2,1)S(1)}, bf16[8,16,384]{2,1,0:T(8,128)(2,1)S(1)}, u32[]{:S(2)}, u32[]{:S(2)}) collective-permute-start(bf16[8,16,384]{2,1,0:T(8,128)(2,1)S(1)} %get-tuple-element.157), channel_id=1, source_target_pairs={{0,1},{1,0},{2,3},{3,2},{4,5},{5,4},{6,7},{7,6},{8,9},{9,8},{10,11... | collective-permute-start | bytes 294920 | tf_op jit(solution)/shard_map/ppermute | solution.py:679
  224.9 23.0 %collective-permute-start.24 = (bf16[2,144,384]{2,1,0:T(8,128)(2,1)S(1)}, bf16[2,144,384]{2,1,0:T(8,128)(2,1)S(1)}, u32[]{:S(2)}, u32[]{:S(2)}) collective-permute-start(bf16[2,144,384]{2,1,0:T(8,128)(2,1)S(1)} %get-tuple-element.153), channel_id=1, source_target_pairs={{0,2},{1,3},{2,0},{3,1},{4,6},{5,7},{6,4},{7,5},{8,10},{9,11},{10,... | collective-permute-start | bytes 663560 | tf_op jit(solution)/shard_map/ppermute | solution.py:580
  226.1 22.0 %collective-permute-start.25 = (bf16[2,144,384]{2,1,0:T(8,128)(2,1)S(1)}, bf16[2,144,384]{2,1,0:T(8,128)(2,1)S(1)}, u32[]{:S(2)}, u32[]{:S(2)}) collective-permute-start(bf16[2,144,384]{2,1,0:T(8,128)(2,1)S(1)} %get-tuple-element.155), channel_id=1, source_target_pairs={{0,16},{16,0},{1,17},{17,1},{2,18},{18,2},{3,19},{19,3},{4,20},{20... | collective-permute-start | bytes 663560 | tf_op jit(solution)/shard_map/ppermute | solution.py:580
  227.4 11.2 %collective-permute-start.21 = (bf16[96,768]{1,0:T(8,128)(2,1)S(1)}, bf16[96,768]{1,0:T(8,128)(2,1)S(1)}, u32[]{:S(2)}, u32[]{:S(2)}) collective-permute-start(bf16[96,768]{1,0:T(8,128)(2,1)S(1)} %get-tuple-element.149), channel_id=1, source_target_pairs={{0,4},{1,5},{2,6},{3,7},{4,8},{5,9},{6,10},{7,11},{8,12},{9,13},{1... | collective-permute-start | bytes 442376 | tf_op jit(solution)/shard_map/ppermute | solution.py:586
  227.4 20.4 %collective-permute-start.22 = (bf16[96,768]{1,0:T(8,128)(2,1)S(1)}, bf16[96,768]{1,0:T(8,128)(2,1)S(1)}, u32[]{:S(2)}, u32[]{:S(2)}) collective-permute-start(bf16[96,768]{1,0:T(8,128)(2,1)S(1)} %get-tuple-element.150), channel_id=1, source_target_pairs={{0,8},{1,9},{2,10},{3,11},{4,12},{5,13},{6,14},{7,15},{8,0},{9,1},... | collective-permute-start | bytes 442376 | tf_op jit(solution)/shard_map/ppermute | solution.py:586
  228.6 19.3 %collective-permute-start.23 = (bf16[96,768]{1,0:T(8,128)(2,1)S(1)}, bf16[96,768]{1,0:T(8,128)(2,1)S(1)}, u32[]{:S(2)}, u32[]{:S(2)}) collective-permute-start(bf16[96,768]{1,0:T(8,128)(2,1)S(1)} %get-tuple-element.151), channel_id=1, source_target_pairs={{0,12},{1,13},{2,14},{3,15},{4,0},{5,1},{6,2},{7,3},{8,4},{9,5},{1... | collective-permute-start | bytes 442376 | tf_op jit(solution)/shard_map/ppermute | solution.py:586
  238.6 9.4 %collective-permute-start.27 = (bf16[4,16,384]{2,1,0:T(8,128)(2,1)S(1)}, bf16[4,16,384]{2,1,0:T(8,128)(2,1)S(1)}, u32[]{:S(2)}, u32[]{:S(2)}) collective-permute-start(bf16[4,16,384]{2,1,0:T(8,128)(2,1)S(1)} %dynamic-slice_bitcast_fusion.12), channel_id=1, source_target_pairs={{0,2},{1,3},{2,0},{3,1},{4,6},{5,7},{6,4},{7,5},{8,10},{9,11},{10,... | collective-permute-start | bytes 147464 | tf_op jit(solution)/shard_map/ppermute | solution.py:680
  250.6 8.2 %collective-permute-start.28 = (bf16[160,384]{1,0:T(8,128)(2,1)S(1)}, bf16[160,384]{1,0:T(8,128)(2,1)S(1)}, u32[]{:S(2)}, u32[]{:S(2)}) collective-permute-start(bf16[160,384]{1,0:T(8,128)(2,1)S(1)} %get-tuple-element.163), channel_id=1, source_target_pairs={{0,4},{1,5},{2,6},{3,7},{4,8},{5,9},{6,10},{7,11},{8,12},{9,13},{1... | collective-permute-start | bytes 368648 | tf_op jit(solution)/shard_map/ppermute | solution.py:586
  252.6 9.7 %collective-permute-start.29 = (bf16[160,384]{1,0:T(8,128)(2,1)S(1)}, bf16[160,384]{1,0:T(8,128)(2,1)S(1)}, u32[]{:S(2)}, u32[]{:S(2)}) collective-permute-start(bf16[160,384]{1,0:T(8,128)(2,1)S(1)} %get-tuple-element.164), channel_id=1, source_target_pairs={{0,8},{1,9},{2,10},{3,11},{4,12},{5,13},{6,14},{7,15},{8,0},{9,1},... | collective-permute-start | bytes 368648 | tf_op jit(solution)/shard_map/ppermute | solution.py:586
  253.5 8.8 %collective-permute-start.30 = (bf16[160,384]{1,0:T(8,128)(2,1)S(1)}, bf16[160,384]{1,0:T(8,128)(2,1)S(1)}, u32[]{:S(2)}, u32[]{:S(2)}) collective-permute-start(bf16[160,384]{1,0:T(8,128)(2,1)S(1)} %get-tuple-element.165), channel_id=1, source_target_pairs={{0,12},{1,13},{2,14},{3,15},{4,0},{5,1},{6,2},{7,3},{8,4},{9,5},{1... | collective-permute-start | bytes 368648 | tf_op jit(solution)/shard_map/ppermute | solution.py:586
  255.1 16.8 %copy-start.17 = (bf16[1,240,768]{2,1,0:T(8,128)(2,1)S(1)}, bf16[1,240,768]{2,1,0:T(8,128)(2,1)}, u32[]{:S(2)}) copy-start(bf16[1,240,768]{2,1,0:T(8,128)(2,1)} %reduce-scatter.2.cloned.1.call-done) | copy-start | bytes 1105924
  255.1 9.5 %collective-permute-start.33 = (bf16[96,768]{1,0:T(8,128)(2,1)S(1)}, bf16[96,768]{1,0:T(8,128)(2,1)S(1)}, u32[]{:S(2)}, u32[]{:S(2)}) collective-permute-start(bf16[96,768]{1,0:T(8,128)(2,1)S(1)} %add_convert_fusion.11), channel_id=1, source_target_pairs={{0,16},{16,0},{1,17},{17,1},{2,18},{18,2},{3,19},{19,3},{4,20},{20... | collective-permute-start | bytes 442376 | tf_op jit(solution)/shard_map/ppermute | solution.py:592
  256.2 15.7 %collective-permute-start.32 = (bf16[240,768]{1,0:T(8,128)(2,1)}, bf16[240,768]{1,0:T(8,128)(2,1)S(1)}, u32[]{:S(2)}, u32[]{:S(2)}) collective-permute-start(bf16[240,768]{1,0:T(8,128)(2,1)} %bitcast.120), channel_id=1, source_target_pairs={{0,16},{16,0},{1,17},{17,1},{2,18},{18,2},{3,19},{19,3},{4,20},{20... | collective-permute-start | bytes 1105928 | tf_op jit(solution)/shard_map/ppermute | solution.py:685
  262.4 8.1 %collective-permute-start.31 = (bf16[160,384]{1,0:T(8,128)(2,1)S(1)}, bf16[160,384]{1,0:T(8,128)(2,1)S(1)}, u32[]{:S(2)}, u32[]{:S(2)}) collective-permute-start(bf16[160,384]{1,0:T(8,128)(2,1)S(1)} %add_convert_fusion.12), channel_id=1, source_target_pairs={{0,16},{16,0},{1,17},{17,1},{2,18},{18,2},{3,19},{19,3},{4,20},{20... | collective-permute-start | bytes 368648 | tf_op jit(solution)/shard_map/ppermute | solution.py:592
  271.8 1.7 copy-start.20
  (3 other events, 3.0 us)
Sparse Core Ops, SparseCore 0:
  10.9 95.4 all-gather.2
  156.9 93.7 reduce-scatter.1

commit v3 on v2

--- a/solution.py
+++ b/solution.py
@@ -221,7 +221,7 @@
 
 def mlp_kernel(
     group_ref, place_ref, tok_ref, mask_ref, cot_ref, att_ref, vec_ref, wo_ref, wu_ref, wd_ref,
-    out_ref, gb_ref, gw_ref, keep_ref, send_ref, gvec_ref,
+    out_ref, gb_ref, gw_ref, keep_ref, send_ref, keep_out_ref, send_out_ref, gvec_ref,
     hidden, n2, gr, act, gpre, acc, gn2,
 ):
     j = pl.program_id(0)
@@ -287,7 +287,8 @@
             gb = gh.astype(BF)
             gb_ref[rows] = gb
             gvec_ref[B_OUT : B_OUT + 1] += colsum(gb.astype(F32))
-        gw_ref[...] = dot_tn(att_ref[...], gb_ref[...]).astype(BF).reshape(gw_ref.shape)
+        grad = dot_tn(att_ref[...], gb_ref[...]).astype(BF).reshape(BLOCKS // 2, 2, 48, dim)
+        store_by_core(place_ref[2], grad, keep_out_ref, send_out_ref, slice(0, 48))
 
 
 def whole(*shape):
@@ -315,9 +316,11 @@
             out_specs=[
                 whole(rows, dim),
                 whole(rows, dim),
-                pl.BlockSpec((BLOCKS, 48, dim), lambda j, *_: (0, j, 0)),
+                pl.BlockSpec((BLOCKS, 48, dim), lambda j, *_: (0, jnp.minimum(j, 3), 0)),
                 pl.BlockSpec((2, 192, dim), lambda j, *_: (jnp.minimum(j, 3), 0, 0)),
                 pl.BlockSpec((2, 192, dim), lambda j, *_: (jnp.minimum(j, 3), 0, 0)),
+                whole(BLOCKS // 2, 48, dim),
+                whole(BLOCKS // 2, 48, dim),
                 whole(16, dim),
             ],
             scratch_shapes=[
@@ -333,9 +336,11 @@
         out_shape=[
             out((rows, dim), BF),
             out((rows, dim), BF),
-            out((BLOCKS, 240, dim), BF),
+            out((BLOCKS, 192, dim), BF),
             out((BLOCKS // 2, 192, dim), BF),
             out((BLOCKS // 2, 192, dim), BF),
+            out((BLOCKS // 2, 48, dim), BF),
+            out((BLOCKS // 2, 48, dim), BF),
             out((16, dim), F32),
         ],
         compiler_params=pltpu.CompilerParams(vmem_limit_bytes=VMEM_LIMIT),
@@ -653,7 +658,7 @@
     mask = jnp.any(mask_pos[:, :, None] == positions[None, None, :], axis=1).astype(F32)[..., None]
     normed, qkv, att, lse, vecs, w1 = forward_call(group_id, place, tokens, mask, pieces)
     flat = lambda a: a.reshape(clips * seq, a.shape[-1])
-    output, gb, g2, down_keep, down_send, gvec = mlp_call(
+    output, gb, g2, down_keep, down_send, out_keep, out_send, gvec = mlp_call(
         group_id, place, flat(tokens), flat(mask), flat(cotangent), flat(att), vecs, w1, w2
     )
     gb3 = gb.reshape(tokens.shape)
@@ -661,7 +666,7 @@
     back = lambda part, gb3: attention_back_call(part, group_id, place, qkv, lse, gb3, w1, flat(normed))
     after = lambda gj0, gj1, gvec: norm_one_call(place, flat(tokens), flat(mask), gb, flat(gj0), flat(gj1), vecs, w1, gvec)
     if n == BLOCKS:
-        down = Scatter([down_keep], [down_send], z, y, r)
+        down = Scatter([down_keep, out_keep], [down_send, out_send], z, y, r)
         step([down])
         (gb3,) = step([down], gb3)
         gj0, keep0, send0 = back(0, gb3)
@@ -675,9 +680,10 @@
         (gvec,) = step([rest], gvec)
         token_grad, keep2, send2 = after(gj0, gj1, gvec)
         keep2, send2 = step([rest], keep2, send2)
-        keep2, send2 = step([down, rest], keep2, send2)
+        rest.value, keep2, send2 = lax.optimization_barrier((rest.value, keep2, send2))
         few = add(keep2, lax.ppermute(send2, "fsdp", swap(1))).reshape(4, 2, *keep2.shape[1:])
-        few = add(pick(few, y, 1), lax.ppermute(pick(few, 1 - y, 1), "fsdp", swap(2)))
+        few = step([down, rest], pick(few, 1 - y, 1), pick(few, y, 1))
+        few = add(few[1], lax.ppermute(few[0], "fsdp", swap(2)))
         extra.append(few)
         step([down, rest])
         own2 = lax.psum_scatter(g2, "fsdp", scatter_dimension=0)
@@ -688,15 +694,15 @@
         sum2 = own2.astype(F32) + other2.astype(F32)
         sum1, few = rest.steps.send(rest.value)
         down_grad, _ = down.value
-        up_grad, out_grad = sum2[: 4 * width], sum2[4 * width :]
+        up_grad, down_grad, out_grad = sum2, down_grad[: 4 * width], down_grad[4 * width :]
         qkv_grad = jnp.concatenate([sum1[i * width : (i + 1) * width] for i in (0, 3, 1, 4, 2, 5)], 1)
         vg = [few[k, :width] for k in range(B_UP)] + [few[B_UP, : 4 * width]]
     else:
         (gj0, *parts0), (gj1, *parts1) = (back(part, gb3) for part in range(GROUPS))
         token_grad, *table = after(gj0, gj1, gvec)
         down_grad = scatter_whole(from_blocks(by_core(down_keep, down_send, place[2]), 1, n))
-        rest = scatter_whole(from_blocks(g2, 5, n))
-        up_grad, out_grad = rest[: 4 * width], rest[4 * width :]
+        up_grad = scatter_whole(from_blocks(g2, 4, n))
+        out_grad = scatter_whole(from_blocks(by_core(out_keep, out_send, place[2]), 1, n))
         sums = [scatter_whole(from_blocks(by_core(*parts, place[2]), 3, n)) for parts in (parts0, parts1)]
         qkv_grad = jnp.concatenate([a[i * width : (i + 1) * width] for i in range(3) for a in sums], 1)
         table = by_core(*table, place[2])

time: 286 us -> 285 us (level)
    ppermute x6, waiting for transfers between devices: 20.9 us -> 16 us  [scatter_steps(): got = [lax.ppermute(sent[k], 'fsdp', turn(k)) for k in (1, 2, 3)]]
    convert_element_type x13 -> x14, other arithmetic: 6.43 us -> 6.62 us  [add(): return (a.astype(F32) + b.astype(F32)).astype(BF)]
  transfers between devices with their start and end apart: 36 -> 37, of which waited for: 15 -> 16; matrix products, arithmetic and copies ran while one was open for 6% -> 6% of each run, Pallas kernels for 23% -> 23%
where the time goes in v3:
time: 285 us; the launch traced here: 279 us
  Pallas kernels  118 us (41%)
  waiting for transfers between devices  84.4 us (30%)
  starting transfers between devices  38.5 us (14%)
  between operations  15 us (5%)
  local copies, waits for them, and re-layouts  13.7 us (5%)
  other arithmetic  9.38 us (3%)
    pallas_call x1, Pallas kernels, mlp_call(): pl.pallas_call(mlp_kernel, grid_spec=pltpu.PrefetchScalarGridSpec(num_sca...  50.2 us
    pallas_call x2, Pallas kernels, attention_back_call(): pl.pallas_call(functools.partial(attention_back_kernel, part), grid_spec=...  30.4 us
    pallas_call x1, Pallas kernels, forward_call(): pl.pallas_call(functools.partial(forward_kernel, len(pieces)), grid_spec=...  25.7 us
    all_gather x1, waiting for transfers between devices, local(): w2 = lax.all_gather(pack2, 'fsdp', axis=0)  22.2 us
    ppermute x6, waiting for transfers between devices, scatter_steps(): got = [lax.ppermute(sent[k], 'fsdp', turn(k)) for k in (1, 2, 3)]  16 us
    ppermute x1, waiting for transfers between devices, gather_pieces(): by_x = lax.ppermute(along_z, 'rep', REP)  12.2 us
    ppermute x3, waiting for transfers between devices, gather_pieces(): lax.ppermute(half, 'fsdp', turn(k))  10.9 us
    ppermute x6, starting transfers between devices, scatter_steps(): got = [lax.ppermute(sent[k], 'fsdp', turn(k)) for k in (1, 2, 3)]  9.78 us
  transfers between devices with their start and end apart: 37, of which 16 were waited for; matrix products, arithmetic and copies ran while one was open for 6% of the time, Pallas kernels for 23%

profile of v3, /device:TPU:0, one launch (start us, length us, event | category | flops | bytes accessed | tf_op | source)
XLA Modules:
  0.0 279.0 jit_solution(3444116321956493292)
XLA Ops:
  7.2 2.5 pack.1
  9.8 0.9 constant_dynamic-slice_fusion.8
  10.8 3.1 %collective-permute-start = (bf16[208,384]{1,0:T(8,128)(2,1)S(1)}, bf16[208,384]{1,0:T(8,128)(2,1)S(1)}, u32[]{:S(2)}, u32[]{:S(2)}) collective-permute-start(bf16[208,384]{1,0:T(8,128)(2,1)S(1)} %constant_dynamic-slice_fusion.8), channel_id=1, source_target_pairs={{0,4},{1,5},{2,6},{3,7},{4,8},{5,9},{6,10},{7,11},{8,12},{9,13},{1... | collective-permute-start | bytes 479240 | tf_op jit(solution)/shard_map/ppermute | solution.py:551
  13.8 2.6 collective-permute-start.1
  16.4 1.3 collective-permute-start.2
  17.8 0.9 fusion.14
  18.7 2.2 collective-permute-done
  20.9 8.7 %collective-permute-done.1 = bf16[208,384]{1,0:T(8,128)(2,1)S(1)} collective-permute-done((bf16[208,384]{1,0:T(8,128)(2,1)S(1)}, bf16[208,384]{1,0:T(8,128)(2,1)S(1)}, u32[]{:S(2)}, u32[]{:S(2)}) %collective-permute-start.1) | collective-permute-done | bytes 159776 | tf_op jit(solution)/shard_map/ppermute | solution.py:551
  29.7 1.6 collective-permute-start.3
  31.3 1.6 collective-permute-start.4
  32.8 12.2 %collective-permute-done.3.refs_1_ = bf16[4,208,384]{2,1,0:T(8,128)(2,1)S(1)} collective-permute-done((bf16[4,208,384]{2,1,0:T(8,128)(2,1)S(1)}, bf16[4,208,384]{2,1,0:T(8,128)(2,1)S(1)}, u32[]{:S(2)}, u32[]{:S(2)}) %collective-permute-start.3) | collective-permute-done | bytes 639008 | tf_op jit(solution)/shard_map/ppermute | solution.py:552
  45.1 1.6 collective-permute-start.5
  46.7 1.6 collective-permute-start.6
  48.3 0.5 collective-permute-start.8
  49.0 4.1 %collective-permute-done.5.refs_3_ = bf16[2,208,384]{2,1,0:T(8,128)(2,1)S(1)} collective-permute-done((bf16[2,208,384]{2,1,0:T(8,128)(2,1)S(1)}, bf16[2,208,384]{2,1,0:T(8,128)(2,1)S(1)}, u32[]{:S(2)}, u32[]{:S(2)}) %collective-permute-start.5) | collective-permute-done | bytes 319520 | tf_op jit(solution)/shard_map/ppermute | solution.py:554
  53.1 1.1 collective-permute-done.6.refs_4_
  54.3 1.0 copy.37.mask_ref
  55.3 1.0 copy.41
  56.3 0.6 pad_add_fusion.place_ref
  57.0 0.7 copy-done.23
  57.8 0.7 copy-done.25
  58.5 25.7 %attention_forward.1 = (bf16[2,512,768]{2,1,0:T(8,128)(2,1)}, bf16[2,512,2304]{2,1,0:T(8,128)(2,1)}, bf16[2,512,768]{2,1,0:T(8,128)(2,1)}, f32[2,12,512]{2,1,0:T...) custom-call(s32[2]{0:T(128)} %group_ref.7, s32[4]{0:T(128)} %pad_add_fusion.place_ref, ...), custom_call_target="tpu_custom_call" | custom-call | flops 8999999488 | bytes 16777216 | tf_op jit(solution)/shard_map/attention_forward/pallas_call | solution.py:190
  84.2 22.2 %all-gather.3.cloned.1.call-done = bf16[6144,768]{1,0:T(8,128)(2,1)} async-done(((bf16[384,768]{1,0:T(8,128)(2,1)}), bf16[6144,768]{1,0:T(8,128)(2,1)}) %all-gather.3.cloned.1.call-update) | async-done | bytes 9437200 | tf_op jit(solution)/shard_map/all_gather | solution.py:636
  106.3 50.2 %mlp.1 = (bf16[1024,768]{1,0:T(8,128)(2,1)}, bf16[1024,768]{1,0:T(8,128)(2,1)}, bf16[16,192,768]{2,1,0:T(8,128)(2,1)}, bf16[8,192,768]{2,1,0:T(8,128)(2,1)}, bf1...) custom-call(s32[2]{0:T(128)} %group_ref.7, ...), custom_call_target="tpu_custom_call" | custom-call | flops 44999999488 | bytes 31457280 | tf_op jit(solution)/shard_map/mlp/pallas_call | solution.py:301
  157.2 5.1 %collective-permute-done.13 = bf16[8,48,768]{2,1,0:T(8,128)(2,1)S(1)} collective-permute-done((bf16[8,48,768]{2,1,0:T(8,128)(2,1)}, bf16[8,48,768]{2,1,0:T(8,128)(2,1)S(1)}, u32[]{:S(2)}, u32[]{:S(2)}) %collective-permute-start.13) | collective-permute-done | bytes 589856 | tf_op jit(solution)/shard_map/ppermute | solution.py:574
  162.5 2.5 add_convert_fusion
  165.5 1.5 collective-permute-start.15
  167.0 1.0 collective-permute-start.14
  168.4 0.5 copy-done
  168.9 15.1 %attention_backward.2 = (bf16[2,512,1152]{2,1,0:T(8,128)(2,1)S(1)}, bf16[8,144,384]{2,1,0:T(8,128)(2,1)S(1)}, bf16[8,144,384]{2,1,0:T(8,128)(2,1)}) custom-call(s32[2]{0:T(128)S(1)} %copy-done.12, s32[4]{0:T(128)S(1)} %copy-done.11, bf16[2,512,2304]{2,1,0:T(8,128)(2,1)S(1)} %bitcast.98, bf16[2,512,2304]{2,1,0:T(8,128)(2,1)S(1)} %bitcast.98, ...), custom_call_target="tpu_custom_call" | custom-call | flops 100000000 | bytes 1048576 | tf_op jit(solution)/shard_map/attention_backward/pallas_call | solution.py:409
  184.3 1.2 constant_dynamic-slice_fusion.4
  185.9 0.9 dynamic-slice_bitcast_fusion.4
  186.8 15.3 %attention_backward.3 = (bf16[2,512,1152]{2,1,0:T(8,128)(2,1)S(1)}, bf16[8,144,384]{2,1,0:T(8,128)(2,1)S(1)}, bf16[8,144,384]{2,1,0:T(8,128)(2,1)}) custom-call(s32[2]{0:T(128)S(1)} %copy-done.12, s32[4]{0:T(128)S(1)} %copy-done.11, bf16[2,512,2304]{2,1,0:T(8,128)(2,1)S(1)} %bitcast.98, bf16[2,512,2304]{2,1,0:T(8,128)(2,1)S(1)} %bitcast.98, ...), custom_call_target="tpu_custom_call" | custom-call | flops 100000000 | bytes 1048576 | tf_op jit(solution)/shard_map/attention_backward/pallas_call | solution.py:409
  202.1 1.4 copy-done.4
  203.6 0.5 collective-permute-start.17
  204.1 0.7 collective-permute-start.19
  204.7 1.7 collective-permute-start.18
  206.5 1.5 add_convert_fusion.2
  208.0 1.6 add_convert_fusion.1
  210.0 1.4 collective-permute-start.21
  211.4 3.4 %collective-permute-done.19 = bf16[2,120,768]{2,1,0:T(8,128)(2,1)S(1)} collective-permute-done((bf16[2,120,768]{2,1,0:T(8,128)(2,1)}, bf16[2,120,768]{2,1,0:T(8,128)(2,1)S(1)}, u32[]{:S(2)}, u32[]{:S(2)}) %collective-permute-start.19) | collective-permute-done | bytes 368672 | tf_op jit(solution)/shard_map/ppermute | solution.py:585
  214.9 1.2 collective-permute-start.20
  216.5 9.2 %norm_one_backward.1 = (bf16[1024,768]{1,0:T(8,128)(2,1)}, bf16[8,16,384]{2,1,0:T(8,128)(2,1)S(1)}, bf16[8,16,384]{2,1,0:T(8,128)(2,1)S(1)}) custom-call(s32[4]{0:T(128)S(1)} %copy-done.11, bf16[1024,768]{1,0:T(8,128)(2,1)S(1)} %bitcast.112, f32[1024,1]{1,0:T(8,128)S(1)} %bitcast.110, bf16[1024,768]{1,0:T(8,128)(2,1)S(1)} %copy-done, ...), custom_call_target="tpu_custom_call" | custom-call | flops 100000000 | bytes 1048576 | tf_op jit(solution)/shard_map/norm_one_backward/pallas_call | solution.py:488
  225.7 2.6 collective-permute-done.21
  229.0 1.0 collective-permute-done.22
  230.1 1.5 collective-permute-start.28
  231.6 0.6 collective-permute-start.26
  232.2 0.9 collective-permute-start.27
  233.1 1.9 collective-permute-start.24
  235.0 1.9 collective-permute-start.25
  236.9 5.6 %collective-permute-done.23 = bf16[120,768]{1,0:T(8,128)(2,1)S(1)} collective-permute-done((bf16[120,768]{1,0:T(8,128)(2,1)S(1)}, bf16[120,768]{1,0:T(8,128)(2,1)S(1)}, u32[]{:S(2)}, u32[]{:S(2)}) %collective-permute-start.23) | collective-permute-done | bytes 184352 | tf_op jit(solution)/shard_map/ppermute | solution.py:591
  242.5 6.3 %collective-permute-done.24 = bf16[120,768]{1,0:T(8,128)(2,1)S(1)} collective-permute-done((bf16[120,768]{1,0:T(8,128)(2,1)S(1)}, bf16[120,768]{1,0:T(8,128)(2,1)S(1)}, u32[]{:S(2)}, u32[]{:S(2)}) %collective-permute-start.24) | collective-permute-done | bytes 184352 | tf_op jit(solution)/shard_map/ppermute | solution.py:591
  249.2 3.5 %collective-permute-start.29 = (bf16[160,384]{1,0:T(8,128)(2,1)S(1)}, bf16[160,384]{1,0:T(8,128)(2,1)S(1)}, u32[]{:S(2)}, u32[]{:S(2)}) collective-permute-start(bf16[160,384]{1,0:T(8,128)(2,1)S(1)} %get-tuple-element.183), channel_id=1, source_target_pairs={{0,4},{1,5},{2,6},{3,7},{4,8},{5,9},{6,10},{7,11},{8,12},{9,13},{1... | collective-permute-start | bytes 368648 | tf_op jit(solution)/shard_map/ppermute | solution.py:591
  252.8 2.4 collective-permute-start.31
  255.2 1.2 collective-permute-start.34
  256.4 0.9 collective-permute-start.33
  257.2 4.1 %collective-permute-done.30 = bf16[160,384]{1,0:T(8,128)(2,1)S(1)} collective-permute-done((bf16[160,384]{1,0:T(8,128)(2,1)S(1)}, bf16[160,384]{1,0:T(8,128)(2,1)S(1)}, u32[]{:S(2)}, u32[]{:S(2)}) %collective-permute-start.30) | collective-permute-done | bytes 122912 | tf_op jit(solution)/shard_map/ppermute | solution.py:591
  261.4 1.2 collective-permute-start.32
  262.7 5.4 %collective-permute-done.33 = bf16[120,768]{1,0:T(8,128)(2,1)S(1)} collective-permute-done((bf16[120,768]{1,0:T(8,128)(2,1)S(1)}, bf16[120,768]{1,0:T(8,128)(2,1)S(1)}, u32[]{:S(2)}, u32[]{:S(2)}) %collective-permute-start.33) | collective-permute-done | bytes 184352 | tf_op jit(solution)/shard_map/ppermute | solution.py:597
  268.1 0.9 slice.169
  269.0 0.7 slice.162
  269.8 0.6 slice_bitcast_fusion
  270.4 0.6 slice.168
  271.1 0.9 pad_maximum_fusion.3
  (144 shorter events, 5.1 us)
Async XLA Ops:
  7.2 99.2 %all-gather.3.cloned.1.call-start = ((), (), s32[]{:S(2)}) async-start(), calls=%async_computation.2 | async-start | bytes 10027008 | tf_op jit(solution)/shard_map/all_gather | solution.py:636
  9.8 39.1 %copy-start.22 = (s32[2,128]{1,0:T(2,128)S(1)}, s32[2,128]{1,0:T(2,128)}, u32[]{:S(2)}) copy-start(s32[2,128]{1,0:T(2,128)} %param.19) | copy-start | bytes 3076
  9.8 239.5 %reduce-scatter.2.cloned.1.call-start = ((), (), s32[]{:S(2)}) async-start(), calls=%async_computation.1 | async-start | bytes 5013504 | tf_op jit(solution)/shard_map/reduce_scatter | solution.py:689
  10.8 10.1 %collective-permute-start = (bf16[208,384]{1,0:T(8,128)(2,1)S(1)}, bf16[208,384]{1,0:T(8,128)(2,1)S(1)}, u32[]{:S(2)}, u32[]{:S(2)}) collective-permute-start(bf16[208,384]{1,0:T(8,128)(2,1)S(1)} %constant_dynamic-slice_fusion.8), channel_id=1, source_target_pairs={{0,4},{1,5},{2,6},{3,7},{4,8},{5,9},{6,10},{7,11},{8,12},{9,13},{1... | collective-permute-start | bytes 479240 | tf_op jit(solution)/shard_map/ppermute | solution.py:551
  13.8 15.7 %collective-permute-start.1 = (bf16[208,384]{1,0:T(8,128)(2,1)S(1)}, bf16[208,384]{1,0:T(8,128)(2,1)S(1)}, u32[]{:S(2)}, u32[]{:S(2)}) collective-permute-start(bf16[208,384]{1,0:T(8,128)(2,1)S(1)} %constant_dynamic-slice_fusion.8), channel_id=1, source_target_pairs={{0,8},{1,9},{2,10},{3,11},{4,12},{5,13},{6,14},{7,15},{8,0},{9,1},... | collective-permute-start | bytes 479240 | tf_op jit(solution)/shard_map/ppermute | solution.py:551
  16.4 13.2 %collective-permute-start.2 = (bf16[208,384]{1,0:T(8,128)(2,1)S(1)}, bf16[208,384]{1,0:T(8,128)(2,1)S(1)}, u32[]{:S(2)}, u32[]{:S(2)}) collective-permute-start(bf16[208,384]{1,0:T(8,128)(2,1)S(1)} %constant_dynamic-slice_fusion.8), channel_id=1, source_target_pairs={{0,12},{1,13},{2,14},{3,15},{4,0},{5,1},{6,2},{7,3},{8,4},{9,5},{1... | collective-permute-start | bytes 479240 | tf_op jit(solution)/shard_map/ppermute | solution.py:551
  29.7 27.3 %copy-start.16 = (bf16[4,208,384]{2,1,0:T(8,128)(2,1)}, bf16[4,208,384]{2,1,0:T(8,128)(2,1)S(1)}, u32[]{:S(2)}) copy-start(bf16[4,208,384]{2,1,0:T(8,128)(2,1)S(1)} %pad_maximum_fusion.2.refs_0_) | copy-start | bytes 1916932
  29.7 15.3 %collective-permute-start.3 = (bf16[4,208,384]{2,1,0:T(8,128)(2,1)S(1)}, bf16[4,208,384]{2,1,0:T(8,128)(2,1)S(1)}, u32[]{:S(2)}, u32[]{:S(2)}) collective-permute-start(bf16[4,208,384]{2,1,0:T(8,128)(2,1)S(1)} %pad_maximum_fusion.2.refs_0_), channel_id=1, source_target_pairs={{0,16},{16,0},{1,17},{17,1},{2,18},{18,2},{3,19},{19,3},{4,20},{20... | collective-permute-start | bytes 1916936 | tf_op jit(solution)/shard_map/ppermute | solution.py:552
  31.3 15.4 %collective-permute-start.4 = (bf16[4,208,384]{2,1,0:T(8,128)(2,1)S(1)}, bf16[4,208,384]{2,1,0:T(8,128)(2,1)S(1)}, u32[]{:S(2)}, u32[]{:S(2)}) collective-permute-start(bf16[4,208,384]{2,1,0:T(8,128)(2,1)S(1)} %pad_maximum_fusion.2.refs_0_), channel_id=1, source_target_pairs={{0,2},{1,3},{2,0},{3,1},{4,6},{5,7},{6,4},{7,5},{8,10},{9,11},{10,... | collective-permute-start | bytes 1916936 | tf_op jit(solution)/shard_map/ppermute | solution.py:553
  45.0 11.9 %copy-start.19 = (bf16[4,208,384]{2,1,0:T(8,128)(2,1)}, bf16[4,208,384]{2,1,0:T(8,128)(2,1)S(1)}, u32[]{:S(2)}) copy-start(bf16[4,208,384]{2,1,0:T(8,128)(2,1)S(1)} %collective-permute-done.3.refs_1_) | copy-start | bytes 1916932
  45.1 8.0 %collective-permute-start.5 = (bf16[2,208,384]{2,1,0:T(8,128)(2,1)S(1)}, bf16[2,208,384]{2,1,0:T(8,128)(2,1)S(1)}, u32[]{:S(2)}, u32[]{:S(2)}) collective-permute-start(bf16[2,208,384]{2,1,0:T(8,128)(2,1)S(1)} %slice.144), channel_id=1, source_target_pairs={{0,2},{1,3},{2,0},{3,1},{4,6},{5,7},{6,4},{7,5},{8,10},{9,11},{10,... | collective-permute-start | bytes 958472 | tf_op jit(solution)/shard_map/ppermute | solution.py:554
  46.7 10.3 %copy-start.20 = (bf16[4,208,384]{2,1,0:T(8,128)(2,1)}, bf16[4,208,384]{2,1,0:T(8,128)(2,1)S(1)}, u32[]{:S(2)}) copy-start(bf16[4,208,384]{2,1,0:T(8,128)(2,1)S(1)} %collective-permute-done.4.refs_2_) | copy-start | bytes 1916932
  46.7 7.5 %collective-permute-start.6 = (bf16[2,208,384]{2,1,0:T(8,128)(2,1)S(1)}, bf16[2,208,384]{2,1,0:T(8,128)(2,1)}, u32[]{:S(2)}, u32[]{:S(2)}) collective-permute-start(bf16[2,208,384]{2,1,0:T(8,128)(2,1)S(1)} %slice.145), channel_id=1, source_target_pairs={{0,16},{16,0},{1,17},{17,1},{2,18},{18,2},{3,19},{19,3},{4,20},{20... | collective-permute-start | bytes 958472 | tf_op jit(solution)/shard_map/ppermute | solution.py:555
  48.3 8.6 %collective-permute-start.7 = (bf16[4,208,384]{2,1,0:T(8,128)(2,1)S(1)}, bf16[4,208,384]{2,1,0:T(8,128)(2,1)S(1)}, u32[]{:S(2)}, u32[]{:S(2)}) collective-permute-start(bf16[4,208,384]{2,1,0:T(8,128)(2,1)S(1)} %pad_maximum_fusion.2.refs_0_), channel_id=1, source_target_pairs={{0,1},{1,0},{2,3},{3,2},{4,5},{5,4},{6,7},{7,6},{8,9},{9,8},{10,11... | collective-permute-start | bytes 1916936 | tf_op jit(solution)/shard_map/ppermute | solution.py:557
  48.3 8.6 %collective-permute-start.8 = (bf16[4,208,384]{2,1,0:T(8,128)(2,1)S(1)}, bf16[4,208,384]{2,1,0:T(8,128)(2,1)}, u32[]{:S(2)}, u32[]{:S(2)}) collective-permute-start(bf16[4,208,384]{2,1,0:T(8,128)(2,1)S(1)} %collective-permute-done.3.refs_1_), channel_id=1, source_target_pairs={{0,1},{1,0},{2,3},{3,2},{4,5},{5,4},{6,7},{7,6},{8,9},{9,8},{10,11... | collective-permute-start | bytes 1916936 | tf_op jit(solution)/shard_map/ppermute | solution.py:557
  48.8 8.1 %collective-permute-start.9 = (bf16[4,208,384]{2,1,0:T(8,128)(2,1)S(1)}, bf16[4,208,384]{2,1,0:T(8,128)(2,1)}, u32[]{:S(2)}, u32[]{:S(2)}) collective-permute-start(bf16[4,208,384]{2,1,0:T(8,128)(2,1)S(1)} %collective-permute-done.4.refs_2_), channel_id=1, source_target_pairs={{0,1},{1,0},{2,3},{3,2},{4,5},{5,4},{6,7},{7,6},{8,9},{9,8},{10,11... | collective-permute-start | bytes 1916936 | tf_op jit(solution)/shard_map/ppermute | solution.py:557
  53.1 3.9 %copy-start.24 = (bf16[2,208,384]{2,1,0:T(8,128)(2,1)}, bf16[2,208,384]{2,1,0:T(8,128)(2,1)S(1)}, u32[]{:S(2)}) copy-start(bf16[2,208,384]{2,1,0:T(8,128)(2,1)S(1)} %collective-permute-done.5.refs_3_) | copy-start | bytes 958468
  53.1 3.8 %collective-permute-start.10 = (bf16[2,208,384]{2,1,0:T(8,128)(2,1)S(1)}, bf16[2,208,384]{2,1,0:T(8,128)(2,1)}, u32[]{:S(2)}, u32[]{:S(2)}) collective-permute-start(bf16[2,208,384]{2,1,0:T(8,128)(2,1)S(1)} %collective-permute-done.5.refs_3_), channel_id=1, source_target_pairs={{0,1},{1,0},{2,3},{3,2},{4,5},{5,4},{6,7},{7,6},{8,9},{9,8},{10,11... | collective-permute-start | bytes 958472 | tf_op jit(solution)/shard_map/ppermute | solution.py:557
  54.2 2.7 collective-permute-start.11
  156.6 5.9 %collective-permute-start.12 = (bf16[8,192,768]{2,1,0:T(8,128)(2,1)}, bf16[8,192,768]{2,1,0:T(8,128)(2,1)}, u32[]{:S(2)}, u32[]{:S(2)}) collective-permute-start(bf16[8,192,768]{2,1,0:T(8,128)(2,1)} %get-tuple-element.114), channel_id=1, source_target_pairs={{0,1},{1,0},{2,3},{3,2},{4,5},{5,4},{6,7},{7,6},{8,9},{9,8},{10,11... | collective-permute-start | bytes 7077896 | tf_op jit(solution)/shard_map/ppermute | solution.py:574
  156.9 5.4 %collective-permute-start.13 = (bf16[8,48,768]{2,1,0:T(8,128)(2,1)}, bf16[8,48,768]{2,1,0:T(8,128)(2,1)S(1)}, u32[]{:S(2)}, u32[]{:S(2)}) collective-permute-start(bf16[8,48,768]{2,1,0:T(8,128)(2,1)} %get-tuple-element.116), channel_id=1, source_target_pairs={{0,1},{1,0},{2,3},{3,2},{4,5},{5,4},{6,7},{7,6},{8,9},{9,8},{10,11... | collective-permute-start | bytes 1769480 | tf_op jit(solution)/shard_map/ppermute | solution.py:574
  157.1 5.1 %copy-start.17 = (bf16[8,48,768]{2,1,0:T(8,128)(2,1)S(1)}, bf16[8,48,768]{2,1,0:T(8,128)(2,1)}, u32[]{:S(2)}) copy-start(bf16[8,48,768]{2,1,0:T(8,128)(2,1)} %get-tuple-element.115) | copy-start | bytes 1769476
  157.1 5.3 %copy-start.13 = (bf16[8,192,768]{2,1,0:T(8,128)(2,1)S(1)}, bf16[8,192,768]{2,1,0:T(8,128)(2,1)}, u32[]{:S(2)}) copy-start(bf16[8,192,768]{2,1,0:T(8,128)(2,1)} %get-tuple-element.113) | copy-start | bytes 7077892
  162.4 5.5 %slice-start = ((s8[4718592]{0:T(1024)(128)(4,1)}), s8[4194304]{0:T(1024)(128)(4,1)S(1)}, s32[]{:S(2)}) async-start(s8[4718592]{0:T(1024)(128)(4,1)} %bitcast.97), calls=%async_computation.3 | async-start | bytes 8388608
  162.4 5.5 %slice-start.2 = ((s8[5111808]{0:T(1024)(128)(4,1)}), s8[4194304]{0:T(1024)(128)(4,1)S(1)}, s32[]{:S(2)}) async-start(s8[5111808]{0:T(1024)(128)(4,1)} %bitcast.99), calls=%async_computation.5 | async-start | bytes 8388608
  165.0 3.0 %slice-start.1 = ((s8[4718592]{0:T(1024)(128)(4,1)}), s8[524288]{0:T(1024)(128)(4,1)S(1)}, s32[]{:S(2)}) async-start(s8[4718592]{0:T(1024)(128)(4,1)} %bitcast.97), calls=%async_computation.4 | async-start | bytes 1048576
  165.0 3.0 %slice-start.3 = ((s8[5111808]{0:T(1024)(128)(4,1)}), s8[917504]{0:T(1024)(128)(4,1)S(1)}, s32[]{:S(2)}) async-start(s8[5111808]{0:T(1024)(128)(4,1)} %bitcast.99), calls=%async_computation.6 | async-start | bytes 1835008
  165.2 3.2 %copy-start.1 = (bf16[2,512,768]{2,1,0:T(8,128)(2,1)S(1)}, bf16[2,512,768]{2,1,0:T(8,128)(2,1)}, u32[]{:S(2)}) copy-start(bf16[2,512,768]{2,1,0:T(8,128)(2,1)} %get-tuple-element.118) | copy-start | bytes 4718596
  165.3 3.6 %copy-start = (bf16[1024,768]{1,0:T(8,128)(2,1)S(1)}, bf16[1024,768]{1,0:T(8,128)(2,1)}, u32[]{:S(2)}) copy-start(bf16[1024,768]{1,0:T(8,128)(2,1)} %get-tuple-element.108.gb_ref) | copy-start | bytes 4718596
  165.3 3.6 %copy-start.8 = (f32[2,12,512]{2,1,0:T(8,128)S(1)}, f32[2,12,512]{2,1,0:T(8,128)}, u32[]{:S(2)}) copy-start(f32[2,12,512]{2,1,0:T(8,128)} %get-tuple-element.110.lse_ref) | copy-start | bytes 147460
  165.4 3.6 %copy-start.11 = (s32[4]{0:T(128)S(1)}, s32[4]{0:T(128)}, u32[]{:S(2)}) copy-start(s32[4]{0:T(128)} %pad_add_fusion.place_ref) | copy-start | bytes 52
  165.4 3.5 %copy-start.12 = (s32[2]{0:T(128)S(1)}, s32[2]{0:T(128)}, u32[]{:S(2)}) copy-start(s32[2]{0:T(128)} %group_ref.7) | copy-start | bytes 28
  165.5 18.6 %collective-permute-start.15 = (bf16[2,240,768]{2,1,0:T(8,128)(2,1)S(1)}, bf16[2,240,768]{2,1,0:T(8,128)(2,1)S(1)}, u32[]{:S(2)}, u32[]{:S(2)}) collective-permute-start(bf16[2,240,768]{2,1,0:T(8,128)(2,1)S(1)} %get-tuple-element.127), channel_id=1, source_target_pairs={{0,2},{1,3},{2,0},{3,1},{4,6},{5,7},{6,4},{7,5},{8,10},{9,11},{10,... | collective-permute-start | bytes 2211848 | tf_op jit(solution)/shard_map/ppermute | solution.py:581
  167.0 18.7 %collective-permute-start.14 = (bf16[2,2,120,768]{3,2,1,0:T(8,128)(2,1)S(1)}, bf16[2,2,120,768]{3,2,1,0:T(8,128)(2,1)S(1)}, u32[]{:S(2)}, u32[]{:S(2)}) collective-permute-start(bf16[2,2,120,768]{3,2,1,0:T(8,128)(2,1)S(1)} %get-tuple-element.125), channel_id=1, source_target_pairs={{0,16},{16,0},{1,17},{17,1},{2,18},{18,2},{3,19},{19,3},{4,20},{20... | collective-permute-start | bytes 2211848 | tf_op jit(solution)/shard_map/ppermute | solution.py:581
  203.6 2.9 %collective-permute-start.16 = (bf16[8,144,384]{2,1,0:T(8,128)(2,1)}, bf16[8,144,384]{2,1,0:T(8,128)(2,1)}, u32[]{:S(2)}, u32[]{:S(2)}) collective-permute-start(bf16[8,144,384]{2,1,0:T(8,128)(2,1)} %get-tuple-element.139), channel_id=1, source_target_pairs={{0,1},{1,0},{2,3},{3,2},{4,5},{5,4},{6,7},{7,6},{8,9},{9,8},{10,11... | collective-permute-start | bytes 2654216 | tf_op jit(solution)/shard_map/ppermute | solution.py:574
  203.6 4.4 %collective-permute-start.17 = (bf16[8,144,384]{2,1,0:T(8,128)(2,1)}, bf16[8,144,384]{2,1,0:T(8,128)(2,1)}, u32[]{:S(2)}, u32[]{:S(2)}) collective-permute-start(bf16[8,144,384]{2,1,0:T(8,128)(2,1)} %get-tuple-element.141), channel_id=1, source_target_pairs={{0,1},{1,0},{2,3},{3,2},{4,5},{5,4},{6,7},{7,6},{8,9},{9,8},{10,11... | collective-permute-start | bytes 2654216 | tf_op jit(solution)/shard_map/ppermute | solution.py:574
  204.1 10.7 %collective-permute-start.19 = (bf16[2,120,768]{2,1,0:T(8,128)(2,1)}, bf16[2,120,768]{2,1,0:T(8,128)(2,1)S(1)}, u32[]{:S(2)}, u32[]{:S(2)}) collective-permute-start(bf16[2,120,768]{2,1,0:T(8,128)(2,1)} %get-tuple-element.148), channel_id=1, source_target_pairs={{0,16},{16,0},{1,17},{17,1},{2,18},{18,2},{3,19},{19,3},{4,20},{20... | collective-permute-start | bytes 1105928 | tf_op jit(solution)/shard_map/ppermute | solution.py:585
  204.7 11.6 %collective-permute-start.18 = (bf16[2,120,768]{2,1,0:T(8,128)(2,1)}, bf16[2,120,768]{2,1,0:T(8,128)(2,1)S(1)}, u32[]{:S(2)}, u32[]{:S(2)}) collective-permute-start(bf16[2,120,768]{2,1,0:T(8,128)(2,1)} %get-tuple-element.146), channel_id=1, source_target_pairs={{0,2},{1,3},{2,0},{3,1},{4,6},{5,7},{6,4},{7,5},{8,10},{9,11},{10,... | collective-permute-start | bytes 1105928 | tf_op jit(solution)/shard_map/ppermute | solution.py:585
  206.5 8.3 %copy-start.14 = (bf16[2,120,768]{2,1,0:T(8,128)(2,1)S(1)}, bf16[2,120,768]{2,1,0:T(8,128)(2,1)}, u32[]{:S(2)}) copy-start(bf16[2,120,768]{2,1,0:T(8,128)(2,1)} %get-tuple-element.147) | copy-start | bytes 1105924
  206.5 9.9 %copy-start.15 = (bf16[2,120,768]{2,1,0:T(8,128)(2,1)S(1)}, bf16[2,120,768]{2,1,0:T(8,128)(2,1)}, u32[]{:S(2)}) copy-start(bf16[2,120,768]{2,1,0:T(8,128)(2,1)} %get-tuple-element.145) | copy-start | bytes 1105924
  206.5 10.0 %copy-start.9 = (f32[16,768]{1,0:T(8,128)S(1)}, f32[16,768]{1,0:T(8,128)}, u32[]{:S(2)}) copy-start(f32[16,768]{1,0:T(8,128)} %get-tuple-element.104.vec_ref) | copy-start | bytes 147460
  206.5 10.0 %copy-start.10 = (f32[16,768]{1,0:T(8,128)S(1)}, f32[16,768]{1,0:T(8,128)}, u32[]{:S(2)}) copy-start(f32[16,768]{1,0:T(8,128)} %get-tuple-element.143.gmlp_ref) | copy-start | bytes 147460
  208.0 8.5 %slice-start.4 = ((s8[5111808]{0:T(1024)(128)(4,1)}), s8[4194304]{0:T(1024)(128)(4,1)S(1)}, s32[]{:S(2)}) async-start(s8[5111808]{0:T(1024)(128)(4,1)} %bitcast.101), calls=%async_computation.7 | async-start | bytes 8388608
  209.5 6.9 %slice-start.5 = ((s8[5111808]{0:T(1024)(128)(4,1)}), s8[917504]{0:T(1024)(128)(4,1)S(1)}, s32[]{:S(2)}) async-start(s8[5111808]{0:T(1024)(128)(4,1)} %bitcast.101), calls=%async_computation.8 | async-start | bytes 1835008
  209.6 6.9 %copy-start.7 = (bf16[2,512,768]{2,1,0:T(8,128)(2,1)S(1)}, bf16[2,512,768]{2,1,0:T(8,128)(2,1)}, u32[]{:S(2)}) copy-start(bf16[2,512,768]{2,1,0:T(8,128)(2,1)} %tok_ref.1) | copy-start | bytes 4718596
  209.8 6.7 %copy-start.5 = (bf16[2,512,1152]{2,1,0:T(8,128)(2,1)S(1)}, bf16[2,512,1152]{2,1,0:T(8,128)(2,1)}, u32[]{:S(2)}) copy-start(bf16[2,512,1152]{2,1,0:T(8,128)(2,1)} %copy-done.4) | copy-start | bytes 7077892
  209.9 6.6 %copy-start.3 = (bf16[2,512,1152]{2,1,0:T(8,128)(2,1)S(1)}, bf16[2,512,1152]{2,1,0:T(8,128)(2,1)}, u32[]{:S(2)}) copy-start(bf16[2,512,1152]{2,1,0:T(8,128)(2,1)} %copy-done.2) | copy-start | bytes 7077892
  209.9 6.6 %copy-start.6 = (f32[1,1024]{0,1:T(8,128)S(1)}, f32[1,1024]{0,1:T(8,128)}, u32[]{:S(2)}) copy-start(f32[1,1024]{0,1:T(8,128)} %copy.41) | copy-start | bytes 12292
  210.0 18.3 %collective-permute-start.21 = (bf16[2,288,384]{2,1,0:T(8,128)(2,1)S(1)}, bf16[2,288,384]{2,1,0:T(8,128)(2,1)S(1)}, u32[]{:S(2)}, u32[]{:S(2)}) collective-permute-start(bf16[2,288,384]{2,1,0:T(8,128)(2,1)S(1)} %get-tuple-element.156), channel_id=1, source_target_pairs={{0,2},{1,3},{2,0},{3,1},{4,6},{5,7},{6,4},{7,5},{8,10},{9,11},{10,... | collective-permute-start | bytes 1327112 | tf_op jit(solution)/shard_map/ppermute | solution.py:581
  214.9 13.6 %collective-permute-start.20 = (bf16[2,2,144,384]{3,2,1,0:T(8,128)(2,1)S(1)}, bf16[2,2,144,384]{3,2,1,0:T(8,128)(2,1)S(1)}, u32[]{:S(2)}, u32[]{:S(2)}) collective-permute-start(bf16[2,2,144,384]{3,2,1,0:T(8,128)(2,1)S(1)} %get-tuple-element.154), channel_id=1, source_target_pairs={{0,16},{16,0},{1,17},{17,1},{2,18},{18,2},{3,19},{19,3},{4,20},{20... | collective-permute-start | bytes 1327112 | tf_op jit(solution)/shard_map/ppermute | solution.py:581
  228.7 1.4 collective-permute-start.22
  230.1 4.9 %collective-permute-start.28 = (bf16[4,16,384]{2,1,0:T(8,128)(2,1)S(1)}, bf16[4,16,384]{2,1,0:T(8,128)(2,1)S(1)}, u32[]{:S(2)}, u32[]{:S(2)}) collective-permute-start(bf16[4,16,384]{2,1,0:T(8,128)(2,1)S(1)} %get-tuple-element.177), channel_id=1, source_target_pairs={{0,2},{1,3},{2,0},{3,1},{4,6},{5,7},{6,4},{7,5},{8,10},{9,11},{10,... | collective-permute-start | bytes 147464 | tf_op jit(solution)/shard_map/ppermute | solution.py:686
  231.6 17.3 %collective-permute-start.26 = (bf16[2,144,384]{2,1,0:T(8,128)(2,1)S(1)}, bf16[2,144,384]{2,1,0:T(8,128)(2,1)S(1)}, u32[]{:S(2)}, u32[]{:S(2)}) collective-permute-start(bf16[2,144,384]{2,1,0:T(8,128)(2,1)S(1)} %get-tuple-element.173), channel_id=1, source_target_pairs={{0,2},{1,3},{2,0},{3,1},{4,6},{5,7},{6,4},{7,5},{8,10},{9,11},{10,... | collective-permute-start | bytes 663560 | tf_op jit(solution)/shard_map/ppermute | solution.py:585
  232.2 16.8 %collective-permute-start.27 = (bf16[2,144,384]{2,1,0:T(8,128)(2,1)S(1)}, bf16[2,144,384]{2,1,0:T(8,128)(2,1)S(1)}, u32[]{:S(2)}, u32[]{:S(2)}) collective-permute-start(bf16[2,144,384]{2,1,0:T(8,128)(2,1)S(1)} %get-tuple-element.175), channel_id=1, source_target_pairs={{0,16},{16,0},{1,17},{17,1},{2,18},{18,2},{3,19},{19,3},{4,20},{20... | collective-permute-start | bytes 663560 | tf_op jit(solution)/shard_map/ppermute | solution.py:585
  233.1 9.5 %collective-permute-start.23 = (bf16[120,768]{1,0:T(8,128)(2,1)S(1)}, bf16[120,768]{1,0:T(8,128)(2,1)S(1)}, u32[]{:S(2)}, u32[]{:S(2)}) collective-permute-start(bf16[120,768]{1,0:T(8,128)(2,1)S(1)} %get-tuple-element.169), channel_id=1, source_target_pairs={{0,4},{1,5},{2,6},{3,7},{4,8},{5,9},{6,10},{7,11},{8,12},{9,13},{1... | collective-permute-start | bytes 552968 | tf_op jit(solution)/shard_map/ppermute | solution.py:591
  233.1 15.8 %collective-permute-start.24 = (bf16[120,768]{1,0:T(8,128)(2,1)S(1)}, bf16[120,768]{1,0:T(8,128)(2,1)S(1)}, u32[]{:S(2)}, u32[]{:S(2)}) collective-permute-start(bf16[120,768]{1,0:T(8,128)(2,1)S(1)} %get-tuple-element.170), channel_id=1, source_target_pairs={{0,8},{1,9},{2,10},{3,11},{4,12},{5,13},{6,14},{7,15},{8,0},{9,1},... | collective-permute-start | bytes 552968 | tf_op jit(solution)/shard_map/ppermute | solution.py:591
  235.0 13.9 %collective-permute-start.25 = (bf16[120,768]{1,0:T(8,128)(2,1)S(1)}, bf16[120,768]{1,0:T(8,128)(2,1)S(1)}, u32[]{:S(2)}, u32[]{:S(2)}) collective-permute-start(bf16[120,768]{1,0:T(8,128)(2,1)S(1)} %get-tuple-element.171), channel_id=1, source_target_pairs={{0,12},{1,13},{2,14},{3,15},{4,0},{5,1},{6,2},{7,3},{8,4},{9,5},{1... | collective-permute-start | bytes 552968 | tf_op jit(solution)/shard_map/ppermute | solution.py:591
  249.2 8.0 %collective-permute-start.29 = (bf16[160,384]{1,0:T(8,128)(2,1)S(1)}, bf16[160,384]{1,0:T(8,128)(2,1)S(1)}, u32[]{:S(2)}, u32[]{:S(2)}) collective-permute-start(bf16[160,384]{1,0:T(8,128)(2,1)S(1)} %get-tuple-element.183), channel_id=1, source_target_pairs={{0,4},{1,5},{2,6},{3,7},{4,8},{5,9},{6,10},{7,11},{8,12},{9,13},{1... | collective-permute-start | bytes 368648 | tf_op jit(solution)/shard_map/ppermute | solution.py:591
  252.8 8.6 %collective-permute-start.30 = (bf16[160,384]{1,0:T(8,128)(2,1)S(1)}, bf16[160,384]{1,0:T(8,128)(2,1)S(1)}, u32[]{:S(2)}, u32[]{:S(2)}) collective-permute-start(bf16[160,384]{1,0:T(8,128)(2,1)S(1)} %get-tuple-element.184), channel_id=1, source_target_pairs={{0,8},{1,9},{2,10},{3,11},{4,12},{5,13},{6,14},{7,15},{8,0},{9,1},... | collective-permute-start | bytes 368648 | tf_op jit(solution)/shard_map/ppermute | solution.py:591
  252.8 8.6 %collective-permute-start.31 = (bf16[160,384]{1,0:T(8,128)(2,1)S(1)}, bf16[160,384]{1,0:T(8,128)(2,1)S(1)}, u32[]{:S(2)}, u32[]{:S(2)}) collective-permute-start(bf16[160,384]{1,0:T(8,128)(2,1)S(1)} %get-tuple-element.185), channel_id=1, source_target_pairs={{0,12},{1,13},{2,14},{3,15},{4,0},{5,1},{6,2},{7,3},{8,4},{9,5},{1... | collective-permute-start | bytes 368648 | tf_op jit(solution)/shard_map/ppermute | solution.py:591
  255.2 15.7 %collective-permute-start.34 = (bf16[192,768]{1,0:T(8,128)(2,1)}, bf16[192,768]{1,0:T(8,128)(2,1)S(1)}, u32[]{:S(2)}, u32[]{:S(2)}) collective-permute-start(bf16[192,768]{1,0:T(8,128)(2,1)} %bitcast.118), channel_id=1, source_target_pairs={{0,16},{16,0},{1,17},{17,1},{2,18},{18,2},{3,19},{19,3},{4,20},{20... | collective-permute-start | bytes 884744 | tf_op jit(solution)/shard_map/ppermute | solution.py:691
  256.4 11.7 %collective-permute-start.33 = (bf16[120,768]{1,0:T(8,128)(2,1)S(1)}, bf16[120,768]{1,0:T(8,128)(2,1)S(1)}, u32[]{:S(2)}, u32[]{:S(2)}) collective-permute-start(bf16[120,768]{1,0:T(8,128)(2,1)S(1)} %add_convert_fusion.12), channel_id=1, source_target_pairs={{0,16},{16,0},{1,17},{17,1},{2,18},{18,2},{3,19},{19,3},{4,20},{20... | collective-permute-start | bytes 552968 | tf_op jit(solution)/shard_map/ppermute | solution.py:597
  261.4 8.3 %collective-permute-start.32 = (bf16[160,384]{1,0:T(8,128)(2,1)S(1)}, bf16[160,384]{1,0:T(8,128)(2,1)S(1)}, u32[]{:S(2)}, u32[]{:S(2)}) collective-permute-start(bf16[160,384]{1,0:T(8,128)(2,1)S(1)} %add_convert_fusion.13), channel_id=1, source_target_pairs={{0,16},{16,0},{1,17},{17,1},{2,18},{18,2},{3,19},{19,3},{4,20},{20... | collective-permute-start | bytes 368648 | tf_op jit(solution)/shard_map/ppermute | solution.py:597
  268.1 2.8 %copy-start.18 = (bf16[1,192,768]{2,1,0:T(8,128)(2,1)S(1)}, bf16[1,192,768]{2,1,0:T(8,128)(2,1)}, u32[]{:S(2)}) copy-start(bf16[1,192,768]{2,1,0:T(8,128)(2,1)} %reduce-scatter.2.cloned.1.call-done) | copy-start | bytes 884740
  (5 other events, 5.6 us)
Sparse Core Ops, SparseCore 0:
  10.9 95.4 all-gather.2
  157.3 77.4 reduce-scatter.1

commit v4 on v2

--- a/solution.py
+++ b/solution.py
@@ -423,7 +423,7 @@
             jax.ShapeDtypeStruct((BLOCKS // 2, 144, wide), BF),
             jax.ShapeDtypeStruct((BLOCKS // 2, 144, wide), BF),
         ],
-        compiler_params=pltpu.CompilerParams(vmem_limit_bytes=32 * 2**20),
+        compiler_params=pltpu.CompilerParams(vmem_limit_bytes=28 * 2**20),
         cost_estimate=pl.CostEstimate(flops=10**8, bytes_accessed=2**20, transcendentals=0),
         name="attention_backward",
     )(group_id, place, qkv, qkv, qkv, lse, gb, w1, normed)

time: 286 us -> 286 us (level)
  no operation moved by 1% of the time
where the time goes in v4:
time: 286 us; the launch traced here: 281 us
  Pallas kernels  118 us (41%)
  waiting for transfers between devices  87.2 us (30%)
  starting transfers between devices  37.9 us (13%)
  between operations  15 us (5%)
  local copies, waits for them, and re-layouts  13.2 us (5%)
  other arithmetic  9.72 us (3%)
    pallas_call x1, Pallas kernels, mlp_call(): pl.pallas_call(mlp_kernel, grid_spec=pltpu.PrefetchScalarGridSpec(num_sca...  50 us
    pallas_call x2, Pallas kernels, attention_back_call(): pl.pallas_call(functools.partial(attention_back_kernel, part), grid_spec=...  30.4 us
    pallas_call x1, Pallas kernels, forward_call(): pl.pallas_call(functools.partial(forward_kernel, len(pieces)), grid_spec=...  25.7 us
    all_gather x1, waiting for transfers between devices, local(): w2 = lax.all_gather(pack2, 'fsdp', axis=0)  22.1 us
    ppermute x6, waiting for transfers between devices, scatter_steps(): got = [lax.ppermute(sent[k], 'fsdp', turn(k)) for k in (1, 2, 3)]  21.2 us
    ppermute x1, waiting for transfers between devices, gather_pieces(): by_x = lax.ppermute(along_z, 'rep', REP)  12.2 us
    ppermute x3, waiting for transfers between devices, gather_pieces(): lax.ppermute(half, 'fsdp', turn(k))  10.9 us
    pallas_call x1, Pallas kernels, norm_one_call(): pl.pallas_call(norm_one_kernel, grid_spec=pltpu.PrefetchScalarGridSpec(nu...  8.99 us
  transfers between devices with their start and end apart: 36, of which 15 were waited for; matrix products, arithmetic and copies ran while one was open for 6% of the time, Pallas kernels for 23%

profile of v4, /device:TPU:0, one launch (start us, length us, event | category | flops | bytes accessed | tf_op | source)
XLA Modules:
  0.0 280.6 jit_solution(16145859965913430569)
XLA Ops:
  7.2 2.5 pack.1
  9.8 0.9 constant_dynamic-slice_fusion.8
  10.8 3.1 %collective-permute-start = (bf16[208,384]{1,0:T(8,128)(2,1)S(1)}, bf16[208,384]{1,0:T(8,128)(2,1)S(1)}, u32[]{:S(2)}, u32[]{:S(2)}) collective-permute-start(bf16[208,384]{1,0:T(8,128)(2,1)S(1)} %constant_dynamic-slice_fusion.8), channel_id=1, source_target_pairs={{0,4},{1,5},{2,6},{3,7},{4,8},{5,9},{6,10},{7,11},{8,12},{9,13},{1... | collective-permute-start | bytes 479240 | tf_op jit(solution)/shard_map/ppermute | solution.py:546
  13.8 2.6 collective-permute-start.1
  16.4 1.3 collective-permute-start.2
  17.8 0.9 fusion.15
  18.7 2.2 collective-permute-done
  20.9 8.7 %collective-permute-done.1 = bf16[208,384]{1,0:T(8,128)(2,1)S(1)} collective-permute-done((bf16[208,384]{1,0:T(8,128)(2,1)S(1)}, bf16[208,384]{1,0:T(8,128)(2,1)S(1)}, u32[]{:S(2)}, u32[]{:S(2)}) %collective-permute-start.1) | collective-permute-done | bytes 159776 | tf_op jit(solution)/shard_map/ppermute | solution.py:546
  29.7 1.6 collective-permute-start.3
  31.3 1.6 collective-permute-start.4
  32.8 12.2 %collective-permute-done.3.refs_1_ = bf16[4,208,384]{2,1,0:T(8,128)(2,1)S(1)} collective-permute-done((bf16[4,208,384]{2,1,0:T(8,128)(2,1)S(1)}, bf16[4,208,384]{2,1,0:T(8,128)(2,1)S(1)}, u32[]{:S(2)}, u32[]{:S(2)}) %collective-permute-start.3) | collective-permute-done | bytes 639008 | tf_op jit(solution)/shard_map/ppermute | solution.py:547
  45.1 1.6 collective-permute-start.5
  46.7 1.6 collective-permute-start.6
  49.0 4.1 %collective-permute-done.5.refs_3_ = bf16[2,208,384]{2,1,0:T(8,128)(2,1)S(1)} collective-permute-done((bf16[2,208,384]{2,1,0:T(8,128)(2,1)S(1)}, bf16[2,208,384]{2,1,0:T(8,128)(2,1)S(1)}, u32[]{:S(2)}, u32[]{:S(2)}) %collective-permute-start.5) | collective-permute-done | bytes 319520 | tf_op jit(solution)/shard_map/ppermute | solution.py:549
  53.1 1.1 collective-permute-done.6.refs_4_
  54.3 1.1 copy.37.mask_ref
  55.3 1.0 copy.41
  56.4 0.6 pad_add_fusion.place_ref
  57.0 0.8 copy-done.22
  57.8 0.7 copy-done.24
  58.5 25.7 %attention_forward.1 = (bf16[2,512,768]{2,1,0:T(8,128)(2,1)}, bf16[2,512,2304]{2,1,0:T(8,128)(2,1)}, bf16[2,512,768]{2,1,0:T(8,128)(2,1)}, f32[2,12,512]{2,1,0:T...) custom-call(s32[2]{0:T(128)} %group_ref.7, s32[4]{0:T(128)} %pad_add_fusion.place_ref, ...), custom_call_target="tpu_custom_call" | custom-call | flops 8999999488 | bytes 16777216 | tf_op jit(solution)/shard_map/attention_forward/pallas_call | solution.py:190
  84.2 22.1 %all-gather.3.cloned.1.call-done = bf16[6144,768]{1,0:T(8,128)(2,1)} async-done(((bf16[384,768]{1,0:T(8,128)(2,1)}), bf16[6144,768]{1,0:T(8,128)(2,1)}) %all-gather.3.cloned.1.call-update) | async-done | bytes 9437200 | tf_op jit(solution)/shard_map/all_gather | solution.py:631
  106.3 50.0 %mlp.1 = (bf16[1024,768]{1,0:T(8,128)(2,1)}, bf16[1024,768]{1,0:T(8,128)(2,1)}, bf16[16,240,768]{2,1,0:T(8,128)(2,1)}, bf16[8,192,768]{2,1,0:T(8,128)(2,1)}, bf1...) custom-call(s32[2]{0:T(128)} %group_ref.7, s32[4]{0:T(128)} %pad_add_fusion.place_ref, bf16[1024,768]{1,0:T(8,128)(2,1)} %bitcast.112, ...), custom_call_target="tpu_custom_call" | custom-call | flops 44999999488 | bytes 31457280 | tf_op jit(solution)/shard_map/mlp/pallas_call | solution.py:300
  156.8 4.6 %collective-permute-done.12 = bf16[8,192,768]{2,1,0:T(8,128)(2,1)} collective-permute-done((bf16[8,192,768]{2,1,0:T(8,128)(2,1)}, bf16[8,192,768]{2,1,0:T(8,128)(2,1)}, u32[]{:S(2)}, u32[]{:S(2)}) %collective-permute-start.12) | collective-permute-done | bytes 2359328 | tf_op jit(solution)/shard_map/ppermute | solution.py:569
  161.3 2.5 add_convert_fusion
  164.3 1.4 collective-permute-start.14
  165.7 1.1 collective-permute-start.13
  166.8 0.6 copy-done.1
  167.4 0.6 copy-done
  168.0 15.1 %attention_backward.2 = (bf16[2,512,1152]{2,1,0:T(8,128)(2,1)S(1)}, bf16[8,144,384]{2,1,0:T(8,128)(2,1)S(1)}, bf16[8,144,384]{2,1,0:T(8,128)(2,1)}) custom-call(s32[2]{0:T(128)S(1)} %copy-done.12, s32[4]{0:T(128)S(1)} %copy-done.11, bf16[2,512,2304]{2,1,0:T(8,128)(2,1)S(1)} %bitcast.99, bf16[2,512,2304]{2,1,0:T(8,128)(2,1)S(1)} %bitcast.99, ...), custom_call_target="tpu_custom_call" | custom-call | flops 100000000 | bytes 1048576 | tf_op jit(solution)/shard_map/attention_backward/pallas_call | solution.py:404
  183.3 1.2 constant_dynamic-slice_fusion.4
  184.8 0.8 dynamic-slice_bitcast_fusion.4
  185.7 15.3 %attention_backward.3 = (bf16[2,512,1152]{2,1,0:T(8,128)(2,1)S(1)}, bf16[8,144,384]{2,1,0:T(8,128)(2,1)S(1)}, bf16[8,144,384]{2,1,0:T(8,128)(2,1)}) custom-call(s32[2]{0:T(128)S(1)} %copy-done.12, s32[4]{0:T(128)S(1)} %copy-done.11, bf16[2,512,2304]{2,1,0:T(8,128)(2,1)S(1)} %bitcast.99, bf16[2,512,2304]{2,1,0:T(8,128)(2,1)S(1)} %bitcast.99, ...), custom_call_target="tpu_custom_call" | custom-call | flops 100000000 | bytes 1048576 | tf_op jit(solution)/shard_map/attention_backward/pallas_call | solution.py:404
  201.0 1.4 copy-done.4
  202.9 0.9 collective-permute-start.18
  203.8 1.5 collective-permute-start.17
  205.3 1.6 add_convert_fusion.2
  207.0 1.5 add_convert_fusion.1
  209.0 1.0 collective-permute-start.20
  210.0 2.2 collective-permute-done.18
  212.3 1.2 collective-permute-done.17
  213.6 1.5 collective-permute-start.19
  215.4 9.0 %norm_one_backward.1 = (bf16[1024,768]{1,0:T(8,128)(2,1)}, bf16[8,16,384]{2,1,0:T(8,128)(2,1)S(1)}, bf16[8,16,384]{2,1,0:T(8,128)(2,1)S(1)}) custom-call(s32[4]{0:T(128)S(1)} %copy-done.11, bf16[1024,768]{1,0:T(8,128)(2,1)S(1)} %bitcast.113, f32[1024,1]{1,0:T(8,128)S(1)} %bitcast.111, bf16[1024,768]{1,0:T(8,128)(2,1)S(1)} %copy-done, ...), custom_call_target="tpu_custom_call" | custom-call | flops 100000000 | bytes 1048576 | tf_op jit(solution)/shard_map/norm_one_backward/pallas_call | solution.py:483
  224.9 1.2 collective-permute-start.24
  226.1 1.3 collective-permute-start.25
  227.4 1.4 collective-permute-start.22
  228.8 2.5 collective-permute-start.23
  231.3 7.4 %collective-permute-done.21 = bf16[96,768]{1,0:T(8,128)(2,1)S(1)} collective-permute-done((bf16[96,768]{1,0:T(8,128)(2,1)S(1)}, bf16[96,768]{1,0:T(8,128)(2,1)S(1)}, u32[]{:S(2)}, u32[]{:S(2)}) %collective-permute-start.21) | collective-permute-done | bytes 147488 | tf_op jit(solution)/shard_map/ppermute | solution.py:586
  238.7 0.8 collective-permute-start.27
  239.5 8.5 %collective-permute-done.22 = bf16[96,768]{1,0:T(8,128)(2,1)S(1)} collective-permute-done((bf16[96,768]{1,0:T(8,128)(2,1)S(1)}, bf16[96,768]{1,0:T(8,128)(2,1)S(1)}, u32[]{:S(2)}, u32[]{:S(2)}) %collective-permute-start.22) | collective-permute-done | bytes 147488 | tf_op jit(solution)/shard_map/ppermute | solution.py:586
  248.4 1.9 reduce-scatter.2.cloned.1.call-done
  250.3 2.2 collective-permute-start.28
  252.6 0.7 collective-permute-start.29
  253.2 1.8 collective-permute-start.30
  255.0 1.1 collective-permute-start.33
  256.1 0.9 collective-permute-start.32
  257.0 1.4 collective-permute-done.28
  258.4 3.9 %collective-permute-done.29 = bf16[160,384]{1,0:T(8,128)(2,1)S(1)} collective-permute-done((bf16[160,384]{1,0:T(8,128)(2,1)S(1)}, bf16[160,384]{1,0:T(8,128)(2,1)S(1)}, u32[]{:S(2)}, u32[]{:S(2)}) %collective-permute-start.29) | collective-permute-done | bytes 122912 | tf_op jit(solution)/shard_map/ppermute | solution.py:586
  262.5 1.7 collective-permute-start.31
  264.2 0.9 fusion.2
  265.1 5.5 %collective-permute-done.31 = bf16[160,384]{1,0:T(8,128)(2,1)S(1)} collective-permute-done((bf16[160,384]{1,0:T(8,128)(2,1)S(1)}, bf16[160,384]{1,0:T(8,128)(2,1)S(1)}, u32[]{:S(2)}, u32[]{:S(2)}) %collective-permute-start.31) | collective-permute-done | bytes 122912 | tf_op jit(solution)/shard_map/ppermute | solution.py:592
  270.6 0.6 slice.169
  272.0 0.7 fusion.14
  272.7 0.9 pad_maximum_fusion.2
  (137 shorter events, 5.3 us)
Async XLA Ops:
  7.2 99.2 %all-gather.3.cloned.1.call-start = ((), (), s32[]{:S(2)}) async-start(), calls=%async_computation.2 | async-start | bytes 10027008 | tf_op jit(solution)/shard_map/all_gather | solution.py:631
  9.8 39.1 %copy-start.21 = (s32[2,128]{1,0:T(2,128)S(1)}, s32[2,128]{1,0:T(2,128)}, u32[]{:S(2)}) copy-start(s32[2,128]{1,0:T(2,128)} %param.19) | copy-start | bytes 3076
  9.8 240.6 %reduce-scatter.2.cloned.1.call-start = ((), (), s32[]{:S(2)}) async-start(), calls=%async_computation.1 | async-start | bytes 6266880 | tf_op jit(solution)/shard_map/reduce_scatter | solution.py:683
  10.8 10.1 %collective-permute-start = (bf16[208,384]{1,0:T(8,128)(2,1)S(1)}, bf16[208,384]{1,0:T(8,128)(2,1)S(1)}, u32[]{:S(2)}, u32[]{:S(2)}) collective-permute-start(bf16[208,384]{1,0:T(8,128)(2,1)S(1)} %constant_dynamic-slice_fusion.8), channel_id=1, source_target_pairs={{0,4},{1,5},{2,6},{3,7},{4,8},{5,9},{6,10},{7,11},{8,12},{9,13},{1... | collective-permute-start | bytes 479240 | tf_op jit(solution)/shard_map/ppermute | solution.py:546
  13.8 15.7 %collective-permute-start.1 = (bf16[208,384]{1,0:T(8,128)(2,1)S(1)}, bf16[208,384]{1,0:T(8,128)(2,1)S(1)}, u32[]{:S(2)}, u32[]{:S(2)}) collective-permute-start(bf16[208,384]{1,0:T(8,128)(2,1)S(1)} %constant_dynamic-slice_fusion.8), channel_id=1, source_target_pairs={{0,8},{1,9},{2,10},{3,11},{4,12},{5,13},{6,14},{7,15},{8,0},{9,1},... | collective-permute-start | bytes 479240 | tf_op jit(solution)/shard_map/ppermute | solution.py:546
  16.4 13.2 %collective-permute-start.2 = (bf16[208,384]{1,0:T(8,128)(2,1)S(1)}, bf16[208,384]{1,0:T(8,128)(2,1)S(1)}, u32[]{:S(2)}, u32[]{:S(2)}) collective-permute-start(bf16[208,384]{1,0:T(8,128)(2,1)S(1)} %constant_dynamic-slice_fusion.8), channel_id=1, source_target_pairs={{0,12},{1,13},{2,14},{3,15},{4,0},{5,1},{6,2},{7,3},{8,4},{9,5},{1... | collective-permute-start | bytes 479240 | tf_op jit(solution)/shard_map/ppermute | solution.py:546
  29.7 27.3 %copy-start.16 = (bf16[4,208,384]{2,1,0:T(8,128)(2,1)}, bf16[4,208,384]{2,1,0:T(8,128)(2,1)S(1)}, u32[]{:S(2)}) copy-start(bf16[4,208,384]{2,1,0:T(8,128)(2,1)S(1)} %pad_maximum_fusion.1.refs_0_) | copy-start | bytes 1916932
  29.7 15.3 %collective-permute-start.3 = (bf16[4,208,384]{2,1,0:T(8,128)(2,1)S(1)}, bf16[4,208,384]{2,1,0:T(8,128)(2,1)S(1)}, u32[]{:S(2)}, u32[]{:S(2)}) collective-permute-start(bf16[4,208,384]{2,1,0:T(8,128)(2,1)S(1)} %pad_maximum_fusion.1.refs_0_), channel_id=1, source_target_pairs={{0,16},{16,0},{1,17},{17,1},{2,18},{18,2},{3,19},{19,3},{4,20},{20... | collective-permute-start | bytes 1916936 | tf_op jit(solution)/shard_map/ppermute | solution.py:547
  31.3 15.4 %collective-permute-start.4 = (bf16[4,208,384]{2,1,0:T(8,128)(2,1)S(1)}, bf16[4,208,384]{2,1,0:T(8,128)(2,1)S(1)}, u32[]{:S(2)}, u32[]{:S(2)}) collective-permute-start(bf16[4,208,384]{2,1,0:T(8,128)(2,1)S(1)} %pad_maximum_fusion.1.refs_0_), channel_id=1, source_target_pairs={{0,2},{1,3},{2,0},{3,1},{4,6},{5,7},{6,4},{7,5},{8,10},{9,11},{10,... | collective-permute-start | bytes 1916936 | tf_op jit(solution)/shard_map/ppermute | solution.py:548
  45.0 12.0 %copy-start.18 = (bf16[4,208,384]{2,1,0:T(8,128)(2,1)}, bf16[4,208,384]{2,1,0:T(8,128)(2,1)S(1)}, u32[]{:S(2)}) copy-start(bf16[4,208,384]{2,1,0:T(8,128)(2,1)S(1)} %collective-permute-done.3.refs_1_) | copy-start | bytes 1916932
  45.1 8.0 %collective-permute-start.5 = (bf16[2,208,384]{2,1,0:T(8,128)(2,1)S(1)}, bf16[2,208,384]{2,1,0:T(8,128)(2,1)S(1)}, u32[]{:S(2)}, u32[]{:S(2)}) collective-permute-start(bf16[2,208,384]{2,1,0:T(8,128)(2,1)S(1)} %slice.145), channel_id=1, source_target_pairs={{0,2},{1,3},{2,0},{3,1},{4,6},{5,7},{6,4},{7,5},{8,10},{9,11},{10,... | collective-permute-start | bytes 958472 | tf_op jit(solution)/shard_map/ppermute | solution.py:549
  46.7 10.3 %copy-start.19 = (bf16[4,208,384]{2,1,0:T(8,128)(2,1)}, bf16[4,208,384]{2,1,0:T(8,128)(2,1)S(1)}, u32[]{:S(2)}) copy-start(bf16[4,208,384]{2,1,0:T(8,128)(2,1)S(1)} %collective-permute-done.4.refs_2_) | copy-start | bytes 1916932
  46.7 7.5 %collective-permute-start.6 = (bf16[2,208,384]{2,1,0:T(8,128)(2,1)S(1)}, bf16[2,208,384]{2,1,0:T(8,128)(2,1)}, u32[]{:S(2)}, u32[]{:S(2)}) collective-permute-start(bf16[2,208,384]{2,1,0:T(8,128)(2,1)S(1)} %slice.146), channel_id=1, source_target_pairs={{0,16},{16,0},{1,17},{17,1},{2,18},{18,2},{3,19},{19,3},{4,20},{20... | collective-permute-start | bytes 958472 | tf_op jit(solution)/shard_map/ppermute | solution.py:550
  48.3 8.6 %collective-permute-start.7 = (bf16[4,208,384]{2,1,0:T(8,128)(2,1)S(1)}, bf16[4,208,384]{2,1,0:T(8,128)(2,1)S(1)}, u32[]{:S(2)}, u32[]{:S(2)}) collective-permute-start(bf16[4,208,384]{2,1,0:T(8,128)(2,1)S(1)} %pad_maximum_fusion.1.refs_0_), channel_id=1, source_target_pairs={{0,1},{1,0},{2,3},{3,2},{4,5},{5,4},{6,7},{7,6},{8,9},{9,8},{10,11... | collective-permute-start | bytes 1916936 | tf_op jit(solution)/shard_map/ppermute | solution.py:552
  48.3 8.6 %collective-permute-start.8 = (bf16[4,208,384]{2,1,0:T(8,128)(2,1)S(1)}, bf16[4,208,384]{2,1,0:T(8,128)(2,1)}, u32[]{:S(2)}, u32[]{:S(2)}) collective-permute-start(bf16[4,208,384]{2,1,0:T(8,128)(2,1)S(1)} %collective-permute-done.3.refs_1_), channel_id=1, source_target_pairs={{0,1},{1,0},{2,3},{3,2},{4,5},{5,4},{6,7},{7,6},{8,9},{9,8},{10,11... | collective-permute-start | bytes 1916936 | tf_op jit(solution)/shard_map/ppermute | solution.py:552
  48.8 8.1 %collective-permute-start.9 = (bf16[4,208,384]{2,1,0:T(8,128)(2,1)S(1)}, bf16[4,208,384]{2,1,0:T(8,128)(2,1)}, u32[]{:S(2)}, u32[]{:S(2)}) collective-permute-start(bf16[4,208,384]{2,1,0:T(8,128)(2,1)S(1)} %collective-permute-done.4.refs_2_), channel_id=1, source_target_pairs={{0,1},{1,0},{2,3},{3,2},{4,5},{5,4},{6,7},{7,6},{8,9},{9,8},{10,11... | collective-permute-start | bytes 1916936 | tf_op jit(solution)/shard_map/ppermute | solution.py:552
  53.1 3.9 %copy-start.23 = (bf16[2,208,384]{2,1,0:T(8,128)(2,1)}, bf16[2,208,384]{2,1,0:T(8,128)(2,1)S(1)}, u32[]{:S(2)}) copy-start(bf16[2,208,384]{2,1,0:T(8,128)(2,1)S(1)} %collective-permute-done.5.refs_3_) | copy-start | bytes 958468
  53.1 3.9 %collective-permute-start.10 = (bf16[2,208,384]{2,1,0:T(8,128)(2,1)S(1)}, bf16[2,208,384]{2,1,0:T(8,128)(2,1)}, u32[]{:S(2)}, u32[]{:S(2)}) collective-permute-start(bf16[2,208,384]{2,1,0:T(8,128)(2,1)S(1)} %collective-permute-done.5.refs_3_), channel_id=1, source_target_pairs={{0,1},{1,0},{2,3},{3,2},{4,5},{5,4},{6,7},{7,6},{8,9},{9,8},{10,11... | collective-permute-start | bytes 958472 | tf_op jit(solution)/shard_map/ppermute | solution.py:552
  54.2 2.8 collective-permute-start.11
  156.4 4.9 %collective-permute-start.12 = (bf16[8,192,768]{2,1,0:T(8,128)(2,1)}, bf16[8,192,768]{2,1,0:T(8,128)(2,1)}, u32[]{:S(2)}, u32[]{:S(2)}) collective-permute-start(bf16[8,192,768]{2,1,0:T(8,128)(2,1)} %get-tuple-element.102), channel_id=1, source_target_pairs={{0,1},{1,0},{2,3},{3,2},{4,5},{5,4},{6,7},{7,6},{8,9},{9,8},{10,11... | collective-permute-start | bytes 7077896 | tf_op jit(solution)/shard_map/ppermute | solution.py:569
  156.7 4.6 %copy-start.13 = (bf16[8,192,768]{2,1,0:T(8,128)(2,1)S(1)}, bf16[8,192,768]{2,1,0:T(8,128)(2,1)}, u32[]{:S(2)}) copy-start(bf16[8,192,768]{2,1,0:T(8,128)(2,1)} %get-tuple-element.101) | copy-start | bytes 7077892
  161.3 5.4 %slice-start = ((s8[4718592]{0:T(1024)(128)(4,1)}), s8[4194304]{0:T(1024)(128)(4,1)S(1)}, s32[]{:S(2)}) async-start(s8[4718592]{0:T(1024)(128)(4,1)} %bitcast.98), calls=%async_computation.3 | async-start | bytes 8388608
  161.3 5.4 %slice-start.2 = ((s8[5111808]{0:T(1024)(128)(4,1)}), s8[4194304]{0:T(1024)(128)(4,1)S(1)}, s32[]{:S(2)}) async-start(s8[5111808]{0:T(1024)(128)(4,1)} %bitcast.100), calls=%async_computation.5 | async-start | bytes 8388608
  163.8 2.9 %slice-start.1 = ((s8[4718592]{0:T(1024)(128)(4,1)}), s8[524288]{0:T(1024)(128)(4,1)S(1)}, s32[]{:S(2)}) async-start(s8[4718592]{0:T(1024)(128)(4,1)} %bitcast.98), calls=%async_computation.4 | async-start | bytes 1048576
  163.9 3.0 %slice-start.3 = ((s8[5111808]{0:T(1024)(128)(4,1)}), s8[917504]{0:T(1024)(128)(4,1)S(1)}, s32[]{:S(2)}) async-start(s8[5111808]{0:T(1024)(128)(4,1)} %bitcast.100), calls=%async_computation.6 | async-start | bytes 1835008
  164.0 3.4 %copy-start.1 = (bf16[2,512,768]{2,1,0:T(8,128)(2,1)S(1)}, bf16[2,512,768]{2,1,0:T(8,128)(2,1)}, u32[]{:S(2)}) copy-start(bf16[2,512,768]{2,1,0:T(8,128)(2,1)} %get-tuple-element.104) | copy-start | bytes 4718596
  164.1 3.8 %copy-start = (bf16[1024,768]{1,0:T(8,128)(2,1)S(1)}, bf16[1024,768]{1,0:T(8,128)(2,1)}, u32[]{:S(2)}) copy-start(bf16[1024,768]{1,0:T(8,128)(2,1)} %get-tuple-element.98.gb_ref) | copy-start | bytes 4718596
  164.1 3.8 %copy-start.8 = (f32[2,12,512]{2,1,0:T(8,128)S(1)}, f32[2,12,512]{2,1,0:T(8,128)}, u32[]{:S(2)}) copy-start(f32[2,12,512]{2,1,0:T(8,128)} %get-tuple-element.100.lse_ref) | copy-start | bytes 147460
  164.2 3.8 %copy-start.11 = (s32[4]{0:T(128)S(1)}, s32[4]{0:T(128)}, u32[]{:S(2)}) copy-start(s32[4]{0:T(128)} %pad_add_fusion.place_ref) | copy-start | bytes 52
  164.2 3.8 %copy-start.12 = (s32[2]{0:T(128)S(1)}, s32[2]{0:T(128)}, u32[]{:S(2)}) copy-start(s32[2]{0:T(128)} %group_ref.7) | copy-start | bytes 28
  164.3 18.8 %collective-permute-start.14 = (bf16[2,192,768]{2,1,0:T(8,128)(2,1)S(1)}, bf16[2,192,768]{2,1,0:T(8,128)(2,1)S(1)}, u32[]{:S(2)}, u32[]{:S(2)}) collective-permute-start(bf16[2,192,768]{2,1,0:T(8,128)(2,1)S(1)} %get-tuple-element.113), channel_id=1, source_target_pairs={{0,2},{1,3},{2,0},{3,1},{4,6},{5,7},{6,4},{7,5},{8,10},{9,11},{10,... | collective-permute-start | bytes 1769480 | tf_op jit(solution)/shard_map/ppermute | solution.py:576
  165.7 18.7 %collective-permute-start.13 = (bf16[2,2,96,768]{3,2,1,0:T(8,128)(2,1)S(1)}, bf16[2,2,96,768]{3,2,1,0:T(8,128)(2,1)S(1)}, u32[]{:S(2)}, u32[]{:S(2)}) collective-permute-start(bf16[2,2,96,768]{3,2,1,0:T(8,128)(2,1)S(1)} %get-tuple-element.111), channel_id=1, source_target_pairs={{0,16},{16,0},{1,17},{17,1},{2,18},{18,2},{3,19},{19,3},{4,20},{20... | collective-permute-start | bytes 1769480 | tf_op jit(solution)/shard_map/ppermute | solution.py:576
  183.1 1.7 copy-start.2
  202.4 3.0 %collective-permute-start.15 = (bf16[8,144,384]{2,1,0:T(8,128)(2,1)}, bf16[8,144,384]{2,1,0:T(8,128)(2,1)}, u32[]{:S(2)}, u32[]{:S(2)}) collective-permute-start(bf16[8,144,384]{2,1,0:T(8,128)(2,1)} %get-tuple-element.125), channel_id=1, source_target_pairs={{0,1},{1,0},{2,3},{3,2},{4,5},{5,4},{6,7},{7,6},{8,9},{9,8},{10,11... | collective-permute-start | bytes 2654216 | tf_op jit(solution)/shard_map/ppermute | solution.py:569
  202.6 4.3 %collective-permute-start.16 = (bf16[8,144,384]{2,1,0:T(8,128)(2,1)}, bf16[8,144,384]{2,1,0:T(8,128)(2,1)}, u32[]{:S(2)}, u32[]{:S(2)}) collective-permute-start(bf16[8,144,384]{2,1,0:T(8,128)(2,1)} %get-tuple-element.127), channel_id=1, source_target_pairs={{0,1},{1,0},{2,3},{3,2},{4,5},{5,4},{6,7},{7,6},{8,9},{9,8},{10,11... | collective-permute-start | bytes 2654216 | tf_op jit(solution)/shard_map/ppermute | solution.py:569
  202.9 9.4 %collective-permute-start.18 = (bf16[2,96,768]{2,1,0:T(8,128)(2,1)}, bf16[2,96,768]{2,1,0:T(8,128)(2,1)S(1)}, u32[]{:S(2)}, u32[]{:S(2)}) collective-permute-start(bf16[2,96,768]{2,1,0:T(8,128)(2,1)} %get-tuple-element.134), channel_id=1, source_target_pairs={{0,16},{16,0},{1,17},{17,1},{2,18},{18,2},{3,19},{19,3},{4,20},{20... | collective-permute-start | bytes 884744 | tf_op jit(solution)/shard_map/ppermute | solution.py:580
  203.8 9.7 %collective-permute-start.17 = (bf16[2,96,768]{2,1,0:T(8,128)(2,1)}, bf16[2,96,768]{2,1,0:T(8,128)(2,1)S(1)}, u32[]{:S(2)}, u32[]{:S(2)}) collective-permute-start(bf16[2,96,768]{2,1,0:T(8,128)(2,1)} %get-tuple-element.132), channel_id=1, source_target_pairs={{0,2},{1,3},{2,0},{3,1},{4,6},{5,7},{6,4},{7,5},{8,10},{9,11},{10,... | collective-permute-start | bytes 884744 | tf_op jit(solution)/shard_map/ppermute | solution.py:580
  205.3 10.0 %slice-start.4 = ((s8[5111808]{0:T(1024)(128)(4,1)}), s8[4194304]{0:T(1024)(128)(4,1)S(1)}, s32[]{:S(2)}) async-start(s8[5111808]{0:T(1024)(128)(4,1)} %bitcast.102), calls=%async_computation.7 | async-start | bytes 8388608
  208.4 6.9 %slice-start.5 = ((s8[5111808]{0:T(1024)(128)(4,1)}), s8[917504]{0:T(1024)(128)(4,1)S(1)}, s32[]{:S(2)}) async-start(s8[5111808]{0:T(1024)(128)(4,1)} %bitcast.102), calls=%async_computation.8 | async-start | bytes 1835008
  208.5 6.9 %copy-start.7 = (bf16[2,512,768]{2,1,0:T(8,128)(2,1)S(1)}, bf16[2,512,768]{2,1,0:T(8,128)(2,1)}, u32[]{:S(2)}) copy-start(bf16[2,512,768]{2,1,0:T(8,128)(2,1)} %tok_ref.1) | copy-start | bytes 4718596
  208.7 3.6 %copy-start.14 = (bf16[2,96,768]{2,1,0:T(8,128)(2,1)S(1)}, bf16[2,96,768]{2,1,0:T(8,128)(2,1)}, u32[]{:S(2)}) copy-start(bf16[2,96,768]{2,1,0:T(8,128)(2,1)} %get-tuple-element.133) | copy-start | bytes 884740
  208.7 4.9 %copy-start.15 = (bf16[2,96,768]{2,1,0:T(8,128)(2,1)S(1)}, bf16[2,96,768]{2,1,0:T(8,128)(2,1)}, u32[]{:S(2)}) copy-start(bf16[2,96,768]{2,1,0:T(8,128)(2,1)} %get-tuple-element.131) | copy-start | bytes 884740
  208.7 6.7 %copy-start.6 = (f32[1,1024]{0,1:T(8,128)S(1)}, f32[1,1024]{0,1:T(8,128)}, u32[]{:S(2)}) copy-start(f32[1,1024]{0,1:T(8,128)} %copy.41) | copy-start | bytes 12292
  208.7 6.7 %copy-start.9 = (f32[16,768]{1,0:T(8,128)S(1)}, f32[16,768]{1,0:T(8,128)}, u32[]{:S(2)}) copy-start(f32[16,768]{1,0:T(8,128)} %get-tuple-element.94.vec_ref) | copy-start | bytes 147460
  208.7 6.7 %copy-start.10 = (f32[16,768]{1,0:T(8,128)S(1)}, f32[16,768]{1,0:T(8,128)}, u32[]{:S(2)}) copy-start(f32[16,768]{1,0:T(8,128)} %get-tuple-element.129.gmlp_ref) | copy-start | bytes 147460
  208.8 6.6 %copy-start.5 = (bf16[2,512,1152]{2,1,0:T(8,128)(2,1)S(1)}, bf16[2,512,1152]{2,1,0:T(8,128)(2,1)}, u32[]{:S(2)}) copy-start(bf16[2,512,1152]{2,1,0:T(8,128)(2,1)} %copy-done.4) | copy-start | bytes 7077892
  209.0 6.5 %copy-start.3 = (bf16[2,512,1152]{2,1,0:T(8,128)(2,1)S(1)}, bf16[2,512,1152]{2,1,0:T(8,128)(2,1)}, u32[]{:S(2)}) copy-start(bf16[2,512,1152]{2,1,0:T(8,128)(2,1)} %copy-done.2) | copy-start | bytes 7077892
  209.0 15.5 %collective-permute-start.20 = (bf16[2,288,384]{2,1,0:T(8,128)(2,1)S(1)}, bf16[2,288,384]{2,1,0:T(8,128)(2,1)S(1)}, u32[]{:S(2)}, u32[]{:S(2)}) collective-permute-start(bf16[2,288,384]{2,1,0:T(8,128)(2,1)S(1)} %get-tuple-element.142), channel_id=1, source_target_pairs={{0,2},{1,3},{2,0},{3,1},{4,6},{5,7},{6,4},{7,5},{8,10},{9,11},{10,... | collective-permute-start | bytes 1327112 | tf_op jit(solution)/shard_map/ppermute | solution.py:576
  213.6 11.0 %collective-permute-start.19 = (bf16[2,2,144,384]{3,2,1,0:T(8,128)(2,1)S(1)}, bf16[2,2,144,384]{3,2,1,0:T(8,128)(2,1)S(1)}, u32[]{:S(2)}, u32[]{:S(2)}) collective-permute-start(bf16[2,2,144,384]{3,2,1,0:T(8,128)(2,1)S(1)} %get-tuple-element.140), channel_id=1, source_target_pairs={{0,16},{16,0},{1,17},{17,1},{2,18},{18,2},{3,19},{19,3},{4,20},{20... | collective-permute-start | bytes 1327112 | tf_op jit(solution)/shard_map/ppermute | solution.py:576
  224.8 4.0 %collective-permute-start.26 = (bf16[8,16,384]{2,1,0:T(8,128)(2,1)S(1)}, bf16[8,16,384]{2,1,0:T(8,128)(2,1)S(1)}, u32[]{:S(2)}, u32[]{:S(2)}) collective-permute-start(bf16[8,16,384]{2,1,0:T(8,128)(2,1)S(1)} %get-tuple-element.157), channel_id=1, source_target_pairs={{0,1},{1,0},{2,3},{3,2},{4,5},{5,4},{6,7},{7,6},{8,9},{9,8},{10,11... | collective-permute-start | bytes 294920 | tf_op jit(solution)/shard_map/ppermute | solution.py:679
  224.9 23.3 %collective-permute-start.24 = (bf16[2,144,384]{2,1,0:T(8,128)(2,1)S(1)}, bf16[2,144,384]{2,1,0:T(8,128)(2,1)S(1)}, u32[]{:S(2)}, u32[]{:S(2)}) collective-permute-start(bf16[2,144,384]{2,1,0:T(8,128)(2,1)S(1)} %get-tuple-element.153), channel_id=1, source_target_pairs={{0,2},{1,3},{2,0},{3,1},{4,6},{5,7},{6,4},{7,5},{8,10},{9,11},{10,... | collective-permute-start | bytes 663560 | tf_op jit(solution)/shard_map/ppermute | solution.py:580
  226.1 22.1 %collective-permute-start.25 = (bf16[2,144,384]{2,1,0:T(8,128)(2,1)S(1)}, bf16[2,144,384]{2,1,0:T(8,128)(2,1)S(1)}, u32[]{:S(2)}, u32[]{:S(2)}) collective-permute-start(bf16[2,144,384]{2,1,0:T(8,128)(2,1)S(1)} %get-tuple-element.155), channel_id=1, source_target_pairs={{0,16},{16,0},{1,17},{17,1},{2,18},{18,2},{3,19},{19,3},{4,20},{20... | collective-permute-start | bytes 663560 | tf_op jit(solution)/shard_map/ppermute | solution.py:580
  227.4 11.3 %collective-permute-start.21 = (bf16[96,768]{1,0:T(8,128)(2,1)S(1)}, bf16[96,768]{1,0:T(8,128)(2,1)S(1)}, u32[]{:S(2)}, u32[]{:S(2)}) collective-permute-start(bf16[96,768]{1,0:T(8,128)(2,1)S(1)} %get-tuple-element.149), channel_id=1, source_target_pairs={{0,4},{1,5},{2,6},{3,7},{4,8},{5,9},{6,10},{7,11},{8,12},{9,13},{1... | collective-permute-start | bytes 442376 | tf_op jit(solution)/shard_map/ppermute | solution.py:586
  227.4 20.6 %collective-permute-start.22 = (bf16[96,768]{1,0:T(8,128)(2,1)S(1)}, bf16[96,768]{1,0:T(8,128)(2,1)S(1)}, u32[]{:S(2)}, u32[]{:S(2)}) collective-permute-start(bf16[96,768]{1,0:T(8,128)(2,1)S(1)} %get-tuple-element.150), channel_id=1, source_target_pairs={{0,8},{1,9},{2,10},{3,11},{4,12},{5,13},{6,14},{7,15},{8,0},{9,1},... | collective-permute-start | bytes 442376 | tf_op jit(solution)/shard_map/ppermute | solution.py:586
  228.8 19.2 %collective-permute-start.23 = (bf16[96,768]{1,0:T(8,128)(2,1)S(1)}, bf16[96,768]{1,0:T(8,128)(2,1)S(1)}, u32[]{:S(2)}, u32[]{:S(2)}) collective-permute-start(bf16[96,768]{1,0:T(8,128)(2,1)S(1)} %get-tuple-element.151), channel_id=1, source_target_pairs={{0,12},{1,13},{2,14},{3,15},{4,0},{5,1},{6,2},{7,3},{8,4},{9,5},{1... | collective-permute-start | bytes 442376 | tf_op jit(solution)/shard_map/ppermute | solution.py:586
  238.7 9.4 %collective-permute-start.27 = (bf16[4,16,384]{2,1,0:T(8,128)(2,1)S(1)}, bf16[4,16,384]{2,1,0:T(8,128)(2,1)S(1)}, u32[]{:S(2)}, u32[]{:S(2)}) collective-permute-start(bf16[4,16,384]{2,1,0:T(8,128)(2,1)S(1)} %dynamic-slice_bitcast_fusion.12), channel_id=1, source_target_pairs={{0,2},{1,3},{2,0},{3,1},{4,6},{5,7},{6,4},{7,5},{8,10},{9,11},{10,... | collective-permute-start | bytes 147464 | tf_op jit(solution)/shard_map/ppermute | solution.py:680
  250.3 8.1 %collective-permute-start.28 = (bf16[160,384]{1,0:T(8,128)(2,1)S(1)}, bf16[160,384]{1,0:T(8,128)(2,1)S(1)}, u32[]{:S(2)}, u32[]{:S(2)}) collective-permute-start(bf16[160,384]{1,0:T(8,128)(2,1)S(1)} %get-tuple-element.163), channel_id=1, source_target_pairs={{0,4},{1,5},{2,6},{3,7},{4,8},{5,9},{6,10},{7,11},{8,12},{9,13},{1... | collective-permute-start | bytes 368648 | tf_op jit(solution)/shard_map/ppermute | solution.py:586
  252.6 9.8 %collective-permute-start.29 = (bf16[160,384]{1,0:T(8,128)(2,1)S(1)}, bf16[160,384]{1,0:T(8,128)(2,1)S(1)}, u32[]{:S(2)}, u32[]{:S(2)}) collective-permute-start(bf16[160,384]{1,0:T(8,128)(2,1)S(1)} %get-tuple-element.164), channel_id=1, source_target_pairs={{0,8},{1,9},{2,10},{3,11},{4,12},{5,13},{6,14},{7,15},{8,0},{9,1},... | collective-permute-start | bytes 368648 | tf_op jit(solution)/shard_map/ppermute | solution.py:586
  253.2 9.2 %collective-permute-start.30 = (bf16[160,384]{1,0:T(8,128)(2,1)S(1)}, bf16[160,384]{1,0:T(8,128)(2,1)S(1)}, u32[]{:S(2)}, u32[]{:S(2)}) collective-permute-start(bf16[160,384]{1,0:T(8,128)(2,1)S(1)} %get-tuple-element.165), channel_id=1, source_target_pairs={{0,12},{1,13},{2,14},{3,15},{4,0},{5,1},{6,2},{7,3},{8,4},{9,5},{1... | collective-permute-start | bytes 368648 | tf_op jit(solution)/shard_map/ppermute | solution.py:586
  255.0 16.9 %copy-start.17 = (bf16[1,240,768]{2,1,0:T(8,128)(2,1)S(1)}, bf16[1,240,768]{2,1,0:T(8,128)(2,1)}, u32[]{:S(2)}) copy-start(bf16[1,240,768]{2,1,0:T(8,128)(2,1)} %reduce-scatter.2.cloned.1.call-done) | copy-start | bytes 1105924
  255.0 9.2 %collective-permute-start.33 = (bf16[96,768]{1,0:T(8,128)(2,1)S(1)}, bf16[96,768]{1,0:T(8,128)(2,1)S(1)}, u32[]{:S(2)}, u32[]{:S(2)}) collective-permute-start(bf16[96,768]{1,0:T(8,128)(2,1)S(1)} %add_convert_fusion.11), channel_id=1, source_target_pairs={{0,16},{16,0},{1,17},{17,1},{2,18},{18,2},{3,19},{19,3},{4,20},{20... | collective-permute-start | bytes 442376 | tf_op jit(solution)/shard_map/ppermute | solution.py:592
  256.1 15.8 %collective-permute-start.32 = (bf16[240,768]{1,0:T(8,128)(2,1)}, bf16[240,768]{1,0:T(8,128)(2,1)S(1)}, u32[]{:S(2)}, u32[]{:S(2)}) collective-permute-start(bf16[240,768]{1,0:T(8,128)(2,1)} %bitcast.120), channel_id=1, source_target_pairs={{0,16},{16,0},{1,17},{17,1},{2,18},{18,2},{3,19},{19,3},{4,20},{20... | collective-permute-start | bytes 1105928 | tf_op jit(solution)/shard_map/ppermute | solution.py:685
  262.5 8.1 %collective-permute-start.31 = (bf16[160,384]{1,0:T(8,128)(2,1)S(1)}, bf16[160,384]{1,0:T(8,128)(2,1)S(1)}, u32[]{:S(2)}, u32[]{:S(2)}) collective-permute-start(bf16[160,384]{1,0:T(8,128)(2,1)S(1)} %add_convert_fusion.12), channel_id=1, source_target_pairs={{0,16},{16,0},{1,17},{17,1},{2,18},{18,2},{3,19},{19,3},{4,20},{20... | collective-permute-start | bytes 368648 | tf_op jit(solution)/shard_map/ppermute | solution.py:592
  271.8 1.7 copy-start.20
  (3 other events, 3.0 us)
Sparse Core Ops, SparseCore 0:
  10.9 95.4 all-gather.2
  156.9 93.4 reduce-scatter.1
